TPU v7x, 32 devices: a whole 2x2x4 slice. The times are simulated.
32 devices in a mesh: batch: 8 (over z, core), seq: 4 (over y, x).
Axes of the slice: x: 2, y: 2, z: 4, core: 2. Of those that a mesh axis runs over, the one named last changes fastest.
Arguments:
- tokens: bfloat16 [64, 1024, 1152], P('batch', 'seq'), may hold values from -6 to 6
- conditioning: bfloat16 [64, 4, 1152], P('batch'), may hold values from -6 to 6
- segments: int32 [64, 1024], P('batch', 'seq'), may hold values from 0 to 3, as said below
- kept: int32 [64, 512], P('batch', 'seq'), may hold values from 0 to 255, as said below
- cotangent: bfloat16 [64, 1024, 1152], P('batch', 'seq'), may hold values from -6 to 6
- mod_weight: bfloat16 [1152, 6912], P(('batch', 'seq')), may hold values from -0.1875 to 0.1875
- mod_bias: bfloat16 [6912], P(('batch', 'seq')), may hold values from -2 to 2
- qkv_weight: bfloat16 [1152, 3456], P(('batch', 'seq')), may hold values from -0.1875 to 0.1875
- query_bias: bfloat16 [1152], P(('batch', 'seq')), may hold values from -3 to 3
- value_bias: bfloat16 [1152], P(('batch', 'seq')), may hold values from -3 to 3
- out_weight: bfloat16 [1152, 1152], P(('batch', 'seq')), may hold values from -1.5 to 1.5
- out_bias: bfloat16 [1152], P(('batch', 'seq')), may hold values from -2 to 2
- up_weight: bfloat16 [1152, 4608], P(('batch', 'seq')), may hold values from -0.1875 to 0.1875
- up_bias: bfloat16 [4608], P(('batch', 'seq')), may hold values from -3 to 3
- down_weight: bfloat16 [4608, 1152], P(('batch', 'seq')), may hold values from -0.09375 to 0.09375
- down_bias: bfloat16 [1152], P(('batch', 'seq')), may hold values from -4 to 4
Outputs:
- output: bfloat16 [64, 1024, 1152], P('batch', 'seq')
- tokens_grad: bfloat16 [64, 1024, 1152], P('batch', 'seq')
- mod_weight_grad: float32 [1152, 6912], P(('batch', 'seq'))
- mod_bias_grad: float32 [6912], P(('batch', 'seq'))
- qkv_weight_grad: float32 [1152, 3456], P(('batch', 'seq'))
- query_bias_grad: float32 [1152], P(('batch', 'seq'))
- value_bias_grad: float32 [1152], P(('batch', 'seq'))
- out_weight_grad: float32 [1152, 1152], P(('batch', 'seq'))
- out_bias_grad: float32 [1152], P(('batch', 'seq'))
- up_weight_grad: float32 [1152, 4608], P(('batch', 'seq'))
- up_bias_grad: float32 [4608], P(('batch', 'seq'))
- down_weight_grad: float32 [4608, 1152], P(('batch', 'seq'))
- down_bias_grad: float32 [1152], P(('batch', 'seq'))
- sample_counts: int32 [64, 4, 2], P('batch')
Inputs may be any that keep to these rules, and one draw needn't show every extreme that they name: `kept`: in each row, each aligned block of 128 entries lists, in increasing order, distinct positions among the 256 tokens of that row on one index of seq; positions 0 and 255 are always listed. `segments`: each row holds one of three packings: one sample of 1024 tokens, all numbered 0; 4 samples of 256 tokens numbered 0 to 3 in order; or a sample of 640 tokens numbered 0 followed by one of the remaining tokens numbered 1. In each aligned block of 8 rows at least one row is a single sample and at least one is of the third packing. Conditioning slots whose number a row does not use are read by nothing.
All inputs are finite; a program needn't handle non-finite values.
Results may differ from a plain program's by a relative error of at most 0.014.
The roundings to bfloat16 on the way count: a program that leaves them out, or rounds other values in their place, can miss the bound.
Values may be sent and summed in bfloat16 or wider, within the bound.
No kernel may reach another device: no remote copies, remote signals or barrier semaphores. Data moves between devices by JAX's collectives and lax.ppermute only.
A program may use at most 384 MiB of HBM per device.

v0:
```python
import jax
import jax.numpy as jnp
from jax import lax
from jax.sharding import PartitionSpec as P

HEADS = 16


HIGH = lax.Precision.HIGHEST
EPS = 1e-06
GELU_C = 0.7978845608028654
GELU_A = 0.044715


def normalize(values):
    center = values - jnp.mean(values, -1, keepdims=True)
    scale_inv = lax.rsqrt(jnp.mean(center * center, -1, keepdims=True) + EPS)
    return (center * scale_inv, scale_inv)


def norm_back(grad_norm, normed, scale_inv):
    return scale_inv * (
        grad_norm
        - jnp.mean(grad_norm, -1, keepdims=True)
        - normed * jnp.mean(grad_norm * normed, -1, keepdims=True)
    )


def attend_piece(state_now, pieces, query_heads, query_seg, key_seg, head_count, score_scale):
    best, total, accum = state_now
    key_piece, value_piece = pieces
    row_count, piece_count, model_width = key_piece.shape
    key_heads = key_piece.reshape(row_count, piece_count, head_count, model_width // head_count)
    value_heads = value_piece.reshape(row_count, piece_count, head_count, model_width // head_count)
    allowed = (query_seg[:, :, None] == key_seg[:, None, :])[:, None]
    score = (
        jnp.einsum("rqhd,rkhd->rhqk", query_heads, key_heads, preferred_element_type=jnp.float32)
        * score_scale
    )
    score = jnp.where(allowed, score, -1e30)
    newest = jnp.maximum(best, jnp.max(score, -1))
    weights = jnp.where(allowed, jnp.exp(score - newest[..., None]), 0.0)
    total = jnp.sum(weights, -1)
    accum = jnp.einsum(
        "rhqk,rkhd->rhqd",
        weights.astype(jnp.bfloat16),
        value_heads,
        preferred_element_type=jnp.float32,
    )
    return (newest, total, accum)


def probs_for(query_part, key_part, total_part, allowed, score_scale):
    score = (
        jnp.einsum("rqhd,rkhd->rhqk", query_part, key_part, preferred_element_type=jnp.float32)
        * score_scale
    )
    return jnp.exp(jnp.where(allowed, score - total_part[..., None], -1e30))


def body(
    tokens,
    conditioning,
    segments,
    kept,
    cotangent,
    mod_weight,
    mod_bias,
    qkv_weight,
    query_bias,
    value_bias,
    out_weight,
    out_bias,
    up_weight,
    up_bias,
    down_weight,
    down_bias,
):
    row_count, seq_tokens, model_width = tokens.shape
    kept_count = kept.shape[1]
    head_count = HEADS
    head_size = model_width // head_count
    score_scale = head_size ** (-0.5)
    sample_slots = conditioning.shape[1]
    flat_count = row_count * kept_count
    gathered = (
        lax.all_gather(mod_weight, ("batch", "seq"), axis=0, tiled=True),
        lax.all_gather(mod_bias, ("batch", "seq"), axis=0, tiled=True),
        lax.all_gather(qkv_weight, ("batch", "seq"), axis=0, tiled=True),
        lax.all_gather(query_bias, ("batch", "seq"), axis=0, tiled=True),
        lax.all_gather(value_bias, ("batch", "seq"), axis=0, tiled=True),
        lax.all_gather(out_weight, ("batch", "seq"), axis=0, tiled=True),
        lax.all_gather(out_bias, ("batch", "seq"), axis=0, tiled=True),
        lax.all_gather(up_weight, ("batch", "seq"), axis=0, tiled=True),
        lax.all_gather(up_bias, ("batch", "seq"), axis=0, tiled=True),
        lax.all_gather(down_weight, ("batch", "seq"), axis=0, tiled=True),
        lax.all_gather(down_bias, ("batch", "seq"), axis=0, tiled=True),
    )
    (
        whole_mod,
        whole_mod_bias,
        whole_qkv,
        whole_query_bias,
        whole_value_bias,
        whole_out,
        whole_out_bias,
        whole_up,
        whole_up_bias,
        whole_down,
        whole_down_bias,
    ) = gathered
    picked = jnp.take_along_axis(tokens, kept[:, :, None], axis=1)
    inputs = picked.astype(jnp.float32).reshape(flat_count, model_width)
    query_seg = jnp.take_along_axis(segments, kept, axis=1)
    key_seg = lax.all_gather(query_seg, "seq", axis=1, tiled=True)
    numbers = jnp.arange(sample_slots, dtype=jnp.int32)
    kept_hits = jnp.sum((query_seg[:, :, None] == numbers).astype(jnp.int32), 1)
    all_hits = jnp.sum((segments[:, :, None] == numbers).astype(jnp.int32), 1)
    local_counts = jnp.stack([kept_hits, all_hits - kept_hits], -1)
    sample_counts = lax.psum(local_counts, "seq")
    cond_float = conditioning.astype(jnp.float32)
    cond_act = (cond_float / (1.0 + jnp.exp(-cond_float))).astype(jnp.bfloat16)
    modulation = jnp.einsum("rsd,de->rse", cond_act, whole_mod, preferred_element_type=jnp.float32)
    modulation = modulation + whole_mod_bias.astype(jnp.float32)
    one_hot = (query_seg[:, :, None] == numbers).astype(jnp.float32)
    token_mod = jnp.einsum("rks,rse->rke", one_hot, modulation, precision=HIGH).reshape(
        flat_count, 6 * model_width
    )
    shift_one, scale_one, gate_one, shift_two, scale_two, gate_two = jnp.split(
        token_mod, 6, axis=-1
    )
    normed_one, inv_one = normalize(inputs)
    hidden_one = (normed_one * (1.0 + scale_one) + shift_one).astype(jnp.bfloat16)
    qkv = jnp.dot(hidden_one, whole_qkv, preferred_element_type=jnp.float32)
    queries = (qkv[:, :model_width] + whole_query_bias.astype(jnp.float32)).astype(jnp.bfloat16)
    keys = qkv[:, model_width : 2 * model_width].astype(jnp.bfloat16)
    values = (qkv[:, 2 * model_width :] + whole_value_bias.astype(jnp.float32)).astype(jnp.bfloat16)
    queries = queries.reshape(row_count, kept_count, model_width)
    keys = keys.reshape(row_count, kept_count, model_width)
    values = values.reshape(row_count, kept_count, model_width)
    query_heads = queries.reshape(row_count, kept_count, head_count, head_size)
    start_state = (
        jnp.full((row_count, head_count, kept_count), -1e30, jnp.float32),
        jnp.zeros((row_count, head_count, kept_count), jnp.float32),
        jnp.zeros((row_count, head_count, kept_count, head_size), jnp.float32),
    )
    best, total, accum = attend_piece(
        start_state,
        (
            lax.all_gather(keys, "seq", axis=1, tiled=True),
            lax.all_gather(values, "seq", axis=1, tiled=True),
        ),
        query_heads,
        query_seg,
        key_seg,
        head_count,
        score_scale,
    )
    log_total = best + jnp.log(total)
    attended = jnp.transpose(accum / total[..., None], (0, 2, 1, 3)).reshape(
        flat_count, model_width
    )
    attended_low = attended.astype(jnp.bfloat16)
    branch_attn = jnp.dot(
        attended_low, whole_out, preferred_element_type=jnp.float32
    ) + whole_out_bias.astype(jnp.float32)
    mid = inputs + gate_one * branch_attn
    normed_two, inv_two = normalize(mid)
    hidden_two = (normed_two * (1.0 + scale_two) + shift_two).astype(jnp.bfloat16)
    pre_act = jnp.dot(
        hidden_two, whole_up, preferred_element_type=jnp.float32
    ) + whole_up_bias.astype(jnp.float32)
    tanh_part = jnp.tanh(GELU_C * (pre_act + GELU_A * pre_act * pre_act * pre_act))
    activated = (0.5 * pre_act * (1.0 + tanh_part)).astype(jnp.bfloat16)
    branch_mlp = jnp.dot(
        activated, whole_down, preferred_element_type=jnp.float32
    ) + whole_down_bias.astype(jnp.float32)
    result = mid + gate_two * branch_mlp
    row_ids = jnp.arange(row_count)[:, None]
    output = tokens.at[row_ids, kept].set(
        result.reshape(row_count, kept_count, model_width).astype(jnp.bfloat16)
    )
    back_qkv, back_out, back_up, back_down = (
        lax.all_gather(qkv_weight, ("batch", "seq"), axis=0, tiled=True),
        lax.all_gather(out_weight, ("batch", "seq"), axis=0, tiled=True),
        lax.all_gather(up_weight, ("batch", "seq"), axis=0, tiled=True),
        lax.all_gather(down_weight, ("batch", "seq"), axis=0, tiled=True),
    )
    grad_result = jnp.take_along_axis(cotangent, kept[:, :, None], axis=1).astype(jnp.float32)
    grad_result = grad_result.reshape(flat_count, model_width)
    grad_gate_two = grad_result * branch_mlp
    grad_mlp = (grad_result * gate_two).astype(jnp.bfloat16)
    grad_down = jnp.einsum("nf,nd->fd", activated, grad_mlp, preferred_element_type=jnp.float32)
    grad_down_bias = jnp.sum(grad_mlp.astype(jnp.float32), 0)
    grad_act = jnp.einsum("nd,fd->nf", grad_mlp, back_down, preferred_element_type=jnp.float32)
    slope = 0.5 * (1.0 + tanh_part) + 0.5 * pre_act * (1.0 - tanh_part * tanh_part) * GELU_C * (
        1.0 + 3.0 * GELU_A * pre_act * pre_act
    )
    grad_pre = (grad_act * slope).astype(jnp.bfloat16)
    grad_up = jnp.einsum("nd,nf->df", hidden_two, grad_pre, preferred_element_type=jnp.float32)
    grad_up_bias = jnp.sum(grad_pre.astype(jnp.float32), 0)
    grad_hidden_two = jnp.einsum("nf,df->nd", grad_pre, back_up, preferred_element_type=jnp.float32)
    grad_mid = grad_result + norm_back(grad_hidden_two * (1.0 + scale_two), normed_two, inv_two)
    grad_gate_one = grad_mid * branch_attn
    grad_branch = (grad_mid * gate_one).astype(jnp.bfloat16)
    grad_outw = jnp.einsum(
        "nd,ne->de", attended_low, grad_branch, preferred_element_type=jnp.float32
    )
    grad_out_bias = jnp.sum(grad_branch.astype(jnp.float32), 0)
    grad_attended = jnp.einsum(
        "ne,de->nd", grad_branch, back_out, preferred_element_type=jnp.float32
    )
    grad_attended = grad_attended.astype(jnp.bfloat16).reshape(
        row_count, kept_count, head_count, head_size
    )
    key_full, value_full = (
        lax.all_gather(keys, "seq", axis=1, tiled=True),
        lax.all_gather(values, "seq", axis=1, tiled=True),
    )
    total_keys = key_full.shape[1]
    key_heads = key_full.reshape(row_count, total_keys, head_count, head_size)
    value_heads = value_full.reshape(row_count, total_keys, head_count, head_size)
    allowed = (query_seg[:, :, None] == key_seg[:, None, :])[:, None]
    group_size = 4
    group_total = head_count // group_size

    def head_step(group_index, sums):
        grad_query, grad_key, grad_value = sums
        first_head = group_index * group_size
        query_part = lax.dynamic_slice_in_dim(query_heads, first_head, group_size, 2)
        key_part = lax.dynamic_slice_in_dim(key_heads, first_head, group_size, 2)
        value_part = lax.dynamic_slice_in_dim(value_heads, first_head, group_size, 2)
        grad_part = lax.dynamic_slice_in_dim(grad_attended, first_head, group_size, 2)
        total_part = lax.dynamic_slice_in_dim(log_total, first_head, group_size, 1)
        probs = probs_for(query_part, key_part, total_part, allowed, score_scale)
        grad_prob = jnp.einsum(
            "rqhd,rkhd->rhqk", grad_part, value_part, preferred_element_type=jnp.float32
        )
        inner = jnp.sum(probs * grad_prob, -1, keepdims=True)
        grad_score = (probs * (grad_prob - inner)).astype(jnp.bfloat16)
        query_term = (
            jnp.einsum("rhqk,rkhd->rqhd", grad_score, key_part, preferred_element_type=jnp.float32)
            * score_scale
        )
        key_term = (
            jnp.einsum(
                "rhqk,rqhd->rkhd", grad_score, query_part, preferred_element_type=jnp.float32
            )
            * score_scale
        )
        value_term = jnp.einsum(
            "rhqk,rqhd->rkhd",
            probs.astype(jnp.bfloat16),
            grad_part,
            preferred_element_type=jnp.float32,
        )
        grad_query = lax.dynamic_update_slice_in_dim(grad_query, query_term, first_head, 2)
        grad_key = lax.dynamic_update_slice_in_dim(grad_key, key_term, first_head, 2)
        grad_value = lax.dynamic_update_slice_in_dim(grad_value, value_term, first_head, 2)
        return (grad_query, grad_key, grad_value)

    zero_sums = (
        jnp.zeros((row_count, kept_count, head_count, head_size), jnp.float32),
        jnp.zeros((row_count, total_keys, head_count, head_size), jnp.float32),
        jnp.zeros((row_count, total_keys, head_count, head_size), jnp.float32),
    )
    grad_query, grad_key, grad_value = lax.fori_loop(0, group_total, head_step, zero_sums)
    own_key, own_value = (
        lax.psum_scatter(
            grad_key.reshape(row_count, total_keys, model_width).astype(jnp.bfloat16),
            "seq",
            scatter_dimension=1,
            tiled=True,
        ).astype(jnp.float32),
        lax.psum_scatter(
            grad_value.reshape(row_count, total_keys, model_width).astype(jnp.bfloat16),
            "seq",
            scatter_dimension=1,
            tiled=True,
        ).astype(jnp.float32),
    )
    grad_qkv = jnp.concatenate(
        [
            grad_query.reshape(row_count, kept_count, model_width).astype(jnp.bfloat16),
            own_key.astype(jnp.bfloat16),
            own_value.astype(jnp.bfloat16),
        ],
        -1,
    )
    grad_qkv = grad_qkv.reshape(flat_count, 3 * model_width)
    grad_qkvw = jnp.einsum("nd,ne->de", hidden_one, grad_qkv, preferred_element_type=jnp.float32)
    grad_query_bias = jnp.sum(grad_qkv[:, :model_width].astype(jnp.float32), 0)
    grad_value_bias = jnp.sum(grad_qkv[:, 2 * model_width :].astype(jnp.float32), 0)
    grad_hidden_one = jnp.einsum(
        "ne,de->nd", grad_qkv, back_qkv, preferred_element_type=jnp.float32
    )
    grad_inputs = grad_mid + norm_back(grad_hidden_one * (1.0 + scale_one), normed_one, inv_one)
    grad_token_mod = jnp.concatenate(
        [
            grad_hidden_one,
            grad_hidden_one * normed_one,
            grad_gate_one,
            grad_hidden_two,
            grad_hidden_two * normed_two,
            grad_gate_two,
        ],
        -1,
    )
    grad_token_mod = grad_token_mod.reshape(row_count, kept_count, 6 * model_width)
    grad_mod = jnp.einsum("rks,rke->rse", one_hot, grad_token_mod, precision=HIGH)
    grad_modw = jnp.einsum("rsd,rse->de", cond_act.astype(jnp.float32), grad_mod, precision=HIGH)
    grad_mod_bias = jnp.sum(grad_mod, (0, 1))
    summed = (
        lax.psum_scatter(grad_modw, ("batch", "seq"), scatter_dimension=0, tiled=True),
        lax.psum_scatter(grad_mod_bias, ("batch", "seq"), scatter_dimension=0, tiled=True),
        lax.psum_scatter(grad_qkvw, ("batch", "seq"), scatter_dimension=0, tiled=True),
        lax.psum_scatter(grad_query_bias, ("batch", "seq"), scatter_dimension=0, tiled=True),
        lax.psum_scatter(grad_value_bias, ("batch", "seq"), scatter_dimension=0, tiled=True),
        lax.psum_scatter(grad_outw, ("batch", "seq"), scatter_dimension=0, tiled=True),
        lax.psum_scatter(grad_out_bias, ("batch", "seq"), scatter_dimension=0, tiled=True),
        lax.psum_scatter(grad_up, ("batch", "seq"), scatter_dimension=0, tiled=True),
        lax.psum_scatter(grad_up_bias, ("batch", "seq"), scatter_dimension=0, tiled=True),
        lax.psum_scatter(grad_down, ("batch", "seq"), scatter_dimension=0, tiled=True),
        lax.psum_scatter(grad_down_bias, ("batch", "seq"), scatter_dimension=0, tiled=True),
    )
    mod_weight_part = summed[0]
    mod_bias_part = summed[1]
    other_sums = summed[2:]
    tokens_grad = cotangent.at[row_ids, kept].set(
        grad_inputs.reshape(row_count, kept_count, model_width).astype(jnp.bfloat16)
    )
    return (
        output,
        tokens_grad,
        mod_weight_part,
        mod_bias_part,
        other_sums[0],
        other_sums[1],
        other_sums[2],
        other_sums[3],
        other_sums[4],
        other_sums[5],
        other_sums[6],
        other_sums[7],
        other_sums[8],
        sample_counts,
    )


def solution(mesh):
    placed = (
        P("batch", "seq", None),
        P("batch", None, None),
        P("batch", "seq"),
        P("batch", "seq"),
        P("batch", "seq", None),
        P(("batch", "seq"), None),
        P(("batch", "seq")),
        P(("batch", "seq"), None),
        P(("batch", "seq")),
        P(("batch", "seq")),
        P(("batch", "seq"), None),
        P(("batch", "seq")),
        P(("batch", "seq"), None),
        P(("batch", "seq")),
        P(("batch", "seq"), None),
        P(("batch", "seq")),
    )
    return jax.shard_map(
        body,
        mesh=mesh,
        in_specs=placed,
        out_specs=(
            P("batch", "seq", None),
            P("batch", "seq", None),
            P(("batch", "seq"), None),
            P(("batch", "seq")),
            P(("batch", "seq"), None),
            P(("batch", "seq")),
            P(("batch", "seq")),
            P(("batch", "seq"), None),
            P(("batch", "seq")),
            P(("batch", "seq"), None),
            P(("batch", "seq")),
            P(("batch", "seq"), None),
            P(("batch", "seq")),
            P("batch", None, None),
        ),
        check_vma=False,
    )
```

profile of v0, /device:TPU:1, one launch (start us, length us, event | category | flops | bytes accessed | tf_op | source)
XLA Modules:
  0.0 3437.2 jit_solution(8619234387264449476)
XLA Ops:
  20.8 42.9 %all-reduce.21 = (bf16[1152]{0:T(1024)(128)(2,1)S(1)}, bf16[6912]{0:T(1024)(128)(2,1)S(1)}, bf16[1152]{0:T(1024)(128)(2,1)S(1)}, bf16[1152]{0:T(1024)(128)(2,1)S...) all-reduce(bf16[1152]{0:T(1024)(128)(2,1)S(1)} %dynamic-update-slic, ...), channel_id=1, replica_groups=mesh['batch'=8,'seq'=4] {'batch','seq'}, use_global_device_ids=true, to_apply=%add.3 | all-reduce | flops 16128 | bytes 64512
  70.5 16.4 gather_fusion.1
  89.4 10.0 all-gather.20.cloned.1.call-done
  99.4 12.5 reshape.244
  112.0 108.3 %all-gather.18.cloned.1.call-done = bf16[32,36,6912]{2,1,0:T(8,128)(2,1)} async-done(((bf16[1,36,6912]{2,1,0:T(8,128)(2,1)}), bf16[32,36,6912]{2,1,0:T(8,128)(2,1)}) %all-gather.18.cloned.1.call-update) | async-done | bytes 15925264 | tf_op jit(solution)/shard_map/all_gather | solution.py:87
  220.2 18.4 reshape.257
  247.0 14.9 fusion.87
  267.1 9.6 fusion.106
  291.0 21.8 gather_fusion.2
  329.3 45.0 %all-gather.24.cloned.1.call-done = bf16[32,36,4608]{2,1,0:T(8,128)(2,1)} async-done(((bf16[1,36,4608]{2,1,0:T(8,128)(2,1)}), bf16[32,36,4608]{2,1,0:T(8,128)(2,1)}) %all-gather.24.cloned.1.call-update) | async-done | bytes 10616848 | tf_op jit(solution)/shard_map/all_gather | solution.py:94
  374.3 14.6 reshape.248
  389.0 9.6 reshape.265
  404.8 65.5 %all-gather.12.cloned.1.call-done = bf16[8,512,1152]{2,1,0:T(8,128)(2,1)} async-done(((bf16[8,128,1152]{2,1,0:T(8,128)(2,1)}), bf16[8,512,1152]{2,1,0:T(8,128)(2,1)}) %all-gather.12.cloned.1.call-update) | async-done | bytes 9437200 | tf_op jit(solution)/shard_map/all_gather | solution.py:150
  470.3 12.9 copy.74
  483.2 85.2 %all-gather.14.cloned.1.call-done = bf16[8,512,1152]{2,1,0:T(8,128)(2,1)} async-done(((bf16[8,128,1152]{2,1,0:T(8,128)(2,1)}), bf16[8,512,1152]{2,1,0:T(8,128)(2,1)}) %all-gather.14.cloned.1.call-update) | async-done | bytes 9437200 | tf_op jit(solution)/shard_map/all_gather | solution.py:151
  568.4 12.7 copy.76
  581.0 18.6 fusion.41
  599.6 16.4 fusion.42
  616.0 16.0 fusion.60
  659.2 15.4 fusion.107
  674.6 29.3 convert_reduce_fusion
  703.9 21.9 fusion.99
  725.8 10.6 convert_reduce_fusion.3
  767.0 92.2 %while.18 = (s32[]{:T(128)}, bf16[8,128,16,72]{1,3,2,0:T(8,128)(2,1)}, bf16[8,512,16,72]{1,3,2,0:T(8,128)(2,1)}, bf16[8,512,16,72]{1,3,2,0:T(8,128)(2,1)}, bf16[...) while((s32[]{:T(128)}, ...), condition=%wide.region_11.13_spmd.clone, body=%wide.region_9.12_spmd.clone.sunk | while | flops 1543401472 | bytes 85206216 | solution.py:267
  859.2 13.1 copy.88
  881.8 13.7 copy.86
  895.5 9.8 copy.93
  914.0 18.1 fusion.109
  932.0 24.3 fusion.101
  956.4 20.5 reduce-scatter.20.cloned.1.call-done
  983.6 91.5 %reduce-scatter.18.cloned.1.call-done = bf16[128,9216]{1,0:T(8,128)(2,1)} async-done(((bf16[512,9216]{1,0:T(8,128)(2,1)}), bf16[128,9216]{1,0:T(8,128)(2,1)}) %reduce-scatter.18.cloned.1.call-update) | async-done | bytes 2359312
  1088.7 10.9 copy.81
  1099.7 18.5 fusion.100
  1118.2 11.6 fusion.64
  1143.6 23.8 fusion.55
  1167.5 13.9 fusion.105
  1181.4 17.4 convolution_bitcast_fusion
  1198.8 916.5 %fusion.102 = (f32[40,6912]{1,0:T(8,128)S(1)}, f32[48,1152]{1,0:T(8,128)}) fusion(f32[1152,6912]{1,0:T(8,128)} %convolution_bitcast_fusion, f32[1152,1152]{1,0:T(8,128)} %fusion.76), kind=kCustom, calls=%all-reduce-scatter.4 | all-reduce-scatter fusion | flops 10616834 | bytes 38486016
  2119.9 14.6 fusion.108
  2134.5 946.0 %fusion.103 = (f32[48,3456]{1,0:T(8,128)S(1)}, f32[40,4608]{1,0:T(8,128)}) fusion(f32[1152,3456]{1,0:T(8,128)} %fusion.108, f32[1152,4608]{1,0:T(8,128)} %fusion.109), kind=kCustom, calls=%all-reduce-scatter.5 | all-reduce-scatter fusion | flops 11206658 | bytes 38559744
  3129.5 46.8 %collective-permute-start.7 = (f32[48,3456]{1,0:T(8,128)S(1)}, f32[48,3456]{1,0:T(8,128)}, u32[]{:S(2)}, u32[]{:S(2)}) collective-permute-start(f32[48,3456]{1,0:T(8,128)S(1)} %get-tuple-element.386), channel_id=1, source_target_pairs={{0,4},{1,5},{2,6},{3,7},{4,8},{5,9},{6,10},{7,11},{8,12},{9,13},{1... | collective-permute-start | bytes 1990664
  3186.5 36.1 %psum.7 = s32[8,4,2]{0,1,2:T(4,128)S(1)} all-reduce(s32[8,4,2]{0,1,2:T(4,128)S(1)} %pad_add_fusion.1), channel_id=1, replica_groups=mesh['batch'=8,'seq'=4] {'seq'}, use_global_device_ids=true, to_apply=%region_36.38 | all-reduce | flops 64 | bytes 512 | tf_op jit(solution)/shard_map/psum | solution.py:120
  3235.3 59.2 %all-reduce.20 = (f32[6912]{0:T(1024)}, f32[1152]{0:T(1024)S(1)}, f32[1152]{0:T(1024)S(1)}, f32[1152]{0:T(1024)S(1)}, f32[4608]{0:T(1024)S(1)}, /*index=5*/f32[1152]{0:T(1024)S(1)}) all-reduce(f32[6912]{0:T(1024)S(1)} %get-tuple-element.415, ...), channel_id=5, replica_groups=mesh['batch'=8,'seq'=4] {'batch','seq'}, use_global_device_ids=true, to_apply=%region_19.21.clone | all-reduce | flops 16128 | bytes 129024
  3296.9 13.5 scatter_custom_fusion
  3310.4 10.6 scatter_fusion
  3343.3 36.8 %concatenate.25 = f32[420,3456]{1,0:T(8,128)} concatenate(f32[36,3456]{1,0:T(8,128)} %copy-done.30, f32[48,3456]{1,0:T(8,128)} %copy-done.29, f32[48,3456]{1,0:T(8,128)} %collective-permute-done.9, f32[48,3456]{1,0:T(8,128)} %collective-permute-done.8, f32[48,3456]{1,0:T(8,128)} %collective-permute-done.7, f32[48,3456]{1,0:T(8,128)} %collective-permute-done.6, ...), dimensions={0} | concatenate | bytes 11612160
  3385.2 18.1 concatenate.27
  3405.5 22.2 concatenate.24
  (358 shorter events, 385.9 us)
Async XLA Ops:
  7.2 92.2 %all-gather.20.cloned.1.call-start = ((), (), s32[]{:S(2)}) async-start(), calls=%async_computation.8 | async-start | bytes 9123840 | tf_op jit(solution)/shard_map/all_gather | solution.py:89
  17.2 203.1 %all-gather.18.cloned.1.call-start = ((), (), s32[]{:S(2)}) async-start(), calls=%async_computation.7 | async-start | bytes 18247680 | tf_op jit(solution)/shard_map/all_gather | solution.py:87
  17.9 305.9 %all-gather.22.cloned.1.call-start = ((), (), s32[]{:S(2)}) async-start(), calls=%async_computation.9 | async-start | bytes 3041280 | tf_op jit(solution)/shard_map/all_gather | solution.py:92
  18.6 355.7 %all-gather.24.cloned.1.call-start = ((), (), s32[]{:S(2)}) async-start(), calls=%async_computation.10 | async-start | bytes 12165120 | tf_op jit(solution)/shard_map/all_gather | solution.py:94
  19.2 451.1 %all-gather.12.cloned.1.call-start = ((), (), s32[]{:S(2)}) async-start(), calls=%async_computation.3 | async-start | bytes 11796480 | tf_op jit(solution)/shard_map/all_gather | solution.py:150
  87.0 546.6 %copy-start.3 = (bf16[1024,1152]{1,0:T(8,128)(2,1)}, bf16[1024,1152]{1,0:T(8,128)(2,1)S(1)}, u32[]{:S(2)}) copy-start(bf16[1024,1152]{1,0:T(8,128)(2,1)S(1)} %gather_fusion.1) | copy-start | bytes 7077892
  87.0 546.5 %copy-start.44 = (pred[8,128]{1,0:T(8,128)(4,1)}, pred[8,128]{1,0:T(8,128)(4,1)S(1)}, u32[]{:S(2)}) copy-start(pred[8,128]{1,0:T(8,128)(4,1)S(1)} %and_bitcast_fusion) | copy-start | bytes 3076
  87.6 174.2 %copy-start.48 = (f32[1024]{0:T(1024)}, f32[1024]{0:T(1024)S(1)}, u32[]{:S(2)}) copy-start(f32[1024]{0:T(1024)S(1)} %get-tuple-element.401) | copy-start | bytes 12292
  88.8 173.1 %copy-start.50 = (f32[1024]{0:T(1024)}, f32[1024]{0:T(1024)S(1)}, u32[]{:S(2)}) copy-start(f32[1024]{0:T(1024)S(1)} %rsqrt_bitcast_fusion) | copy-start | bytes 12292
  89.4 230.4 %copy-start.24 = (s32[8,128]{1,0:T(8,128)}, s32[8,128]{1,0:T(8,128)S(1)}, u32[]{:S(2)}) copy-start(s32[8,128]{1,0:T(8,128)S(1)} %get-tuple-element.502) | copy-start | bytes 12292
  283.4 284.9 %all-gather.14.cloned.1.call-start = ((), (), s32[]{:S(2)}) async-start(), calls=%async_computation.4 | async-start | bytes 11796480 | tf_op jit(solution)/shard_map/all_gather | solution.py:151
  290.2 384.4 %all-gather.16.cloned.1.call-start = ((), (), s32[]{:S(2)}) async-start(), calls=%async_computation.5 | async-start | bytes 10948608 | tf_op jit(solution)/shard_map/all_gather | solution.py:96
  291.0 685.9 %reduce-scatter.20.cloned.1.call-start = ((), (), s32[]{:S(2)}) async-start(), calls=%async_computation.12 | async-start | bytes 11796480
  312.8 361.8 %copy-start.55 = (f32[4608]{0:T(1024)}, f32[4608]{0:T(1024)S(1)}, u32[]{:S(2)}) copy-start(f32[4608]{0:T(1024)S(1)} %convert_element_type.150) | copy-start | bytes 55300
  881.7 193.3 %reduce-scatter.18.cloned.1.call-start = ((), (), s32[]{:S(2)}) async-start(), calls=%async_computation.11 | async-start | bytes 11796480
  905.2 2524.9 %reduce-scatter.16.cloned.1.call-start = ((), (), s32[]{:S(2)}) async-start(), calls=%async_computation.6 | async-start | bytes 21897216 | tf_op jit(solution)/shard_map/reduce_scatter | solution.py:323
  1198.8 921.1 %copy-start.19 = (bf16[1024,1152]{1,0:T(8,128)(2,1)S(1)}, bf16[1024,1152]{1,0:T(8,128)(2,1)}, u32[]{:S(2)}) copy-start(bf16[1024,1152]{1,0:T(8,128)(2,1)} %copy-done.18) | copy-start | bytes 7077892
  2115.3 1119.3 %copy-start.15 = (f32[40,6912]{1,0:T(8,128)}, f32[40,6912]{1,0:T(8,128)S(1)}, u32[]{:S(2)}) copy-start(f32[40,6912]{1,0:T(8,128)S(1)} %get-tuple-element.382) | copy-start | bytes 3317764
  2117.1 981.2 %collective-permute-start.19 = (f32[36,1152]{1,0:T(8,128)}, f32[36,1152]{1,0:T(8,128)}, u32[]{:S(2)}, u32[]{:S(2)}) collective-permute-start(f32[36,1152]{1,0:T(8,128)} %slice.34), channel_id=1, source_target_pairs={{0,8},{1,9},{2,10},{3,11},{4,12},{5,13},{6,14},{7,15},{8,16},{9,17... | collective-permute-start | bytes 497672
  2134.5 948.9 %copy-start.23 = (f32[48,1152]{1,0:T(8,128)S(1)}, f32[48,1152]{1,0:T(8,128)}, u32[]{:S(2)}) copy-start(f32[48,1152]{1,0:T(8,128)} %get-tuple-element.383) | copy-start | bytes 663556
  2134.5 989.7 %copy-start.47 = (s32[8,128,1]{1,0,2:T(8,128)S(1)}, s32[8,128,1]{1,0,2:T(8,128)}, u32[]{:S(2)}) copy-start(s32[8,128,1]{1,0,2:T(8,128)} %get-tuple-element.406) | copy-start | bytes 12292
  2134.5 989.7 %copy-start.59 = (s32[2]{0:T(128)S(1)}, s32[2]{0:T(128)}, u32[]{:S(2)}) copy-start(s32[2]{0:T(128)} %constant.125) | copy-start | bytes 28
  2134.5 989.8 %copy-start.1 = (s32[8,256]{1,0:T(8,128)S(1)}, s32[8,256]{1,0:T(8,128)}, u32[]{:S(2)}) copy-start(s32[8,256]{1,0:T(8,128)} %param.22) | copy-start | bytes 24580
  2134.5 1088.8 %copy-start.58 = (s32[2]{0:T(128)S(1)}, s32[2]{0:T(128)}, u32[]{:S(2)}) copy-start(s32[2]{0:T(128)} %constant.128) | copy-start | bytes 28
  3080.5 154.9 %copy-start.54 = (f32[4608]{0:T(1024)S(1)}, f32[4608]{0:T(1024)}, u32[]{:S(2)}) copy-start(f32[4608]{0:T(1024)} %get-tuple-element.417) | copy-start | bytes 55300
  3081.4 14.9 collective-permute-start.23
  3083.4 18.4 collective-permute-start.18
  3089.7 13.4 collective-permute-start.17
  3094.3 12.2 collective-permute-start.16
  3096.3 14.2 collective-permute-start.15
  3098.3 16.6 collective-permute-start.14
  3101.7 74.5 %collective-permute-start.11 = (f32[36,3456]{1,0:T(8,128)}, f32[36,3456]{1,0:T(8,128)S(1)}, u32[]{:S(2)}, u32[]{:S(2)}) collective-permute-start(f32[36,3456]{1,0:T(8,128)} %slice.33), channel_id=1, source_target_pairs={{0,8},{1,9},{2,10},{3,11},{4,12},{5,13},{6,14},{7,15},{8,16},{9,17... | collective-permute-start | bytes 1493000
  3103.1 15.9 collective-permute-start.13
  3106.5 71.7 %collective-permute-start.10 = (f32[48,3456]{1,0:T(8,128)S(1)}, f32[48,3456]{1,0:T(8,128)S(1)}, u32[]{:S(2)}, u32[]{:S(2)}) collective-permute-start(f32[48,3456]{1,0:T(8,128)S(1)} %get-tuple-element.386), channel_id=1, source_target_pairs={{0,7},{1,8},{2,9},{3,10},{4,11},{5,12},{6,13},{7,14},{8,15},{9,16}... | collective-permute-start | bytes 1990664
  3110.5 69.6 %collective-permute-start.9 = (f32[48,3456]{1,0:T(8,128)S(1)}, f32[48,3456]{1,0:T(8,128)}, u32[]{:S(2)}, u32[]{:S(2)}) collective-permute-start(f32[48,3456]{1,0:T(8,128)S(1)} %get-tuple-element.386), channel_id=1, source_target_pairs={{0,6},{1,7},{2,8},{3,9},{4,10},{5,11},{6,12},{7,13},{8,14},{9,15},... | collective-permute-start | bytes 1990664
  3114.9 68.3 %collective-permute-start.8 = (f32[48,3456]{1,0:T(8,128)S(1)}, f32[48,3456]{1,0:T(8,128)}, u32[]{:S(2)}, u32[]{:S(2)}) collective-permute-start(f32[48,3456]{1,0:T(8,128)S(1)} %get-tuple-element.386), channel_id=1, source_target_pairs={{0,5},{1,6},{2,7},{3,8},{4,9},{5,10},{6,11},{7,12},{8,13},{9,14},{... | collective-permute-start | bytes 1990664
  3119.0 10.4 collective-permute-start.12
  3129.5 93.9 %collective-permute-start.7 = (f32[48,3456]{1,0:T(8,128)S(1)}, f32[48,3456]{1,0:T(8,128)}, u32[]{:S(2)}, u32[]{:S(2)}) collective-permute-start(f32[48,3456]{1,0:T(8,128)S(1)} %get-tuple-element.386), channel_id=1, source_target_pairs={{0,4},{1,5},{2,6},{3,7},{4,8},{5,9},{6,10},{7,11},{8,12},{9,13},{1... | collective-permute-start | bytes 1990664
  3176.2 49.1 %collective-permute-start.6 = (f32[48,3456]{1,0:T(8,128)S(1)}, f32[48,3456]{1,0:T(8,128)}, u32[]{:S(2)}, u32[]{:S(2)}) collective-permute-start(f32[48,3456]{1,0:T(8,128)S(1)} %get-tuple-element.386), channel_id=1, source_target_pairs={{0,3},{1,4},{2,5},{3,6},{4,7},{5,8},{6,9},{7,10},{8,11},{9,12},{10... | collective-permute-start | bytes 1990664
  3178.2 152.4 %collective-permute-start.5 = (f32[48,3456]{1,0:T(8,128)S(1)}, f32[48,3456]{1,0:T(8,128)}, u32[]{:S(2)}, u32[]{:S(2)}) collective-permute-start(f32[48,3456]{1,0:T(8,128)S(1)} %get-tuple-element.386), channel_id=1, source_target_pairs={{0,2},{1,3},{2,4},{3,5},{4,6},{5,7},{6,8},{7,9},{8,10},{9,11},{10,... | collective-permute-start | bytes 1990664
  3180.1 154.3 %collective-permute-start.4 = (f32[48,3456]{1,0:T(8,128)S(1)}, f32[48,3456]{1,0:T(8,128)}, u32[]{:S(2)}, u32[]{:S(2)}) collective-permute-start(f32[48,3456]{1,0:T(8,128)S(1)} %get-tuple-element.386), channel_id=1, source_target_pairs={{0,1},{1,2},{2,3},{3,4},{4,5},{5,6},{6,7},{7,8},{8,9},{9,10},{10,1... | collective-permute-start | bytes 1990664
  3183.3 157.0 %collective-permute-start.22 = (f32[40,4608]{1,0:T(8,128)}, f32[40,4608]{1,0:T(8,128)}, u32[]{:S(2)}, u32[]{:S(2)}) collective-permute-start(f32[40,4608]{1,0:T(8,128)} %get-tuple-element.387), channel_id=1, source_target_pairs={{0,3},{1,4},{2,5},{3,6},{4,7},{5,8},{6,9},{7,10},{8,11},{9,12},{10... | collective-permute-start | bytes 2211848
  3223.4 158.8 %collective-permute-start.21 = (f32[40,4608]{1,0:T(8,128)}, f32[40,4608]{1,0:T(8,128)}, u32[]{:S(2)}, u32[]{:S(2)}) collective-permute-start(f32[40,4608]{1,0:T(8,128)} %get-tuple-element.387), channel_id=1, source_target_pairs={{0,2},{1,3},{2,4},{3,5},{4,6},{5,7},{6,8},{7,9},{8,10},{9,11},{10,... | collective-permute-start | bytes 2211848
  3225.3 159.9 %collective-permute-start.20 = (f32[40,4608]{1,0:T(8,128)}, f32[40,4608]{1,0:T(8,128)}, u32[]{:S(2)}, u32[]{:S(2)}) collective-permute-start(f32[40,4608]{1,0:T(8,128)} %get-tuple-element.387), channel_id=1, source_target_pairs={{0,1},{1,2},{2,3},{3,4},{4,5},{5,6},{6,7},{7,8},{8,9},{9,10},{10,1... | collective-permute-start | bytes 2211848
  3330.6 74.9 %collective-permute-start.2 = (f32[40,6912]{1,0:T(8,128)}, f32[40,6912]{1,0:T(8,128)}, u32[]{:S(2)}, u32[]{:S(2)}) collective-permute-start(f32[40,6912]{1,0:T(8,128)} %copy-done.15), channel_id=1, source_target_pairs={{0,3},{1,4},{2,5},{3,6},{4,7},{5,8},{6,9},{7,10},{8,11},{9,12},{10... | collective-permute-start | bytes 3317768
  3334.5 71.0 %collective-permute-start.1 = (f32[40,6912]{1,0:T(8,128)}, f32[40,6912]{1,0:T(8,128)}, u32[]{:S(2)}, u32[]{:S(2)}) collective-permute-start(f32[40,6912]{1,0:T(8,128)} %copy-done.15), channel_id=1, source_target_pairs={{0,2},{1,3},{2,4},{3,5},{4,6},{5,7},{6,8},{7,9},{8,10},{9,11},{10,... | collective-permute-start | bytes 3317768
  3340.2 65.2 %collective-permute-start = (f32[40,6912]{1,0:T(8,128)}, f32[40,6912]{1,0:T(8,128)}, u32[]{:S(2)}, u32[]{:S(2)}) collective-permute-start(f32[40,6912]{1,0:T(8,128)} %copy-done.15), channel_id=1, source_target_pairs={{0,1},{1,2},{2,3},{3,4},{4,5},{5,6},{6,7},{7,8},{8,9},{9,10},{10,1... | collective-permute-start | bytes 3317768
  3382.2 23.3 collective-permute-start.3
  (65 other events, 1610.4 us)
Sparse Core Ops, SparseCore 0:
  17.3 82.0 all-gather.19
  102.3 117.8 all-gather.17
  223.2 57.0 all-gather.21
  283.0 91.3 all-gather.23
  376.0 94.2 all-gather.11
  472.0 96.3 all-gather.13
  571.3 87.6 all-gather.15
  881.9 95.0 reduce-scatter.19
  980.0 95.0 reduce-scatter.17
  1081.9 272.4 reduce-scatter.15
where the time goes:
time: 3450 us; the launch traced here: 3440 us
  blocking collectives  2010 us (58%)
  waiting for transfers between devices  434 us (13%)
  local copies, waits for them, and re-layouts  382 us (11%)
  matrix products  361 us (10%)
  starting transfers between devices  125 us (4%)
  other arithmetic  112 us (3%)
    unnamed x4, blocking collectives  1960 us
    unnamed x207, local copies, waits for them, and re-layouts  259 us
    unnamed x26, starting transfers between devices  124 us
    unnamed x36, waiting for transfers between devices  120 us
    all_gather x1, waiting for transfers between devices, body(): lax.all_gather(mod_weight, ('batch', 'seq'), axis=0, tiled=True)  108 us
    all_gather x1, waiting for transfers between devices, body(): lax.all_gather(values, 'seq', axis=1, tiled=True)  85.2 us
  transfers between devices with their start and end apart: 34, of which 8 were waited for; matrix products, arithmetic and copies ran while one was open for 73% of the time, Pallas kernels for 0%

commit v1 on v0

v1 whole, which is shorter than its diff:
```python
import functools

import jax
import jax.numpy as jnp
from jax import lax
from jax.experimental import pallas as pl
from jax.experimental.pallas import tpu as pltpu
from jax.sharding import PartitionSpec as P

HEADS = 16
EPS = 1e-06
GELU_C = 0.7978845608028654
GELU_A = 0.044715
BF = jnp.bfloat16
F32 = jnp.float32
VMEM = 56 * 1024 * 1024


def normalize(values):
    center = values - jnp.mean(values, -1, keepdims=True)
    scale_inv = lax.rsqrt(jnp.mean(center * center, -1, keepdims=True) + EPS)
    return (center * scale_inv, scale_inv)


def norm_back(grad_norm, normed, scale_inv):
    return scale_inv * (
        grad_norm
        - jnp.mean(grad_norm, -1, keepdims=True)
        - normed * jnp.mean(grad_norm * normed, -1, keepdims=True)
    )


def dot_nn(a, b):
    return lax.dot_general(a, b, (((1,), (0,)), ((), ())), preferred_element_type=F32)


def dot_nt(a, b):
    return lax.dot_general(a, b, (((1,), (1,)), ((), ())), preferred_element_type=F32)


def dot_tn(a, b):
    return lax.dot_general(a, b, (((0,), (0,)), ((), ())), preferred_element_type=F32)


def attn_fwd_kernel(
    head_size, h_ref, qk_ref, vo_ref, qb_ref, vb_ref, ob_ref, segc_ref, segr_ref,
    q_out, k_out, v_out, att_out, lse_out, br_out,
):
    width = qb_ref.shape[-1]
    length = segr_ref.shape[-1]
    model = h_ref.shape[-1]
    h = h_ref[...].reshape(length, model)
    qk = dot_nt(h, qk_ref[0])
    v = (dot_nt(h, vo_ref[0, :width]) + vb_ref[0]).astype(BF)
    q = (qk[:, :width] + qb_ref[0]).astype(BF)
    k = qk[:, width:].astype(BF)
    part = q_out.shape[1:]
    q_out[0] = q.reshape(part)
    k_out[0] = k.reshape(part)
    v_out[0] = v.reshape(part)
    allowed = segc_ref[0] == segr_ref[0]
    scale = head_size ** (-0.5)
    pieces = []
    for i in range(width // head_size):
        cut = slice(i * head_size, (i + 1) * head_size)
        score = jnp.where(allowed, dot_nt(k[:, cut], q[:, cut]) * scale, -1e30)
        top = jnp.max(score, 0, keepdims=True)
        prob = jnp.exp(score - top)
        total = jnp.sum(prob, 0, keepdims=True)
        out_t = dot_tn(v[:, cut], prob.astype(BF)) * (1.0 / total)
        pieces.append(out_t.T)
        lse_out[0, 0, i : i + 1, :] = top + jnp.log(total)
    att = jnp.concatenate(pieces, -1).astype(BF)
    att_out[0] = att.reshape(part)
    term = dot_nn(att, vo_ref[0, width:])

    @pl.when(pl.program_id(1) == 0)
    def _():
        br_out[...] = (term + ob_ref[...]).reshape(br_out.shape)

    @pl.when(pl.program_id(1) != 0)
    def _():
        br_out[...] += term.reshape(br_out.shape)


def attn_bwd_kernel(
    head_size, h_ref, gb_ref, qk_ref, vo_ref, q_ref, k_ref, v_ref, att_ref, lse_ref, segc_ref, segr_ref,
    gqk_out, gvo_out, gh_out, gqb_out, gvb_out, sum_qkv, sum_out,
):
    width = q_ref.shape[-1]
    length = segr_ref.shape[-1]
    model = h_ref.shape[-1]
    block, row = pl.program_id(0), pl.program_id(1)
    h = h_ref[:, pl.ds(row, 1)].reshape(length, model)
    gb = gb_ref[:, pl.ds(row, 1)].reshape(length, model)
    grad_att = dot_nt(gb, vo_ref[0, width:]).astype(BF)
    q = q_ref[...].reshape(length, width)
    k = k_ref[...].reshape(length, width)
    v = v_ref[...].reshape(length, width)
    att = att_ref[...].reshape(length, width)
    allowed = segc_ref[0] == segr_ref[0]
    scale = head_size ** (-0.5)
    gq, gk, gv = [], [], []
    for i in range(width // head_size):
        cut = slice(i * head_size, (i + 1) * head_size)
        score = dot_nt(k[:, cut], q[:, cut]) * scale - lse_ref[0, 0, i : i + 1, :]
        prob = jnp.exp(jnp.where(allowed, score, -1e30))
        grad_prob = dot_nt(v[:, cut], grad_att[:, cut])
        inner = jnp.sum(prob * grad_prob, 0, keepdims=True)
        grad_score = (prob * (grad_prob - inner)).astype(BF)
        gq.append((dot_tn(k[:, cut], grad_score) * scale).T)
        gk.append(dot_nn(grad_score, q[:, cut]) * scale)
        gv.append(dot_nn(prob.astype(BF), grad_att[:, cut]))
    gq, gk, gv = [jnp.concatenate(p, -1).astype(BF) for p in (gq, gk, gv)]
    grad_qkv = jnp.concatenate([gq, gk, gv], -1)
    weights = jnp.concatenate([qk_ref[0], vo_ref[0, :width]], 0)
    term = dot_nn(grad_qkv, weights).reshape(gh_out.shape[0], 1, gh_out.shape[2], model)
    term_qkv = dot_tn(grad_qkv, h)
    term_out = dot_tn(att, gb)
    qb_sum = jnp.sum(gq.astype(F32), 0, keepdims=True)
    vb_sum = jnp.sum(gv.astype(F32), 0, keepdims=True)

    @pl.when(block == 0)
    def _():
        gh_out[:, pl.ds(row, 1)] = term

    @pl.when(block != 0)
    def _():
        gh_out[:, pl.ds(row, 1)] += term

    @pl.when(row == 0)
    def _():
        sum_qkv[...] = term_qkv
        sum_out[...] = term_out
        gqb_out[0] = qb_sum
        gvb_out[0] = vb_sum

    @pl.when(row != 0)
    def _():
        sum_qkv[...] += term_qkv
        sum_out[...] += term_out
        gqb_out[0] += qb_sum
        gvb_out[0] += vb_sum

    @pl.when(row == pl.num_programs(1) - 1)
    def _():
        gqk_out[0] = sum_qkv[: 2 * width].astype(BF)
        gvo_out[0, :width] = sum_qkv[2 * width :].astype(BF)
        gvo_out[0, width:] = sum_out[...].astype(BF)


def attn_fwd(hidden, qk_w, vo_w, query_bias, value_bias, out_bias, seg_col, seg_row, head_size):
    n_seq, rows, kept_count, model = hidden.shape
    blocks, _, width = query_bias.shape
    length = n_seq * kept_count
    heads = width // head_size
    token = pl.BlockSpec((n_seq, 1, kept_count, model), lambda r, e: (0, r, 0, 0))
    part = pl.BlockSpec((1, n_seq, 1, kept_count, width), lambda r, e: (e, 0, r, 0, 0))
    weight = pl.BlockSpec((1, 2 * width, model), lambda r, e: (e, 0, 0))
    bias = pl.BlockSpec((1, 1, width), lambda r, e: (e, 0, 0))
    part_shape = jax.ShapeDtypeStruct((blocks, n_seq, rows, kept_count, width), BF)
    return pl.pallas_call(
        functools.partial(attn_fwd_kernel, head_size),
        grid=(rows, blocks),
        in_specs=[
            token, weight, weight, bias, bias,
            pl.BlockSpec((1, model), lambda r, e: (0, 0)),
            pl.BlockSpec((1, length, 1), lambda r, e: (r, 0, 0)),
            pl.BlockSpec((1, 1, length), lambda r, e: (r, 0, 0)),
        ],
        out_specs=[
            part, part, part, part,
            pl.BlockSpec((1, 1, heads, length), lambda r, e: (e, r, 0, 0)),
            token,
        ],
        out_shape=[
            part_shape, part_shape, part_shape, part_shape,
            jax.ShapeDtypeStruct((blocks, rows, heads, length), F32),
            jax.ShapeDtypeStruct(hidden.shape, F32),
        ],
        compiler_params=pltpu.CompilerParams(vmem_limit_bytes=VMEM),
        cost_estimate=pl.CostEstimate(
            flops=2 * rows * length * model * width * blocks * 6, bytes_accessed=40 << 20, transcendentals=0
        ),
    )(hidden, qk_w, vo_w, query_bias, value_bias, out_bias, seg_col, seg_row)


def attn_bwd(hidden, grad_branch, qk_w, vo_w, q, k, v, att, lse, seg_col, seg_row, head_size):
    n_seq, rows, kept_count, model = hidden.shape
    blocks, width = q.shape[0], q.shape[-1]
    length = n_seq * kept_count
    heads = width // head_size
    whole = pl.BlockSpec(hidden.shape, lambda e, r: (0, 0, 0, 0))
    part = pl.BlockSpec((1, n_seq, 1, kept_count, width), lambda e, r: (e, 0, r, 0, 0))
    weight = pl.BlockSpec((1, 2 * width, model), lambda e, r: (e, 0, 0))
    bias = pl.BlockSpec((1, 1, width), lambda e, r: (e, 0, 0))
    return pl.pallas_call(
        functools.partial(attn_bwd_kernel, head_size),
        grid=(blocks, rows),
        in_specs=[
            whole, whole, weight, weight, part, part, part, part,
            pl.BlockSpec((1, 1, heads, length), lambda e, r: (e, r, 0, 0)),
            pl.BlockSpec((1, length, 1), lambda e, r: (r, 0, 0)),
            pl.BlockSpec((1, 1, length), lambda e, r: (r, 0, 0)),
        ],
        out_specs=[weight, weight, whole, bias, bias],
        out_shape=[
            jax.ShapeDtypeStruct(qk_w.shape, BF),
            jax.ShapeDtypeStruct(vo_w.shape, BF),
            jax.ShapeDtypeStruct(hidden.shape, F32),
            jax.ShapeDtypeStruct((blocks, 1, width), F32),
            jax.ShapeDtypeStruct((blocks, 1, width), F32),
        ],
        scratch_shapes=[pltpu.VMEM((3 * width, model), F32), pltpu.VMEM((width, model), F32)],
        compiler_params=pltpu.CompilerParams(vmem_limit_bytes=VMEM),
        cost_estimate=pl.CostEstimate(
            flops=2 * rows * length * model * width * blocks * 14, bytes_accessed=40 << 20, transcendentals=0
        ),
    )(hidden, grad_branch, qk_w, vo_w, q, k, v, att, lse, seg_col, seg_row)


def body(
    n_batch, n_seq,
    tokens, conditioning, segments, kept, cotangent,
    mod_weight, mod_bias, qkv_weight, query_bias, value_bias, out_weight, out_bias,
    up_weight, up_bias, down_weight, down_bias,
):
    row_count, seq_tokens, model = tokens.shape
    kept_count = kept.shape[1]
    slots = conditioning.shape[1]
    head_size = model // HEADS
    rows = row_count // n_seq
    shard = qkv_weight.shape[0]
    n_z = n_batch // 2
    blocks = 2 * n_seq
    width = model // blocks
    flat = n_seq * rows * kept_count
    ff_shard = down_weight.shape[0]
    batch_at = lax.axis_index("batch")
    seq_at = lax.axis_index("seq")
    core_at = batch_at % 2
    block_at = core_at * n_seq + seq_at
    relative = block_at ^ jnp.arange(blocks)
    seq_relative = seq_at ^ jnp.arange(n_seq)
    bits = [1 << i for i in range(n_seq.bit_length() - 1)]
    z_groups = [[2 * z + c for z in range(n_z)] for c in range(2)]

    def over_core(value):
        return lax.ppermute(value, "batch", [(i, i ^ 1) for i in range(n_batch)])

    def over_seq(value, by):
        return lax.ppermute(value, "seq", [(i, i ^ by) for i in range(n_seq)])

    def over_block(value, by):
        moves = []
        for b in range(n_batch):
            for s in range(n_seq):
                to = (b ^ (by // n_seq)) * n_seq + (s ^ (by % n_seq))
                moves.append((b * n_seq + s, to))
        return lax.ppermute(value, ("batch", "seq"), moves)

    def exchange_blocks(value):
        mine = jnp.take(value, relative, axis=0)
        got = [mine[0]] + [over_block(mine[j], j) for j in range(1, blocks)]
        return jnp.take(jnp.stack(got), relative, axis=0)

    def gather_z(value):
        return lax.all_gather(value, "batch", axis=0, tiled=True, axis_index_groups=z_groups)

    def scatter_z(value):
        return lax.psum_scatter(value, "batch", scatter_dimension=0, tiled=True, axis_index_groups=z_groups)

    def gather_blocks(own, order):
        held = {0: own}
        for bit in order:
            for j in list(held):
                held[j | bit] = over_seq(held[j], bit)
        for j in list(held):
            held[j | n_seq] = over_core(held[j])
        return jnp.stack([held[j] for j in range(blocks)])

    def scatter_blocks(value, order):
        held = {j: value[j] for j in range(blocks)}

        def fold(bit, send):
            for j in [j for j in held if j & bit]:
                got = send(held.pop(j))
                held[j ^ bit] = (held[j ^ bit].astype(F32) + got.astype(F32)).astype(BF)

        fold(n_seq, over_core)
        for bit in order:
            fold(bit, lambda v, bit=bit: over_seq(v, bit))
        return held[0]

    def to_rows(value):
        got = [lax.dynamic_slice_in_dim(value, seq_at * rows, rows, 0)]
        for j in range(1, n_seq):
            got.append(over_seq(lax.dynamic_slice_in_dim(value, (seq_at ^ j) * rows, rows, 0), j))
        return jnp.stack(got)

    def from_rows(value):
        got = [value[0]] + [over_seq(value[j], j) for j in range(1, n_seq)]
        return jnp.take(jnp.stack(got), seq_relative, axis=0).reshape((row_count,) + value.shape[2:])

    places = jnp.arange(seq_tokens, dtype=jnp.int32)
    pick = (kept[:, :, None] == places).astype(BF)
    kept_here = jnp.any(kept[:, :, None] == places, 1)

    def pick_kept(value):
        return jnp.einsum("rkt,rtd->rkd", pick, value, preferred_element_type=F32).astype(BF)

    def put_kept(value, base):
        spread = jnp.einsum("rkt,rkd->rtd", pick, value, preferred_element_type=F32).astype(BF)
        return jnp.where(kept_here[:, :, None], spread, base)

    inputs = to_rows(pick_kept(tokens)).reshape(flat, model).astype(F32)

    qkv_cols = qkv_weight.reshape(shard, 3, blocks, width).transpose(2, 0, 1, 3).reshape(blocks, shard, 3 * width)
    qkv_own = gather_z(exchange_blocks(qkv_cols).reshape(blocks * shard, 3 * width)).T
    spread_out = [(d, ((d // n_z) // n_seq + 2 * (d % n_z)) * n_seq + (d // n_z) % n_seq) for d in range(n_batch * n_seq)]
    out_own = gather_z(lax.ppermute(out_weight, ("batch", "seq"), spread_out))
    qk_w = gather_blocks(qkv_own[: 2 * width], bits)
    vo_w = gather_blocks(jnp.concatenate([qkv_own[2 * width :], out_own]), bits[::-1])
    up_cols = up_weight.reshape(shard, n_z, blocks, ff_shard).transpose(2, 0, 1, 3).reshape(blocks, shard, n_z * ff_shard)
    up_own = gather_z(exchange_blocks(up_cols).reshape(blocks * shard, n_z * ff_shard)).T
    down_own = gather_z(down_weight)
    up_w = gather_blocks(up_own, bits).reshape(-1, model)
    down_w = gather_blocks(down_own, bits[::-1]).reshape(-1, model)

    packed = jnp.concatenate([mod_bias, query_bias, value_bias, out_bias, up_bias, down_bias])
    packed = lax.all_gather(packed, ("batch", "seq"), axis=0).astype(F32)
    cuts = [0]
    for item in (mod_bias, query_bias, value_bias, out_bias, up_bias, down_bias):
        cuts.append(cuts[-1] + item.shape[0])
    mod_b, query_b, value_b, out_b, up_b, down_b = [
        packed[:, cuts[i] : cuts[i + 1]].reshape(-1) for i in range(6)
    ]
    query_b = jnp.take(query_b.reshape(blocks, 1, width), relative, axis=0)
    value_b = jnp.take(value_b.reshape(blocks, 1, width), relative, axis=0)
    up_b = jnp.take(
        up_b.reshape(n_z, blocks, ff_shard).transpose(1, 0, 2).reshape(blocks, -1), relative, axis=0
    ).reshape(1, -1)

    numbers = jnp.arange(slots, dtype=jnp.int32)
    query_seg = jnp.take_along_axis(segments, kept, axis=1)
    kept_hits = jnp.sum((query_seg[:, :, None] == numbers).astype(jnp.int32), 1)
    all_hits = jnp.sum((segments[:, :, None] == numbers).astype(jnp.int32), 1)
    small = jnp.concatenate([query_seg, kept_hits, all_hits - kept_hits], -1)
    small = lax.all_gather(small, "seq", axis=0)
    sample_counts = jnp.sum(small[:, :, kept_count:], 0).reshape(row_count, 2, slots).transpose(0, 2, 1)
    seg = lax.dynamic_slice_in_dim(small[:, :, :kept_count], seq_at * rows, rows, 1)
    seg = jnp.take(seg, seq_relative, axis=0)
    seg_rows = seg.transpose(1, 0, 2).reshape(rows, 1, n_seq * kept_count)
    seg_cols = seg_rows.reshape(rows, n_seq * kept_count, 1)

    cond_float = conditioning.astype(F32)
    cond_act = (cond_float / (1.0 + jnp.exp(-cond_float))).astype(BF)
    act_all = lax.all_gather(cond_act, "batch", axis=0)
    act_mine = lax.dynamic_slice_in_dim(act_all, seq_at * rows, rows, 1).reshape(-1, model)
    act_cols = lax.dynamic_slice_in_dim(act_mine, batch_at * n_seq * shard, n_seq * shard, 1)
    mod_rows = lax.all_gather(mod_weight, "seq", axis=0, tiled=True)
    mod_part = jnp.dot(act_cols, mod_rows, preferred_element_type=F32)
    modulation = lax.psum_scatter(mod_part, "batch", scatter_dimension=0, tiled=True) + mod_b
    modulation = modulation.reshape(rows, slots, 6, model)

    hit = seg[:, :, :, None, None] == numbers[:, None]

    def token_mod(index):
        table = modulation[:, :, index]
        value = table[None, :, None, 0]
        for slot in range(1, slots):
            value = jnp.where(seg[:, :, :, None] == slot, table[None, :, None, slot], value)
        return value.reshape(flat, model)

    def slot_sums(value):
        split = value.reshape(n_seq, rows, kept_count, model)
        sums = [jnp.sum(jnp.where(seg[:, :, :, None] == slot, split, 0.0), (0, 2)) for slot in range(slots)]
        return jnp.stack(sums, 1)

    normed_one, inv_one = normalize(inputs)
    hidden_one = (normed_one * (1.0 + token_mod(1)) + token_mod(0)).astype(BF)
    hidden_one = hidden_one.reshape(n_seq, rows, kept_count, model)
    q, k, v, att, lse, branch_attn = attn_fwd(
        hidden_one, qk_w, vo_w, query_b, value_b, out_b.reshape(1, -1), seg_cols, seg_rows, head_size
    )
    branch_attn = branch_attn.reshape(flat, model)
    mid = inputs + token_mod(2) * branch_attn
    normed_two, inv_two = normalize(mid)
    hidden_two = (normed_two * (1.0 + token_mod(4)) + token_mod(3)).astype(BF)

    grad_result = to_rows(pick_kept(cotangent)).reshape(flat, model).astype(F32)
    grad_mlp = (grad_result * token_mod(5)).astype(BF)

    pre = dot_nt(hidden_two, up_w) + up_b
    tanh_part = jnp.tanh(GELU_C * (pre + GELU_A * pre * pre * pre))
    activated = (0.5 * pre * (1.0 + tanh_part)).astype(BF)
    slope = 0.5 * (1.0 + tanh_part) + 0.5 * pre * (1.0 - tanh_part * tanh_part) * GELU_C * (
        1.0 + 3.0 * GELU_A * pre * pre
    )
    branch_mlp = dot_nn(activated, down_w) + down_b
    grad_pre = (dot_nt(grad_mlp, down_w) * slope).astype(BF)
    grad_down = dot_tn(activated, grad_mlp).astype(BF).reshape(blocks, -1, model)
    grad_up = dot_tn(grad_pre, hidden_two).astype(BF).reshape(blocks, -1, model)
    grad_hidden_two = dot_nn(grad_pre, up_w)
    grad_up_bias = jnp.sum(grad_pre.astype(F32), 0)
    grad_down_bias = jnp.sum(grad_mlp.astype(F32), 0)

    result = (mid + token_mod(5) * branch_mlp).astype(BF).reshape(n_seq, rows, kept_count, model)
    output = put_kept(from_rows(result), tokens)

    down_sum = scatter_z(scatter_blocks(grad_down, bits))
    up_sum = scatter_z(scatter_blocks(grad_up, bits[::-1]).T)

    grad_mid = grad_result + norm_back(grad_hidden_two * (1.0 + token_mod(4)), normed_two, inv_two)
    grad_branch = (grad_mid * token_mod(2)).astype(BF)
    grad_out_bias = jnp.sum(grad_branch.astype(F32), 0)
    grad_qk, grad_vo, grad_hidden_one, grad_query_bias, grad_value_bias = attn_bwd(
        hidden_one, grad_branch.reshape(hidden_one.shape), qk_w, vo_w, q, k, v, att, lse, seg_cols, seg_rows, head_size
    )
    grad_hidden_one = grad_hidden_one.reshape(flat, model)
    grad_inputs = grad_mid + norm_back(grad_hidden_one * (1.0 + token_mod(1)), normed_one, inv_one)
    grad_inputs = grad_inputs.astype(BF).reshape(n_seq, rows, kept_count, model)
    tokens_grad = put_kept(from_rows(grad_inputs), cotangent)

    qk_sum = scatter_blocks(grad_qk, bits)
    vo_sum = scatter_blocks(grad_vo, bits[::-1])
    qkv_sum = scatter_z(jnp.concatenate([qk_sum, vo_sum[:width]]).T)
    out_sum = scatter_z(vo_sum[width:])

    def columns(value, parts):
        value = exchange_blocks(value.reshape(blocks, shard, -1)).reshape(blocks, shard, parts, -1)
        return value.transpose(1, 2, 0, 3).reshape(shard, -1).astype(F32)

    qkv_grad = columns(qkv_sum, 3)
    up_grad = columns(up_sum, n_z)
    out_grad = lax.ppermute(out_sum, ("batch", "seq"), [(t, d) for d, t in spread_out]).astype(F32)
    down_grad = down_sum.astype(F32)

    pieces = [
        slot_sums(grad_hidden_one),
        slot_sums(grad_hidden_one * normed_one),
        slot_sums(grad_mid * branch_attn),
        slot_sums(grad_hidden_two),
        slot_sums(grad_hidden_two * normed_two),
        slot_sums(grad_result * branch_mlp),
    ]
    grad_mod = jnp.concatenate(pieces, -1).reshape(rows * slots, 6 * model).astype(BF)
    grad_mod = lax.all_gather(grad_mod, ("batch", "seq"), axis=0, tiled=True)
    device_at = batch_at * n_seq + seq_at
    act_own = lax.dynamic_slice_in_dim(act_all.reshape(-1, model), device_at * shard, shard, 1)
    mod_grad = dot_tn(act_own, grad_mod)
    mod_bias_grad = lax.dynamic_slice_in_dim(jnp.sum(grad_mod.astype(F32), 0), device_at * mod_bias.shape[0], mod_bias.shape[0])

    def natural(value):
        return jnp.take(value.reshape(blocks, -1), relative, axis=0)

    natural_up = natural(grad_up_bias).reshape(blocks, n_z, ff_shard).transpose(1, 0, 2)
    shares = [
        value.reshape(n_batch * n_seq, -1)
        for value in (natural(grad_query_bias), natural(grad_value_bias), grad_out_bias, natural_up, grad_down_bias)
    ]
    bias_sum = lax.psum_scatter(jnp.concatenate(shares, -1), ("batch", "seq"), scatter_dimension=0, tiled=True)[0]
    bias_grads = []
    at = 0
    for share in shares:
        bias_grads.append(lax.slice_in_dim(bias_sum, at, at + share.shape[1]))
        at += share.shape[1]
    return (
        output, tokens_grad, mod_grad, mod_bias_grad, qkv_grad, bias_grads[0], bias_grads[1],
        out_grad, bias_grads[2], up_grad, bias_grads[3], down_grad, bias_grads[4], sample_counts,
    )


def solution(mesh):
    both = ("batch", "seq")
    row_split = P("batch", "seq", None)
    matrix = P(both, None)
    vector = P(both)
    return jax.shard_map(
        functools.partial(body, mesh.shape["batch"], mesh.shape["seq"]),
        mesh=mesh,
        in_specs=(
            row_split, P("batch", None, None), P("batch", "seq"), P("batch", "seq"), row_split,
            matrix, vector, matrix, vector, vector, matrix, vector, matrix, vector, matrix, vector,
        ),
        out_specs=(
            row_split, row_split, matrix, vector, matrix, vector, vector,
            matrix, vector, matrix, vector, matrix, vector, P("batch", None, None),
        ),
        check_vma=False,
    )
```

time: 3450 us -> 1170 us (0.34)
  blocking collectives: 2010 us -> 176 us
  waiting for transfers between devices: 434 us -> 213 us
  matrix products: 361 us -> 160 us
  local copies, waits for them, and re-layouts: 382 us -> 199 us
  Pallas kernels: 0 us -> 144 us
    unnamed x4 -> x3, blocking collectives: 1960 us -> 116 us
    all_gather x7 -> x4, waiting for transfers between devices: 314 us -> 0.01 us  [the longest x2 0.01 us: gather_z(): lax.all_gather(value, 'batch', axis=0, tiled=True, axis_index_groups=z_gr...]
    ppermute x0 -> x98, waiting for transfers between devices: none -> 212 us  [the longest x36 199 us: over_seq(): return lax.ppermute(value, 'seq', [(i, i ^ by) for i in range(n_seq)])]
    dot_general x38 -> x12, matrix products: 361 us -> 160 us  [the longest x2 49.5 us: dot_nn(): lax.dot_general(a, b, (((1,), (0,)), ((), ())), preferred_element_type=F32)]
    unnamed x207 -> x341, local copies, waits for them, and re-layouts: 259 us -> 77 us
    pallas_call x0 -> x2, Pallas kernels: none -> 144 us  [the longest x1 88 us: attn_bwd(): pl.pallas_call(functools.partial(attn_bwd_kernel, head_size), grid=(block...]
    unnamed x26 -> x1, starting transfers between devices: 124 us -> 1.3 us
    ppermute x0 -> x98, starting transfers between devices: none -> 122 us  [the longest x32 48.7 us: over_core(): return lax.ppermute(value, 'batch', [(i, i ^ 1) for i in range(n_batch)])]
  transfers between devices with their start and end apart: 34 -> 107, of which waited for: 8 -> 26; matrix products, arithmetic and copies ran while one was open for 73% -> 33% of each run, Pallas kernels for 0% -> 12%
where the time goes in v1:
time: 1170 us; the launch traced here: 1160 us
  waiting for transfers between devices  213 us (18%)
  local copies, waits for them, and re-layouts  199 us (17%)
  blocking collectives  176 us (15%)
  matrix products  160 us (14%)
  Pallas kernels  144 us (12%)
  other arithmetic  127 us (11%)
  starting transfers between devices  124 us (11%)
  between operations  17.7 us (2%)
    ppermute x36, waiting for transfers between devices, over_seq(): return lax.ppermute(value, 'seq', [(i, i ^ by) for i in range(n_seq)])  199 us
    unnamed x3, blocking collectives  116 us
    pallas_call x1, Pallas kernels, attn_bwd(): pl.pallas_call(functools.partial(attn_bwd_kernel, head_size), grid=(block...  88 us
    unnamed x341, local copies, waits for them, and re-layouts  77 us
    pallas_call x1, Pallas kernels, attn_fwd(): pl.pallas_call(functools.partial(attn_fwd_kernel, head_size), grid=(rows,...  56.1 us
    dot_general x2, matrix products, dot_nn(): lax.dot_general(a, b, (((1,), (0,)), ((), ())), preferred_element_type=F32)  49.5 us
    ppermute x32, starting transfers between devices, over_core(): return lax.ppermute(value, 'batch', [(i, i ^ 1) for i in range(n_batch)])  48.7 us
    dot_general x2, matrix products, dot_nt(): lax.dot_general(a, b, (((1,), (1,)), ((), ())), preferred_element_type=F32)  47 us
  transfers between devices with their start and end apart: 107, of which 26 were waited for; matrix products, arithmetic and copies ran while one was open for 33% of the time, Pallas kernels for 12%

profile of v1, /device:TPU:1, one launch (start us, length us, event | category | flops | bytes accessed | tf_op | source)
XLA Modules:
  0.0 1159.9 jit_solution(7539707073993170343)
XLA Ops:
  32.6 41.3 %all-reduce = bf16[16128]{0:T(1024)(128)(2,1)S(1)} all-reduce(bf16[16128]{0:T(1024)(128)(2,1)S(1)} %dynamic-update-slice), channel_id=4, replica_groups=mesh['batch'=8,'seq'=4] {'batch','seq'}, use_global_device_ids=true, to_apply=%add | all-reduce | flops 16128 | bytes 64512
  76.3 6.8 gather_fusion.1
  83.5 5.3 all-gather
  93.1 19.7 %all-gather.1 = bf16[64,4,1152]{2,1,0:T(4,128)(2,1)S(1)} all-gather(bf16[8,4,1152]{2,1,0:T(4,128)(2,1)S(1)} %fusion.70), channel_id=3, replica_groups=mesh['batch'=8,'seq'=4] {'batch'}, dimensions={0}, use_global_device_ids=true | all-gather | bytes 663552 | tf_op jit(solution)/shard_map/all_gather | solution.py:358
  118.9 4.7 convolution_convert_fusion.4
  162.1 21.3 %all_gather.43 = bf16[1152,432]{1,0:T(8,128)(2,1)} all-gather(bf16[288,432]{1,0:T(8,128)(2,1)} %reshape.819), channel_id=1, replica_groups={{0,8,16,24},{4,12,20,28},{1,9,17,25},{5,13,21,29},{2,10,18,26},{6,14,22..., dimensions={0}, use_global_device_ids=true | all-gather | bytes 1244160 | tf_op jit(solution)/shard_map/all_gather | solution.py:268
  192.1 13.4 %all-gather.4 = bf16[4,36,1152]{2,1,0:T(8,128)(2,1)} all-gather(bf16[1,36,1152]{2,1,0:T(8,128)(2,1)} %bitcast.40), channel_id=1, replica_groups={{0,8,16,24},{4,12,20,28},{1,9,17,25},{5,13,21,29},{2,10,18,26},{6,14,22..., dimensions={0}, use_global_device_ids=true | all-gather | bytes 414720 | tf_op jit(solution)/shard_map/all_gather | solution.py:268
  212.9 4.7 collective-permute-start.13
  223.1 10.5 collective-permute-start.21
  238.1 9.7 collective-permute-start.14
  252.4 5.1 collective-permute-start.15
  264.2 11.9 %collective-permute-done.20 = bf16[288,1152]{1,0:T(8,128)(2,1)} collective-permute-done((bf16[288,1152]{1,0:T(8,128)(2,1)S(1)}, bf16[288,1152]{1,0:T(8,128)(2,1)}, u32[]{:S(2)}, u32[]{:S(2)}) %collective-permute-start.20) | collective-permute-done | bytes 663584 | tf_op jit(solution)/shard_map/ppermute | solution.py:252
  302.4 9.7 collective-permute-done.39
  320.9 19.6 %collective-permute-done.32 = bf16[576,1152]{1,0:T(8,128)(2,1)} collective-permute-done((bf16[576,1152]{1,0:T(8,128)(2,1)}, bf16[576,1152]{1,0:T(8,128)(2,1)}, u32[]{:S(2)}, u32[]{:S(2)}) %collective-permute-start.32) | collective-permute-done | bytes 1327136 | tf_op jit(solution)/shard_map/ppermute | solution.py:252
  357.4 11.6 %collective-permute-done.41 = bf16[576,1152]{1,0:T(8,128)(2,1)} collective-permute-done((bf16[576,1152]{1,0:T(8,128)(2,1)}, bf16[576,1152]{1,0:T(8,128)(2,1)}, u32[]{:S(2)}, u32[]{:S(2)}) %collective-permute-start.41) | collective-permute-done | bytes 1327136 | tf_op jit(solution)/shard_map/ppermute | solution.py:252
  381.0 22.9 %collective-permute-done.34 = bf16[576,1152]{1,0:T(8,128)(2,1)} collective-permute-done((bf16[576,1152]{1,0:T(8,128)(2,1)}, bf16[576,1152]{1,0:T(8,128)(2,1)}, u32[]{:S(2)}, u32[]{:S(2)}) %collective-permute-start.34) | collective-permute-done | bytes 1327136 | tf_op jit(solution)/shard_map/ppermute | solution.py:252
  432.4 16.1 %copy.242 = bf16[8,576,1152]{2,1,0:T(8,128)(2,1)} copy(bf16[8,576,1152]{1,2,0:T(8,128)(2,1)} %bitcast_dynamic-update-slice_fusion.1) | data formatting | bytes 21233664 | tf_op jit(solution)/shard_map/stack | solution.py:280
  454.2 4.7 fusion.44.h_ref
  459.0 56.1 %shard_map.263 = (bf16[8,4,2,128,144]{4,3,2,1,0:T(8,128)(2,1)}, bf16[8,4,2,128,144]{4,3,2,1,0:T(8,128)(2,1)}, bf16[8,4,2,128,144]{4,3,2,1,0:T(8,128)(2,1)}, bf16...) custom-call(bf16[4,2,128,1152]{3,2,1,0:T(8,128)(2,1)} %fusion.44.h_ref, ...), custom_call_target="tpu_custom_call" | custom-call | flops 16307453952 | bytes 41943040 | tf_op jit(solution)/shard_map/pallas_call | solution.py:162
  522.9 4.7 add_convert_fusion
  527.7 18.7 %fusion.97 = f32[1024,4608]{1,0:T(8,128)} fusion(bf16[1024,1152]{1,0:T(8,128)(2,1)S(1)} %bitcast.784, bf16[4608,1152]{1,0:T(8,128)(2,1)} %bitcast.757), kind=kOutput, calls=%fused_computation.437 | convolution fusion | flops 10871635968 | bytes 31850496 | tf_op jit(solution)/shard_map/dot_general | solution.py:38
  546.6 5.0 convert_reduce_fusion.3
  551.6 25.5 %fusion.27 = (bf16[1024,1152]{1,0:T(8,128)(2,1)}, f32[1024,1152]{1,0:T(8,128)}, f32[1024,1152]{1,0:T(8,128)}) fusion(f32[2,1152]{1,0:T(2,128)} %bitcast.842, f32[2,1152]{1,0:T(2,128)} %bitcast.845, f32[2,1152]{1,0:T(2,128)} %bitcast.848, f32[2,1152]{1,0:T(2,128)} %bitcast.851, pred[1024]{0:T(1024)(128)(4,1)} %eq.74, pred[1024]{0:T(1024)(128)(4,1)} %eq.72, ...), kind=kOutput, calls=%fused_computation.61 | convolution fusion | flops 10931798016 | bytes 43709952 | tf_op jit(solution)/shard_map/dot_general | solution.py:34
  577.2 23.2 %convolution_convert_fusion = bf16[4608,1152]{1,0:T(8,128)(2,1)} fusion(bf16[1024,1152]{1,0:T(8,128)(2,1)} %get-tuple-element.237, f32[1024,4608]{1,0:T(8,128)} %fusion.97, f32[4608]{0:T(1024)} %add.310), kind=kOutput, calls=%fused_computation.20 | convolution fusion | flops 10924130304 | bytes 31868928 | tf_op jit(solution)/shard_map/dot_general | solution.py:42
  600.6 28.3 %convert_reduce_fusion = (f32[4608]{0:T(1024)}, bf16[1024,4608]{1,0:T(8,128)(2,1)}) fusion(f32[1024,4608]{1,0:T(8,128)} %fusion.97, f32[4608]{0:T(1024)S(1)} %copy-done.72, bf16[1024,1152]{1,0:T(8,128)(2,1)S(1)} %bitcast.781, bf16[4608,1152]{1,0:T(8,128)(2,1)} %bitcast.763), kind=kOutput, calls=%fused_computation.29 | convolution fusion | flops 10975440896 | bytes 41324544 | tf_op jit(solution)/shard_map/dot_general | solution.py:38
  629.0 7.4 fusion.11
  636.4 15.6 %convolution_convert_fusion.1 = bf16[4608,1152]{1,0:T(8,128)(2,1)S(1)} fusion(bf16[1024,4608]{1,0:T(8,128)(2,1)} %get-tuple-element.339, bf16[1024,1152]{1,0:T(8,128)(2,1)S(1)} %get-tuple-element.194), kind=kOutput, calls=%fused_computation.21 | convolution fusion | flops 10876944384 | bytes 22413312 | tf_op jit(solution)/shard_map/dot_general | solution.py:42
  658.3 24.0 %fusion.80 = (f32[1024]{0:T(1024)}, f32[1024]{0:T(1024)}, f32[1024,1152]{1,0:T(8,128)}, bf16[1024,1152]{1,0:T(8,128)(2,1)}, f32[1024,1152]{1,0:T(8,128)S(1)}) fusion(f32[2,1152]{1,0:T(2,128)} %bitcast.814, f32[2,1152]{1,0:T(2,128)} %bitcast.818, pred[1024]{0:T(1024)(128)(4,1)} %eq.74, f32[2,1152]{1,0:T(2,128)} %bitcast.822, pred[1024]{0:T(1024)(128)(4,1)} %eq.72, ...), kind=kOutput, calls=%fused_computation.423 | convolution fusion | flops 10891687936 | bytes 41380864 | tf_op jit(solution)/shard_map/dot_general | solution.py:34
  683.7 10.4 convert_reduce_fusion.4
  694.0 88.0 %shard_map.264 = (bf16[8,288,1152]{2,1,0:T(8,128)(2,1)}, bf16[8,288,1152]{2,1,0:T(8,128)(2,1)}, f32[4,2,128,1152]{3,2,1,0:T(8,128)}, f32[8,1,144]{2,1,0:T(1,128)}, f32[8,1,144]{2,1,0:T(1,128)}) custom-call(bf16[4,2,128,1152]{3,2,1,0:T(8,128)(2,1)} %fusion.44.h_ref, bf16[4,2,128,1152]{3,2,1,0:T(8,128)(2,1)} %bitcast.778, ...), custom_call_target="tpu_custom_call" | custom-call | flops 38050725888 | bytes 41943040 | tf_op jit(solution)/shard_map/pallas_call | solution.py:197
  786.8 8.0 select_reduce_fusion.19
  802.3 11.0 collective-permute-done.67
  823.6 8.5 collective-permute-done.64
  834.3 13.1 %collective-permute-done.68 = bf16[288,1152]{1,0:T(8,128)(2,1)S(1)} collective-permute-done((bf16[288,1152]{1,0:T(8,128)(2,1)S(1)}, bf16[288,1152]{1,0:T(8,128)(2,1)S(1)}, u32[]{:S(2)}, u32[]{:S(2)}) %collective-permute-start.68) | collective-permute-done | bytes 663584 | tf_op jit(solution)/shard_map/ppermute | solution.py:252
  856.2 25.8 %collective-permute-done.82 = bf16[576,1152]{1,0:T(8,128)(2,1)} collective-permute-done((bf16[576,1152]{1,0:T(8,128)(2,1)}, bf16[576,1152]{1,0:T(8,128)(2,1)}, u32[]{:S(2)}, u32[]{:S(2)}) %collective-permute-start.82) | collective-permute-done | bytes 1327136 | tf_op jit(solution)/shard_map/ppermute | solution.py:252
  886.2 4.7 add_convert_fusion.6
  894.2 17.8 %collective-permute-done.79 = bf16[576,1152]{1,0:T(8,128)(2,1)S(1)} collective-permute-done((bf16[576,1152]{1,0:T(8,128)(2,1)}, bf16[576,1152]{1,0:T(8,128)(2,1)S(1)}, u32[]{:S(2)}, u32[]{:S(2)}) %collective-permute-start.79) | collective-permute-done | bytes 1327136 | tf_op jit(solution)/shard_map/ppermute | solution.py:252
  920.4 22.8 %collective-permute-done.96 = bf16[576,1152]{1,0:T(8,128)(2,1)} collective-permute-done((bf16[576,1152]{1,0:T(8,128)(2,1)}, bf16[576,1152]{1,0:T(8,128)(2,1)}, u32[]{:S(2)}, u32[]{:S(2)}) %collective-permute-start.96) | collective-permute-done | bytes 1327136 | tf_op jit(solution)/shard_map/ppermute | solution.py:252
  953.4 10.0 bitcast_multiply_fusion.2
  965.9 5.7 collective-permute-done.93
  972.6 11.5 collective-permute-done.97
  991.2 11.4 select_reduce_fusion.15
  1006.6 54.3 %all-reduce.1 = f32[32,288]{1,0:T(8,128)S(1)} all-reduce(f32[32,288]{1,0:T(8,128)S(1)} %concatenate.24), channel_id=7, replica_groups=mesh['batch'=8,'seq'=4] {'batch','seq'}, use_global_device_ids=true, to_apply=%region_41.48.clone | all-reduce | flops 9216 | bytes 73728
  1071.2 4.4 broadcast_select_fusion.2
  1075.6 20.5 %fusion = bf16[48,1152]{1,0:T(8,128)(2,1)S(1)} fusion(bf16[144,1152]{1,0:T(8,128)(2,1)S(1)} %copy-done.14), kind=kCustom, calls=%all-reduce-scatter | all-reduce-scatter fusion | flops 221185 | bytes 442880
  1097.5 5.4 broadcast_select_fusion
  1103.3 5.9 collective-permute-start.76
  1111.1 4.9 broadcast_select_fusion.1
  (734 shorter events, 350.9 us)
Async XLA Ops:
  7.2 274.4 %all-gather.12.cloned.1.call-start = ((), (), s32[]{:S(2)}) async-start(), calls=%async_computation.6 | async-start | bytes 1658880 | tf_op jit(solution)/shard_map/all_gather | solution.py:268
  7.9 280.1 %all-gather.10.cloned.1.call-start = ((), (), s32[]{:S(2)}) async-start(), calls=%async_computation.5 | async-start | bytes 1843200 | tf_op jit(solution)/shard_map/all_gather | solution.py:268
  26.1 270.3 %all-gather.16.cloned.1.call-start = ((), (), s32[]{:S(2)}) async-start(), calls=%async_computation.9 | async-start | bytes 2764800 | tf_op jit(solution)/shard_map/all_gather | solution.py:361
  28.8 109.5 %collective-permute-start.3 = (bf16[36,432]{1,0:T(8,128)(2,1)}, bf16[36,432]{1,0:T(8,128)(2,1)}, u32[]{:S(2)}, u32[]{:S(2)}) collective-permute-start(bf16[36,432]{1,0:T(8,128)(2,1)} %get-tuple-element.287), channel_id=1, source_target_pairs={{0,1},{1,0},{2,3},{3,2},{4,5},{5,4},{6,7},{7,6},{8,9},{9,8},{10,11... | collective-permute-start | bytes 93320 | tf_op jit(solution)/shard_map/ppermute | solution.py:260
  28.9 110.9 %collective-permute-start.4 = (bf16[36,432]{1,0:T(8,128)(2,1)}, bf16[36,432]{1,0:T(8,128)(2,1)}, u32[]{:S(2)}, u32[]{:S(2)}) collective-permute-start(bf16[36,432]{1,0:T(8,128)(2,1)} %get-tuple-element.286), channel_id=1, source_target_pairs={{0,2},{1,3},{2,0},{3,1},{4,6},{5,7},{6,4},{7,5},{8,10},{9,11},{10,... | collective-permute-start | bytes 93320 | tf_op jit(solution)/shard_map/ppermute | solution.py:260
  29.4 113.1 %collective-permute-start.5 = (bf16[36,432]{1,0:T(8,128)(2,1)}, bf16[36,432]{1,0:T(8,128)(2,1)}, u32[]{:S(2)}, u32[]{:S(2)}) collective-permute-start(bf16[36,432]{1,0:T(8,128)(2,1)} %get-tuple-element.285), channel_id=1, source_target_pairs={{0,3},{1,2},{2,1},{3,0},{4,7},{5,6},{6,5},{7,4},{8,11},{9,10},{10,... | collective-permute-start | bytes 93320 | tf_op jit(solution)/shard_map/ppermute | solution.py:260
  31.5 116.5 %collective-permute-start.6 = (bf16[36,432]{1,0:T(8,128)(2,1)}, bf16[36,432]{1,0:T(8,128)(2,1)}, u32[]{:S(2)}, u32[]{:S(2)}) collective-permute-start(bf16[36,432]{1,0:T(8,128)(2,1)} %get-tuple-element.284), channel_id=1, source_target_pairs={{0,4},{1,5},{2,6},{3,7},{4,0},{5,1},{6,2},{7,3},{8,12},{9,13},{10,... | collective-permute-start | bytes 93320 | tf_op jit(solution)/shard_map/ppermute | solution.py:260
  31.9 117.5 %collective-permute-start.7 = (bf16[36,432]{1,0:T(8,128)(2,1)}, bf16[36,432]{1,0:T(8,128)(2,1)}, u32[]{:S(2)}, u32[]{:S(2)}) collective-permute-start(bf16[36,432]{1,0:T(8,128)(2,1)} %get-tuple-element.283), channel_id=1, source_target_pairs={{0,5},{1,4},{2,7},{3,6},{4,1},{5,0},{6,3},{7,2},{8,13},{9,12},{10,... | collective-permute-start | bytes 93320 | tf_op jit(solution)/shard_map/ppermute | solution.py:260
  32.1 416.4 %reduce-scatter.11.cloned.1.call-start = ((), (), s32[]{:S(2)}) async-start(), calls=%async_computation.4 | async-start | bytes 1990656 | tf_op jit(solution)/shard_map/reduce_scatter | solution.py:363
  142.5 49.0 %collective-permute-start.17 = (bf16[36,1152]{1,0:T(8,128)(2,1)}, bf16[36,1152]{1,0:T(8,128)(2,1)}, u32[]{:S(2)}, u32[]{:S(2)}) collective-permute-start(bf16[36,1152]{1,0:T(8,128)(2,1)} %param.38), channel_id=1, source_target_pairs={{0,0},{1,8},{2,16},{3,24},{4,1},{5,9},{6,17},{7,25},{8,2},{9,10},{... | collective-permute-start | bytes 248840 | tf_op jit(solution)/shard_map/ppermute | solution.py:321
  148.0 62.4 %collective-permute-start = (bf16[2,128,1152]{2,1,0:T(8,128)(2,1)}, bf16[2,128,1152]{2,1,0:T(8,128)(2,1)S(1)}, u32[]{:S(2)}, u32[]{:S(2)}) collective-permute-start(bf16[2,128,1152]{2,1,0:T(8,128)(2,1)} %get-tuple-element.254), channel_id=1, source_target_pairs={{0,1},{1,0},{2,3},{3,2},{4,5},{5,4},{6,7},{7,6},{8,9},{9,8},{10,11... | collective-permute-start | bytes 1769480 | tf_op jit(solution)/shard_map/ppermute | solution.py:252
  149.4 63.5 %collective-permute-start.1 = (bf16[2,128,1152]{2,1,0:T(8,128)(2,1)}, bf16[2,128,1152]{2,1,0:T(8,128)(2,1)S(1)}, u32[]{:S(2)}, u32[]{:S(2)}) collective-permute-start(bf16[2,128,1152]{2,1,0:T(8,128)(2,1)} %get-tuple-element.253), channel_id=1, source_target_pairs={{0,2},{1,3},{2,0},{3,1},{4,6},{5,7},{6,4},{7,5},{8,10},{9,11},{10,... | collective-permute-start | bytes 1769480 | tf_op jit(solution)/shard_map/ppermute | solution.py:252
  153.7 63.9 %collective-permute-start.2 = (bf16[2,128,1152]{2,1,0:T(8,128)(2,1)}, bf16[2,128,1152]{2,1,0:T(8,128)(2,1)S(1)}, u32[]{:S(2)}, u32[]{:S(2)}) collective-permute-start(bf16[2,128,1152]{2,1,0:T(8,128)(2,1)} %get-tuple-element.252), channel_id=1, source_target_pairs={{0,3},{1,2},{2,1},{3,0},{4,7},{5,6},{6,5},{7,4},{8,11},{9,10},{10,... | collective-permute-start | bytes 1769480 | tf_op jit(solution)/shard_map/ppermute | solution.py:252
  154.3 392.2 %collective-permute-start.49 = (bf16[2,128,1152]{2,1,0:T(8,128)(2,1)}, bf16[2,128,1152]{2,1,0:T(8,128)(2,1)S(1)}, u32[]{:S(2)}, u32[]{:S(2)}) collective-permute-start(bf16[2,128,1152]{2,1,0:T(8,128)(2,1)} %get-tuple-element.246), channel_id=1, source_target_pairs={{0,1},{1,0},{2,3},{3,2},{4,5},{5,4},{6,7},{7,6},{8,9},{9,8},{10,11... | collective-permute-start | bytes 1769480 | tf_op jit(solution)/shard_map/ppermute | solution.py:252
  212.9 46.6 %collective-permute-start.13 = (bf16[288,1152]{1,0:T(8,128)(2,1)}, bf16[288,1152]{1,0:T(8,128)(2,1)S(1)}, u32[]{:S(2)}, u32[]{:S(2)}) collective-permute-start(bf16[288,1152]{1,0:T(8,128)(2,1)} %slice.607), channel_id=1, source_target_pairs={{0,4},{4,0},{8,12},{12,8},{16,20},{20,16},{24,28},{28,24},{1,5},{5... | collective-permute-start | bytes 1990664 | tf_op jit(solution)/shard_map/ppermute | solution.py:249
  223.1 55.8 %collective-permute-start.21 = (bf16[288,1152]{1,0:T(8,128)(2,1)S(1)}, bf16[288,1152]{1,0:T(8,128)(2,1)S(1)}, u32[]{:S(2)}, u32[]{:S(2)}) collective-permute-start(bf16[288,1152]{1,0:T(8,128)(2,1)S(1)} %pad_maximum_fusion.4), channel_id=1, source_target_pairs={{0,4},{4,0},{8,12},{12,8},{16,20},{20,16},{24,28},{28,24},{1,5},{5... | collective-permute-start | bytes 1990664 | tf_op jit(solution)/shard_map/ppermute | solution.py:249
  283.1 31.4 %collective-permute-start.40 = (bf16[576,1152]{1,0:T(8,128)(2,1)}, bf16[576,1152]{1,0:T(8,128)(2,1)}, u32[]{:S(2)}, u32[]{:S(2)}) collective-permute-start(bf16[576,1152]{1,0:T(8,128)(2,1)} %all-gather.12.cloned.1.call-done), channel_id=1, source_target_pairs={{0,2},{1,3},{2,0},{3,1},{4,6},{5,7},{6,4},{7,5},{8,10},{9,11},{10,... | collective-permute-start | bytes 3981320 | tf_op jit(solution)/shard_map/ppermute | solution.py:252
  290.7 49.9 %collective-permute-start.32 = (bf16[576,1152]{1,0:T(8,128)(2,1)}, bf16[576,1152]{1,0:T(8,128)(2,1)}, u32[]{:S(2)}, u32[]{:S(2)}) collective-permute-start(bf16[576,1152]{1,0:T(8,128)(2,1)} %copy.232), channel_id=1, source_target_pairs={{0,1},{1,0},{2,3},{3,2},{4,5},{5,4},{6,7},{7,6},{8,9},{9,8},{10,11... | collective-permute-start | bytes 3981320 | tf_op jit(solution)/shard_map/ppermute | solution.py:252
  294.3 53.8 %collective-permute-start.33 = (bf16[576,1152]{1,0:T(8,128)(2,1)}, bf16[576,1152]{1,0:T(8,128)(2,1)}, u32[]{:S(2)}, u32[]{:S(2)}) collective-permute-start(bf16[576,1152]{1,0:T(8,128)(2,1)} %copy.232), channel_id=1, source_target_pairs={{0,2},{1,3},{2,0},{3,1},{4,6},{5,7},{6,4},{7,5},{8,10},{9,11},{10,... | collective-permute-start | bytes 3981320 | tf_op jit(solution)/shard_map/ppermute | solution.py:252
  302.4 806.8 %reduce-scatter.15.cloned.1.call-start = ((), (), s32[]{:S(2)}) async-start(), calls=%async_computation.10 | async-start | bytes 1474560 | tf_op jit(solution)/shard_map/reduce_scatter | solution.py:271
  312.1 41.2 %collective-permute-start.35 = (bf16[576,1152]{1,0:T(8,128)(2,1)}, bf16[576,1152]{1,0:T(8,128)(2,1)}, u32[]{:S(2)}, u32[]{:S(2)}) collective-permute-start(bf16[576,1152]{1,0:T(8,128)(2,1)} %copy.232), channel_id=1, source_target_pairs={{0,4},{4,0},{8,12},{12,8},{16,20},{20,16},{24,28},{28,24},{1,5},{5... | collective-permute-start | bytes 3981320 | tf_op jit(solution)/shard_map/ppermute | solution.py:249
  314.4 54.6 %collective-permute-start.41 = (bf16[576,1152]{1,0:T(8,128)(2,1)}, bf16[576,1152]{1,0:T(8,128)(2,1)}, u32[]{:S(2)}, u32[]{:S(2)}) collective-permute-start(bf16[576,1152]{1,0:T(8,128)(2,1)} %collective-permute-done.40), channel_id=1, source_target_pairs={{0,1},{1,0},{2,3},{3,2},{4,5},{5,4},{6,7},{7,6},{8,9},{9,8},{10,11... | collective-permute-start | bytes 3981320 | tf_op jit(solution)/shard_map/ppermute | solution.py:252
  340.5 32.3 %collective-permute-start.42 = (bf16[576,1152]{1,0:T(8,128)(2,1)}, bf16[576,1152]{1,0:T(8,128)(2,1)}, u32[]{:S(2)}, u32[]{:S(2)}) collective-permute-start(bf16[576,1152]{1,0:T(8,128)(2,1)} %all-gather.12.cloned.1.call-done), channel_id=1, source_target_pairs={{0,4},{4,0},{8,12},{12,8},{16,20},{20,16},{24,28},{28,24},{1,5},{5... | collective-permute-start | bytes 3981320 | tf_op jit(solution)/shard_map/ppermute | solution.py:249
  353.3 193.3 %collective-permute-start.50 = (bf16[2,128,1152]{2,1,0:T(8,128)(2,1)}, bf16[2,128,1152]{2,1,0:T(8,128)(2,1)}, u32[]{:S(2)}, u32[]{:S(2)}) collective-permute-start(bf16[2,128,1152]{2,1,0:T(8,128)(2,1)} %get-tuple-element.245), channel_id=1, source_target_pairs={{0,2},{1,3},{2,0},{3,1},{4,6},{5,7},{6,4},{7,5},{8,10},{9,11},{10,... | collective-permute-start | bytes 1769480 | tf_op jit(solution)/shard_map/ppermute | solution.py:252
  376.9 35.8 %collective-permute-start.36 = (bf16[576,1152]{1,0:T(8,128)(2,1)}, bf16[576,1152]{1,0:T(8,128)(2,1)}, u32[]{:S(2)}, u32[]{:S(2)}) collective-permute-start(bf16[576,1152]{1,0:T(8,128)(2,1)} %collective-permute-done.32), channel_id=1, source_target_pairs={{0,4},{4,0},{8,12},{12,8},{16,20},{20,16},{24,28},{28,24},{1,5},{5... | collective-permute-start | bytes 3981320 | tf_op jit(solution)/shard_map/ppermute | solution.py:249
  379.7 38.2 %collective-permute-start.37 = (bf16[576,1152]{1,0:T(8,128)(2,1)}, bf16[576,1152]{1,0:T(8,128)(2,1)}, u32[]{:S(2)}, u32[]{:S(2)}) collective-permute-start(bf16[576,1152]{1,0:T(8,128)(2,1)} %collective-permute-done.33), channel_id=1, source_target_pairs={{0,4},{4,0},{8,12},{12,8},{16,20},{20,16},{24,28},{28,24},{1,5},{5... | collective-permute-start | bytes 3981320 | tf_op jit(solution)/shard_map/ppermute | solution.py:249
  417.9 128.7 %collective-permute-start.51 = (bf16[2,128,1152]{2,1,0:T(8,128)(2,1)}, bf16[2,128,1152]{2,1,0:T(8,128)(2,1)}, u32[]{:S(2)}, u32[]{:S(2)}) collective-permute-start(bf16[2,128,1152]{2,1,0:T(8,128)(2,1)} %get-tuple-element.244), channel_id=1, source_target_pairs={{0,3},{1,2},{2,1},{3,0},{4,7},{5,6},{6,5},{7,4},{8,11},{9,10},{10,... | collective-permute-start | bytes 1769480 | tf_op jit(solution)/shard_map/ppermute | solution.py:252
  657.5 160.0 %collective-permute-start.78 = (bf16[576,1152]{1,0:T(8,128)(2,1)}, bf16[576,1152]{1,0:T(8,128)(2,1)}, u32[]{:S(2)}, u32[]{:S(2)}) collective-permute-start(bf16[576,1152]{1,0:T(8,128)(2,1)} %get-tuple-element.212), channel_id=1, source_target_pairs={{0,4},{4,0},{8,12},{12,8},{16,20},{20,16},{24,28},{28,24},{1,5},{5... | collective-permute-start | bytes 3981320 | tf_op jit(solution)/shard_map/ppermute | solution.py:249
  815.9 34.5 %collective-permute-start.55 = (bf16[288,1152]{1,0:T(8,128)(2,1)S(1)}, bf16[288,1152]{1,0:T(8,128)(2,1)S(1)}, u32[]{:S(2)}, u32[]{:S(2)}) collective-permute-start(bf16[288,1152]{1,0:T(8,128)(2,1)S(1)} %get-tuple-element.222), channel_id=1, source_target_pairs={{0,4},{4,0},{8,12},{12,8},{16,20},{20,16},{24,28},{28,24},{1,5},{5... | collective-permute-start | bytes 1990664 | tf_op jit(solution)/shard_map/ppermute | solution.py:249
  817.4 33.1 %collective-permute-start.57 = (bf16[288,1152]{1,0:T(8,128)(2,1)S(1)}, bf16[288,1152]{1,0:T(8,128)(2,1)S(1)}, u32[]{:S(2)}, u32[]{:S(2)}) collective-permute-start(bf16[288,1152]{1,0:T(8,128)(2,1)S(1)} %get-tuple-element.226), channel_id=1, source_target_pairs={{0,1},{1,0},{2,3},{3,2},{4,5},{5,4},{6,7},{7,6},{8,9},{9,8},{10,11... | collective-permute-start | bytes 1990664 | tf_op jit(solution)/shard_map/ppermute | solution.py:252
  818.9 32.1 %collective-permute-start.61 = (bf16[288,1152]{1,0:T(8,128)(2,1)S(1)}, bf16[288,1152]{1,0:T(8,128)(2,1)S(1)}, u32[]{:S(2)}, u32[]{:S(2)}) collective-permute-start(bf16[288,1152]{1,0:T(8,128)(2,1)S(1)} %add_convert_fusion.19), channel_id=1, source_target_pairs={{0,2},{1,3},{2,0},{3,1},{4,6},{5,7},{6,4},{7,5},{8,10},{9,11},{10,... | collective-permute-start | bytes 1990664 | tf_op jit(solution)/shard_map/ppermute | solution.py:252
  832.1 52.9 %collective-permute-start.92 = (bf16[576,1152]{1,0:T(8,128)(2,1)}, bf16[576,1152]{1,0:T(8,128)(2,1)}, u32[]{:S(2)}, u32[]{:S(2)}) collective-permute-start(bf16[576,1152]{1,0:T(8,128)(2,1)} %get-tuple-element.206), channel_id=1, source_target_pairs={{0,4},{4,0},{8,12},{12,8},{16,20},{20,16},{24,28},{28,24},{1,5},{5... | collective-permute-start | bytes 3981320 | tf_op jit(solution)/shard_map/ppermute | solution.py:249
  847.4 38.8 %collective-permute-start.95 = (bf16[576,1152]{1,0:T(8,128)(2,1)}, bf16[576,1152]{1,0:T(8,128)(2,1)}, u32[]{:S(2)}, u32[]{:S(2)}) collective-permute-start(bf16[576,1152]{1,0:T(8,128)(2,1)} %get-tuple-element.204), channel_id=1, source_target_pairs={{0,4},{4,0},{8,12},{12,8},{16,20},{20,16},{24,28},{28,24},{1,5},{5... | collective-permute-start | bytes 3981320 | tf_op jit(solution)/shard_map/ppermute | solution.py:249
  850.4 70.0 %collective-permute-start.94 = (bf16[576,1152]{1,0:T(8,128)(2,1)}, bf16[576,1152]{1,0:T(8,128)(2,1)}, u32[]{:S(2)}, u32[]{:S(2)}) collective-permute-start(bf16[576,1152]{1,0:T(8,128)(2,1)} %get-tuple-element.205), channel_id=1, source_target_pairs={{0,4},{4,0},{8,12},{12,8},{16,20},{20,16},{24,28},{28,24},{1,5},{5... | collective-permute-start | bytes 3981320 | tf_op jit(solution)/shard_map/ppermute | solution.py:249
  854.2 272.1 %reduce-scatter.17.cloned.1.call-start = ((), (), s32[]{:S(2)}) async-start(), calls=%async_computation.11 | async-start | bytes 1843200 | tf_op jit(solution)/shard_map/reduce_scatter | solution.py:271
  855.8 36.9 %collective-permute-start.77 = (bf16[576,1152]{1,0:T(8,128)(2,1)}, bf16[576,1152]{1,0:T(8,128)(2,1)S(1)}, u32[]{:S(2)}, u32[]{:S(2)}) collective-permute-start(bf16[576,1152]{1,0:T(8,128)(2,1)} %get-tuple-element.209), channel_id=1, source_target_pairs={{0,4},{4,0},{8,12},{12,8},{16,20},{20,16},{24,28},{28,24},{1,5},{5... | collective-permute-start | bytes 3981320 | tf_op jit(solution)/shard_map/ppermute | solution.py:249
  890.8 52.3 %collective-permute-start.96 = (bf16[576,1152]{1,0:T(8,128)(2,1)}, bf16[576,1152]{1,0:T(8,128)(2,1)}, u32[]{:S(2)}, u32[]{:S(2)}) collective-permute-start(bf16[576,1152]{1,0:T(8,128)(2,1)} %get-tuple-element.208), channel_id=1, source_target_pairs={{0,1},{1,0},{2,3},{3,2},{4,5},{5,4},{6,7},{7,6},{8,9},{9,8},{10,11... | collective-permute-start | bytes 3981320 | tf_op jit(solution)/shard_map/ppermute | solution.py:252
  892.7 72.1 %collective-permute-start.91 = (bf16[576,1152]{1,0:T(8,128)(2,1)}, bf16[576,1152]{1,0:T(8,128)(2,1)}, u32[]{:S(2)}, u32[]{:S(2)}) collective-permute-start(bf16[576,1152]{1,0:T(8,128)(2,1)} %get-tuple-element.203), channel_id=1, source_target_pairs={{0,4},{4,0},{8,12},{12,8},{16,20},{20,16},{24,28},{28,24},{1,5},{5... | collective-permute-start | bytes 3981320 | tf_op jit(solution)/shard_map/ppermute | solution.py:249
  912.0 59.6 %collective-permute-start.93 = (bf16[576,1152]{1,0:T(8,128)(2,1)}, bf16[576,1152]{1,0:T(8,128)(2,1)}, u32[]{:S(2)}, u32[]{:S(2)}) collective-permute-start(bf16[576,1152]{1,0:T(8,128)(2,1)} %get-tuple-element.207), channel_id=1, source_target_pairs={{0,1},{1,0},{2,3},{3,2},{4,5},{5,4},{6,7},{7,6},{8,9},{9,8},{10,11... | collective-permute-start | bytes 3981320 | tf_op jit(solution)/shard_map/ppermute | solution.py:252
  920.3 214.7 %reduce-scatter.13.cloned.1.call-start = ((), (), s32[]{:S(2)}) async-start(), calls=%async_computation.8 | async-start | bytes 1658880 | tf_op jit(solution)/shard_map/reduce_scatter | solution.py:271
  946.8 37.2 %collective-permute-start.97 = (bf16[576,1152]{1,0:T(8,128)(2,1)}, bf16[576,1152]{1,0:T(8,128)(2,1)}, u32[]{:S(2)}, u32[]{:S(2)}) collective-permute-start(bf16[576,1152]{1,0:T(8,128)(2,1)} %add_convert_fusion.2), channel_id=1, source_target_pairs={{0,2},{1,3},{2,0},{3,1},{4,6},{5,7},{6,4},{7,5},{8,10},{9,11},{10,... | collective-permute-start | bytes 3981320 | tf_op jit(solution)/shard_map/ppermute | solution.py:252
  951.0 52.6 %collective-permute-start.48 = (bf16[2,128,1152]{2,1,0:T(8,128)(2,1)}, bf16[2,128,1152]{2,1,0:T(8,128)(2,1)S(1)}, u32[]{:S(2)}, u32[]{:S(2)}) collective-permute-start(bf16[2,128,1152]{2,1,0:T(8,128)(2,1)} %bitcast.789), channel_id=1, source_target_pairs={{0,3},{1,2},{2,1},{3,0},{4,7},{5,6},{6,5},{7,4},{8,11},{9,10},{10,... | collective-permute-start | bytes 1769480 | tf_op jit(solution)/shard_map/ppermute | solution.py:252
  952.2 109.9 %collective-permute-start.46 = (bf16[2,128,1152]{2,1,0:T(8,128)(2,1)}, bf16[2,128,1152]{2,1,0:T(8,128)(2,1)}, u32[]{:S(2)}, u32[]{:S(2)}) collective-permute-start(bf16[2,128,1152]{2,1,0:T(8,128)(2,1)} %bitcast.788), channel_id=1, source_target_pairs={{0,1},{1,0},{2,3},{3,2},{4,5},{5,4},{6,7},{7,6},{8,9},{9,8},{10,11... | collective-permute-start | bytes 1769480 | tf_op jit(solution)/shard_map/ppermute | solution.py:252
  964.8 97.3 %collective-permute-start.47 = (bf16[2,128,1152]{2,1,0:T(8,128)(2,1)S(1)}, bf16[2,128,1152]{2,1,0:T(8,128)(2,1)S(1)}, u32[]{:S(2)}, u32[]{:S(2)}) collective-permute-start(bf16[2,128,1152]{2,1,0:T(8,128)(2,1)S(1)} %bitcast.787), channel_id=1, source_target_pairs={{0,2},{1,3},{2,0},{3,1},{4,6},{5,7},{6,4},{7,5},{8,10},{9,11},{10,... | collective-permute-start | bytes 1769480 | tf_op jit(solution)/shard_map/ppermute | solution.py:252
  971.6 95.5 %collective-permute-start.52 = (bf16[2,128,1152]{2,1,0:T(8,128)(2,1)}, bf16[2,128,1152]{2,1,0:T(8,128)(2,1)}, u32[]{:S(2)}, u32[]{:S(2)}) collective-permute-start(bf16[2,128,1152]{2,1,0:T(8,128)(2,1)} %bitcast.126), channel_id=1, source_target_pairs={{0,1},{1,0},{2,3},{3,2},{4,5},{5,4},{6,7},{7,6},{8,9},{9,8},{10,11... | collective-permute-start | bytes 1769480 | tf_op jit(solution)/shard_map/ppermute | solution.py:252
  984.1 83.0 %collective-permute-start.53 = (bf16[2,128,1152]{2,1,0:T(8,128)(2,1)}, bf16[2,128,1152]{2,1,0:T(8,128)(2,1)}, u32[]{:S(2)}, u32[]{:S(2)}) collective-permute-start(bf16[2,128,1152]{2,1,0:T(8,128)(2,1)} %bitcast.128), channel_id=1, source_target_pairs={{0,2},{1,3},{2,0},{3,1},{4,6},{5,7},{6,4},{7,5},{8,10},{9,11},{10,... | collective-permute-start | bytes 1769480 | tf_op jit(solution)/shard_map/ppermute | solution.py:252
  991.0 155.7 %all-gather.14.cloned.1.call-start = ((), (), s32[]{:S(2)}) async-start(), calls=%async_computation.7 | async-start | bytes 3649536 | tf_op jit(solution)/shard_map/all_gather | solution.py:448
  1003.6 63.5 %collective-permute-start.54 = (bf16[2,128,1152]{2,1,0:T(8,128)(2,1)}, bf16[2,128,1152]{2,1,0:T(8,128)(2,1)}, u32[]{:S(2)}, u32[]{:S(2)}) collective-permute-start(bf16[2,128,1152]{2,1,0:T(8,128)(2,1)} %bitcast.130), channel_id=1, source_target_pairs={{0,3},{1,2},{2,1},{3,0},{4,7},{5,6},{6,5},{7,4},{8,11},{9,10},{10,... | collective-permute-start | bytes 1769480 | tf_op jit(solution)/shard_map/ppermute | solution.py:252
  (185 other events, 4097.9 us)
Sparse Core Ops, SparseCore 0:
  9.6 34.3 all-gather.11
  45.6 35.4 all-gather.9
  82.9 35.1 all-gather.15
  302.5 31.8 reduce-scatter.10
  854.4 27.2 reduce-scatter.14
  920.4 35.2 reduce-scatter.16
  991.2 39.6 reduce-scatter.12
  1034.2 61.3 all-gather.13

commit v2 on v1

v2 whole, which is shorter than its diff:
```python
import functools

import jax
import jax.numpy as jnp
from jax import lax
from jax.experimental import pallas as pl
from jax.experimental.pallas import tpu as pltpu
from jax.sharding import Mesh
from jax.sharding import PartitionSpec as P

HEADS = 16
EPS = 1e-06
GELU_C = 0.7978845608028654
GELU_A = 0.044715
BF = jnp.bfloat16
F32 = jnp.float32
VMEM = 58 * 1024 * 1024
ANY = pl.BlockSpec(memory_space=pl.ANY)
EVERY = ("z", "core", "seq")
DENSE = ("core", "seq")


def normalize(values):
    center = values - jnp.mean(values, -1, keepdims=True)
    scale_inv = lax.rsqrt(jnp.mean(center * center, -1, keepdims=True) + EPS)
    return (center * scale_inv, scale_inv)


def norm_back(grad_norm, normed, scale_inv):
    return scale_inv * (
        grad_norm
        - jnp.mean(grad_norm, -1, keepdims=True)
        - normed * jnp.mean(grad_norm * normed, -1, keepdims=True)
    )


def dot_nn(a, b):
    return lax.dot_general(a, b, (((1,), (0,)), ((), ())), preferred_element_type=F32)


def dot_nt(a, b):
    return lax.dot_general(a, b, (((1,), (1,)), ((), ())), preferred_element_type=F32)


def dot_tn(a, b):
    return lax.dot_general(a, b, (((0,), (0,)), ((), ())), preferred_element_type=F32)


def params():
    return pltpu.CompilerParams(vmem_limit_bytes=VMEM)


def cost(micros):
    return pl.CostEstimate(flops=int(micros * 1.15e9), bytes_accessed=0, transcendentals=0)


def shape(dims, kind):
    return jax.ShapeDtypeStruct(tuple(dims), kind)


def pack_kernel(n_z, blocks, qkv_ref, mod_ref, up_ref, mb_ref, qb_ref, vb_ref, ob_ref, ub_ref, db_ref, out_ref):
    shard, model3 = qkv_ref.shape
    model = model3 // 3
    width = model // blocks
    devices = n_z * blocks
    ff_shard = up_ref.shape[1] // devices
    mod_shard = mod_ref.shape[1] // devices
    lanes = out_ref.shape[2]
    qkv = qkv_ref[...].astype(F32)
    mod = mod_ref[...].astype(F32)
    up = up_ref[...].astype(F32)
    tail = [r[...].astype(F32) for r in (mb_ref, ub_ref, qb_ref, vb_ref, ob_ref, db_ref)]
    tail.append(jnp.zeros((1, lanes - sum(r.shape[1] for r in tail)), F32))
    tail = [jnp.concatenate(tail, 1)]
    spare = out_ref.shape[1] - shard - 1
    if spare:
        tail.append(jnp.zeros((spare, lanes), F32))
    for e in range(blocks):
        pieces = []
        for z in range(n_z):
            d = z * blocks + e
            pieces.append(mod[:, d * mod_shard : (d + 1) * mod_shard])
            pieces.append(up[:, d * ff_shard : (d + 1) * ff_shard])
        for i in range(3):
            pieces.append(qkv[:, i * model + e * width : i * model + (e + 1) * width])
        out_ref[e] = jnp.concatenate([jnp.concatenate(pieces, 1)] + tail, 0).astype(BF)


def pack(n_z, blocks, qkv, mod, up, biases):
    shard = qkv.shape[0]
    lanes = (qkv.shape[1] + mod.shape[1] + up.shape[1]) // blocks
    rows = -(-(shard + 1) // 8) * 8
    return pl.pallas_call(
        functools.partial(pack_kernel, n_z, blocks),
        out_shape=shape((blocks, rows, lanes), BF),
        compiler_params=params(),
        cost_estimate=cost(3),
    )(qkv, mod, up, *[b.reshape(1, -1) for b in biases])


def unpack_kernel(n_z, shard, bias_lanes, got_ref, qkv_out, z_out):
    blocks = got_ref.shape[0]
    lanes = z_out.shape[2]
    got = [got_ref[e].astype(F32) for e in range(blocks)]
    whole = jnp.concatenate([g[:shard] for g in got], 0)
    qkv_out[...] = whole[:, n_z * lanes :].astype(BF)
    rows = [g[shard : shard + 1, :lanes] for g in got]
    rest = bias_lanes - lanes
    rows += [jnp.concatenate([g[shard : shard + 1, lanes:bias_lanes], jnp.zeros((1, lanes - rest), F32)], 1) for g in got]
    for z in range(n_z):
        z_out[z] = jnp.concatenate([whole[:, z * lanes : (z + 1) * lanes]] + rows, 0).astype(BF)


def unpack(got, n_z, shard, lanes, bias_lanes):
    blocks = got.shape[0]
    rows = blocks * shard
    return pl.pallas_call(
        functools.partial(unpack_kernel, n_z, shard, bias_lanes),
        out_shape=[
            shape((rows, got.shape[2] - n_z * lanes), BF), shape((n_z, rows + 2 * blocks, lanes), BF),
        ],
        compiler_params=params(),
        cost_estimate=cost(3),
    )(got)


def turn_kernel(n_z, rows, cuts, at_ref, *refs):
    got = refs[:n_z]
    outs, held = refs[n_z:-1], refs[-1]
    for k in range(n_z):
        held[at_ref[0] ^ k] = got[k][...]
    whole = jnp.concatenate([held[z, :rows].astype(F32).T for z in range(n_z)], 1)
    for i, out in enumerate(outs[: len(cuts) - 1]):
        out[...] = whole[cuts[i] : cuts[i + 1]].astype(BF)
    if len(outs) == len(cuts):
        outs[-1][...] = held[:, rows:]


def turn(z_at, got, rows, cuts):
    n_z = len(got)
    outs = [shape((cuts[i + 1] - cuts[i], rows * n_z), BF) for i in range(len(cuts) - 1)]
    if got[0].shape[0] > rows:
        outs.append(shape((n_z, got[0].shape[0] - rows, got[0].shape[1]), BF))
    return pl.pallas_call(
        functools.partial(turn_kernel, n_z, rows, cuts),
        in_specs=[pl.BlockSpec(memory_space=pltpu.SMEM)] + [pl.BlockSpec(memory_space=pltpu.VMEM)] * n_z,
        out_shape=outs,
        scratch_shapes=[pltpu.VMEM((n_z,) + got[0].shape, BF)],
        compiler_params=params(),
        cost_estimate=cost(3),
    )(z_at, *got)


def join_kernel(n_z, at_ref, *refs):
    got, (out, held) = refs[:n_z], refs[n_z:]
    for k in range(n_z):
        held[at_ref[0] ^ k] = got[k][...]
    out[...] = jnp.concatenate([held[z].astype(F32) for z in range(n_z)], 0).astype(BF)


def join(z_at, got):
    n_z = len(got)
    rows, model = got[0].shape
    return pl.pallas_call(
        functools.partial(join_kernel, n_z),
        in_specs=[pl.BlockSpec(memory_space=pltpu.SMEM)] + [pl.BlockSpec(memory_space=pltpu.VMEM)] * n_z,
        out_shape=shape((n_z * rows, model), BF),
        scratch_shapes=[pltpu.VMEM((n_z, rows, model), BF)],
        compiler_params=params(),
        cost_estimate=cost(3),
    )(z_at, *got)


def split_kernel(n_z, width, n_in, *refs):
    total = refs[0][...].astype(F32)
    for ref in refs[1:n_in]:
        total = total + ref[...].astype(F32)
    qkv_out, out_out = refs[n_in:]
    model = total.shape[1]
    part = width // n_z
    turned = total[: 3 * width].T
    rows = model // n_z
    bias = total[4 * width : 4 * width + 1]
    for z in range(n_z):
        qkv_out[z] = turned[z * rows : (z + 1) * rows].astype(BF)
        pieces = [total[3 * width + z * part : 3 * width + (z + 1) * part]]
        for i in range(4):
            at = i * width + z * part
            pieces.append(jnp.concatenate([bias[:, at : at + part], jnp.zeros((1, model - part), F32)], 1))
        spare = out_out.shape[1] - part - 4
        if spare:
            pieces.append(jnp.zeros((spare, model), F32))
        out_out[z] = jnp.concatenate(pieces, 0).astype(BF)


def split_parts(values, n_z):
    rows, model = values[0].shape
    width = (rows - 16) // 4
    out_rows = -(-(width // n_z + 4) // 8) * 8
    return pl.pallas_call(
        functools.partial(split_kernel, n_z, width, len(values)),
        out_shape=[shape((n_z, model // n_z, 3 * width), BF), shape((n_z, out_rows, model), BF)],
        compiler_params=params(),
        cost_estimate=cost(3),
    )(*values)


def deal_kernel(n_in, blocks, *refs):
    sums = []
    for i in range(2):
        total = refs[i * n_in][...].astype(F32)
        for ref in refs[i * n_in + 1 : (i + 1) * n_in]:
            total = total + ref[...].astype(F32)
        sums.append(total)
    total = jnp.concatenate(sums, 1)
    rows = total.shape[0] // blocks
    for e in range(blocks):
        refs[2 * n_in][e] = total[e * rows : (e + 1) * rows].astype(BF)


def deal(first, second, blocks):
    rows = first[0].shape[0]
    lanes = first[0].shape[1] + second[0].shape[1]
    return pl.pallas_call(
        functools.partial(deal_kernel, len(first), blocks),
        out_shape=shape((blocks, rows // blocks, lanes), BF),
        compiler_params=params(),
        cost_estimate=cost(3),
    )(*first, *second)


def turn_up_kernel(n_z, at_ref, *refs):
    got, (out, held) = refs[:n_z], refs[n_z:]
    for t in range(n_z):
        total = got[t][0].astype(F32)
        for s in range(1, got[t].shape[0]):
            total = total + got[t][s].astype(F32)
        held[lax.rem(at_ref[0] - t + n_z, n_z)] = total
    turned = jnp.concatenate([held[z].T for z in range(n_z)], 1)
    rows = out.shape[1]
    for z in range(n_z):
        out[z] = turned[z * rows : (z + 1) * rows].astype(BF)


def turn_up(z_at, got):
    n_z = len(got)
    _, ff, model = got[0].shape
    return pl.pallas_call(
        functools.partial(turn_up_kernel, n_z),
        in_specs=[pl.BlockSpec(memory_space=pltpu.SMEM)] + [pl.BlockSpec(memory_space=pltpu.VMEM)] * n_z,
        out_shape=shape((n_z, model // n_z, n_z * ff), BF),
        scratch_shapes=[pltpu.VMEM((n_z, ff, model), F32)],
        compiler_params=params(),
        cost_estimate=cost(3),
    )(z_at, *got)


def columns_kernel(groups, n_in, *refs):
    for out, (source, rows, start, size, count) in zip(refs[n_in:], groups):
        ref = refs[source]
        pieces = []
        for i in range(count):
            for n in range(ref.shape[0]):
                pieces.append(ref[n].astype(F32)[:rows, start + i * size : start + (i + 1) * size])
        out[...] = jnp.concatenate(pieces, 1)


def columns(sources, groups):
    return pl.pallas_call(
        functools.partial(columns_kernel, groups, len(sources)),
        out_shape=[shape((rows, sources[i].shape[0] * size * count), F32) for i, rows, _, size, count in groups],
        compiler_params=params(),
        cost_estimate=cost(3),
    )(*sources)


def mod_columns_kernel(early_ref, late_ref, out):
    shard = out.shape[0]
    pieces = []
    for ref in (early_ref, late_ref):
        for i in range(ref.shape[2] // shard):
            for n in range(ref.shape[0]):
                pieces.append(ref[n].astype(F32)[:shard, i * shard : (i + 1) * shard])
    out[...] = jnp.concatenate(pieces, 1)


def mod_columns(early, late, shard):
    return pl.pallas_call(
        mod_columns_kernel,
        out_shape=[shape((shard, 6 * shard * early.shape[0]), F32)],
        compiler_params=params(),
        cost_estimate=cost(3),
    )(early, late)


def place_kernel(at_ref, *refs):
    out = refs[-1]
    for k, ref in enumerate(refs[:-1]):
        out[at_ref[0] ^ k] = ref[...]


def place(at, got):
    return pl.pallas_call(
        place_kernel,
        in_specs=[pl.BlockSpec(memory_space=pltpu.SMEM)] + [pl.BlockSpec(memory_space=pltpu.VMEM)] * len(got),
        out_shape=shape((len(got),) + got[0].shape, got[0].dtype),
        compiler_params=params(),
        cost_estimate=cost(3),
    )(at, *got)


def attn_fwd_kernel(head_size, h_ref, w_a, w_b, qb_ref, vb_ref, segc_ref, segr_ref, *rest):
    q_out, k_out, v_out, att_out, lse_out = rest[-5:]
    width = qb_ref.shape[-1]
    length = segr_ref.shape[-1]
    model = h_ref.shape[-1]
    h = h_ref[...].reshape(length, model)
    allowed = segc_ref[0] == segr_ref[0]
    scale = head_size ** (-0.5)
    part = q_out.shape[1:]
    for n, w_ref in enumerate((w_a, w_b)):
        qkv = dot_nt(h, w_ref[...])
        q = (qkv[:, :width] + qb_ref[n]).astype(BF)
        k = qkv[:, width : 2 * width].astype(BF)
        v = (qkv[:, 2 * width :] + vb_ref[n]).astype(BF)
        q_out[n] = q.reshape(part)
        k_out[n] = k.reshape(part)
        v_out[n] = v.reshape(part)
        pieces = []
        for i in range(width // head_size):
            cut = slice(i * head_size, (i + 1) * head_size)
            score = jnp.where(allowed, dot_nt(k[:, cut], q[:, cut]) * scale, -1e30)
            top = jnp.max(score, 0, keepdims=True)
            prob = jnp.exp(score - top)
            total = jnp.sum(prob, 0, keepdims=True)
            out_t = dot_tn(v[:, cut], prob.astype(BF)) * (1.0 / total)
            pieces.append(out_t.T)
            lse_out[n, 0, i : i + 1, :] = top + jnp.log(total)
        att_out[n] = jnp.concatenate(pieces, -1).astype(BF).reshape(part)


def attn_fwd(hidden, w_a, w_b, query_bias, value_bias, seg_col, seg_row, head_size, wait):
    n_seq, rows, kept_count, model = hidden.shape
    width = query_bias.shape[-1]
    length = n_seq * kept_count
    heads = width // head_size
    token = pl.BlockSpec((n_seq, 1, kept_count, model), lambda r: (0, r, 0, 0))
    part = pl.BlockSpec((2, n_seq, 1, kept_count, width), lambda r: (0, 0, r, 0, 0))
    weight = pl.BlockSpec(w_a.shape, lambda r: (0, 0))
    bias = pl.BlockSpec((2, 1, width), lambda r: (0, 0, 0))
    part_shape = shape((2, n_seq, rows, kept_count, width), BF)
    return pl.pallas_call(
        functools.partial(attn_fwd_kernel, head_size),
        grid=(rows,),
        in_specs=[
            token, weight, weight, bias, bias,
            pl.BlockSpec((1, length, 1), lambda r: (r, 0, 0)),
            pl.BlockSpec((1, 1, length), lambda r: (r, 0, 0)),
        ]
        + [ANY] * len(wait),
        out_specs=[part, part, part, part, pl.BlockSpec((2, 1, heads, length), lambda r: (0, r, 0, 0))],
        out_shape=[part_shape] * 4 + [shape((2, rows, heads, length), F32)],
        compiler_params=params(),
        cost_estimate=cost(12),
    )(hidden, w_a, w_b, query_bias, value_bias, seg_col, seg_row, *wait)


def attn_bwd_kernel(head_size, first, n_wait, h_ref, gb_ref, w_a, w_b, o_a, o_b, q_ref, k_ref, v_ref, att_ref, lse_ref,
                    bias_ref, segc_ref, segr_ref, *rest):
    g_a, g_b, gh_out, sum_qkv, sum_out, sum_bias = rest[-6:]
    gh_in = None if first else rest[n_wait]
    width = q_ref.shape[-1]
    length = segr_ref.shape[-1]
    model = h_ref.shape[-1]
    row = pl.program_id(0)
    h = h_ref[...].reshape(length, model)
    gb = gb_ref[...].reshape(length, model)
    allowed = segc_ref[0] == segr_ref[0]
    scale = head_size ** (-0.5)
    total = None
    for n, (w_ref, o_ref) in enumerate(((w_a, o_a), (w_b, o_b))):
        grad_att = dot_nt(gb, o_ref[...]).astype(BF)
        q = q_ref[n].reshape(length, width)
        k = k_ref[n].reshape(length, width)
        v = v_ref[n].reshape(length, width)
        att = att_ref[n].reshape(length, width)
        gq, gk, gv = [], [], []
        for i in range(width // head_size):
            cut = slice(i * head_size, (i + 1) * head_size)
            score = dot_nt(k[:, cut], q[:, cut]) * scale - lse_ref[n, 0, i : i + 1, :]
            prob = jnp.exp(jnp.where(allowed, score, -1e30))
            grad_prob = dot_nt(v[:, cut], grad_att[:, cut])
            inner = jnp.sum(prob * grad_prob, 0, keepdims=True)
            grad_score = (prob * (grad_prob - inner)).astype(BF)
            gq.append((dot_tn(k[:, cut], grad_score) * scale).T)
            gk.append(dot_nn(grad_score, q[:, cut]) * scale)
            gv.append(dot_nn(prob.astype(BF), grad_att[:, cut]))
        grad_qkv = jnp.concatenate(gq + gk + gv, -1).astype(BF)
        term = dot_nn(grad_qkv, w_ref[...])
        total = term if total is None else total + term
        term_qkv = dot_tn(grad_qkv, h)
        term_out = dot_tn(att, gb)
        term_bias = jnp.sum(grad_qkv.astype(F32), 0, keepdims=True)

        @pl.when(row == 0)
        def _():
            sum_qkv[n] = term_qkv
            sum_out[n] = term_out
            sum_bias[n] = term_bias

        @pl.when(row != 0)
        def _():
            sum_qkv[n] += term_qkv
            sum_out[n] += term_out
            sum_bias[n] += term_bias

    if first:
        gh_out[...] = total.reshape(gh_out.shape)
    else:
        gh_out[...] = gh_in[...] + total.reshape(gh_out.shape)

    @pl.when(row == pl.num_programs(0) - 1)
    def _():
        for n, g_ref in enumerate((g_a, g_b)):
            g_ref[: 3 * width] = sum_qkv[n].astype(BF)
            g_ref[3 * width : 4 * width] = sum_out[n].astype(BF)
            biases = jnp.concatenate(
                [sum_bias[n, :, :width], sum_bias[n, :, 2 * width :], bias_ref[n],
                 jnp.zeros((1, model - 4 * width), F32)], -1
            )
            g_ref[4 * width :] = jnp.broadcast_to(biases, (16, model)).astype(BF)


def attn_bwd(hidden, grad_branch, w_a, w_b, o_a, o_b, saved, bias, seg_col, seg_row, head_size, grad_hidden, wait):
    q, k, v, att, lse = saved
    n_seq, rows, kept_count, model = hidden.shape
    width = q.shape[-1]
    length = n_seq * kept_count
    heads = width // head_size
    first = grad_hidden is None
    token = pl.BlockSpec((n_seq, 1, kept_count, model), lambda r: (0, r, 0, 0))
    part = pl.BlockSpec((2, n_seq, 1, kept_count, width), lambda r: (0, 0, r, 0, 0))
    weight = pl.BlockSpec(w_a.shape, lambda r: (0, 0))
    out_weight = pl.BlockSpec(o_a.shape, lambda r: (0, 0))
    out = pl.BlockSpec((4 * width + 16, model), lambda r: (0, 0))
    own = [] if first else [grad_hidden]
    return pl.pallas_call(
        functools.partial(attn_bwd_kernel, head_size, first, len(wait)),
        grid=(rows,),
        in_specs=[
            token, token, weight, weight, out_weight, out_weight, part, part, part, part,
            pl.BlockSpec((2, 1, heads, length), lambda r: (0, r, 0, 0)),
            pl.BlockSpec((2, 1, 2 * width), lambda r: (0, 0, 0)),
            pl.BlockSpec((1, length, 1), lambda r: (r, 0, 0)),
            pl.BlockSpec((1, 1, length), lambda r: (r, 0, 0)),
        ]
        + [ANY] * len(wait)
        + [token] * len(own),
        out_specs=[out, out, token],
        out_shape=[shape((4 * width + 16, model), BF)] * 2 + [shape(hidden.shape, F32)],
        scratch_shapes=[
            pltpu.VMEM((2, 3 * width, model), F32),
            pltpu.VMEM((2, width, model), F32),
            pltpu.VMEM((2, 1, 3 * width), F32),
        ],
        input_output_aliases={} if first else {14 + len(wait): 2},
        compiler_params=params(),
        cost_estimate=cost(24),
    )(hidden, grad_branch, w_a, w_b, o_a, o_b, q, k, v, att, lse, bias, seg_col, seg_row, *wait, *own)


def pick_slot(table_ref, seg, index):
    value = table_ref[0, 0, index : index + 1, :]
    for slot in range(1, table_ref.shape[1]):
        value = jnp.where(seg == slot, table_ref[0, slot, index : index + 1, :], value)
    return value


def add_slots(out_ref, index, seg, value, start):
    for slot in range(out_ref.shape[1]):
        part = jnp.sum(jnp.where(seg == slot, value, 0.0), 0, keepdims=True)
        at = (0, slot, slice(index, index + 1))
        out_ref[at] = jnp.where(start, 0.0, out_ref[at]) + part


def after_attn_kernel(n_blocks, width, x_ref, seg_ref, table_ref, ob_ref, *rest):
    att_refs = rest[: n_blocks // 2]
    w_refs = rest[n_blocks // 2 : n_blocks // 2 + n_blocks]
    br_out, mid_out, h2_out = rest[-3:]
    kept_count, model = x_ref.shape[2:]
    seg = seg_ref[0, 0]
    branch = ob_ref[...]
    for j in range(n_blocks // 2):
        for n in range(2):
            w = w_refs[j + n * (n_blocks // 2)][...]
            branch = branch + dot_nn(att_refs[j][n].reshape(kept_count, width), w)
    mid = x_ref[0, 0].astype(F32) + pick_slot(table_ref, seg, 2) * branch
    normed, _ = normalize(mid)
    br_out[0, 0] = branch
    mid_out[0, 0] = mid
    h2_out[0, 0] = (normed * (1.0 + pick_slot(table_ref, seg, 4)) + pick_slot(table_ref, seg, 3)).astype(BF)


def after_attn(inputs, seg, table, out_bias, atts, weights, wait):
    n_seq, rows, kept_count, model = inputs.shape
    width = atts[0].shape[-1]
    slots = table.shape[1]
    token = pl.BlockSpec((1, 1, kept_count, model), lambda r, j: (j, r, 0, 0))
    part = pl.BlockSpec((2, 1, 1, kept_count, width), lambda r, j: (0, j, r, 0, 0))
    weight = pl.BlockSpec((width, model), lambda r, j: (0, 0))
    return pl.pallas_call(
        functools.partial(after_attn_kernel, len(weights), width),
        grid=(rows, n_seq),
        in_specs=[
            token,
            pl.BlockSpec((1, 1, kept_count, 1), lambda r, j: (j, r, 0, 0)),
            pl.BlockSpec((1, slots, 6, model), lambda r, j: (r, 0, 0, 0)),
            pl.BlockSpec((1, model), lambda r, j: (0, 0)),
        ]
        + [part] * len(atts)
        + [weight] * len(weights)
        + [ANY] * len(wait),
        out_specs=[token] * 3,
        out_shape=[shape(inputs.shape, F32), shape(inputs.shape, F32), shape(inputs.shape, BF)],
        compiler_params=params(),
        cost_estimate=cost(15),
    )(inputs, seg, table, out_bias, *atts, *weights, *wait)


def after_mlp_kernel(mid_ref, mlp_ref, gh_ref, br_ref, ct_ref, seg_ref, table_ref, db_ref, *rest):
    res_out, gm_out, gb_out, sums_out, obias_out = rest[-5:]
    seg = seg_ref[0, 0]
    step = pl.program_id(1)
    mid = mid_ref[0, 0]
    branch_mlp = mlp_ref[0, 0] + db_ref[...]
    grad_hidden = gh_ref[0, 0]
    grad_result = ct_ref[0, 0].astype(F32)
    res_out[0, 0] = (mid + pick_slot(table_ref, seg, 5) * branch_mlp).astype(BF)
    normed, inv = normalize(mid)
    grad_mid = grad_result + norm_back(grad_hidden * (1.0 + pick_slot(table_ref, seg, 4)), normed, inv)
    gm_out[0, 0] = grad_mid
    grad_branch = (grad_mid * pick_slot(table_ref, seg, 2)).astype(BF)
    gb_out[0, 0] = grad_branch
    add_slots(sums_out, 0, seg, grad_mid * br_ref[0, 0], step == 0)
    add_slots(sums_out, 1, seg, grad_hidden, step == 0)
    add_slots(sums_out, 2, seg, grad_hidden * normed, step == 0)
    add_slots(sums_out, 3, seg, grad_result * branch_mlp, step == 0)
    start = jnp.logical_and(step == 0, pl.program_id(0) == 0)
    part = jnp.sum(grad_branch.astype(F32), 0, keepdims=True)
    obias_out[...] = jnp.where(start, 0.0, obias_out[...]) + part


def after_mlp(mid, mlp, grad_hidden, branch, cotangent, seg, table, down_bias, wait):
    n_seq, rows, kept_count, model = mid.shape
    slots = table.shape[1]
    token = pl.BlockSpec((1, 1, kept_count, model), lambda r, j: (j, r, 0, 0))
    vector = pl.BlockSpec((1, model), lambda r, j: (0, 0))
    return pl.pallas_call(
        after_mlp_kernel,
        grid=(rows, n_seq),
        in_specs=[
            token, token, token, token, token,
            pl.BlockSpec((1, 1, kept_count, 1), lambda r, j: (j, r, 0, 0)),
            pl.BlockSpec((1, slots, 6, model), lambda r, j: (r, 0, 0, 0)),
            vector,
        ]
        + [ANY] * len(wait),
        out_specs=[
            token, token, token,
            pl.BlockSpec((1, slots, 4, model), lambda r, j: (r, 0, 0, 0)),
            vector,
        ],
        out_shape=[
            shape(mid.shape, BF), shape(mid.shape, F32), shape(mid.shape, BF),
            shape((rows, slots, 4, model), F32), shape((1, model), F32),
        ],
        compiler_params=params(),
        cost_estimate=cost(21),
    )(mid, mlp, grad_hidden, branch, cotangent, seg, table, down_bias, *wait)


def last_kernel(x_ref, gh_ref, gm_ref, seg_ref, table_ref, *rest):
    gx_out, sums_out = rest[-2:]
    seg = seg_ref[0, 0]
    step = pl.program_id(1)
    grad_hidden = gh_ref[0, 0]
    normed, inv = normalize(x_ref[0, 0].astype(F32))
    back = norm_back(grad_hidden * (1.0 + pick_slot(table_ref, seg, 1)), normed, inv)
    gx_out[0, 0] = (gm_ref[0, 0] + back).astype(BF)
    add_slots(sums_out, 0, seg, grad_hidden, step == 0)
    add_slots(sums_out, 1, seg, grad_hidden * normed, step == 0)


def last_step(inputs, grad_hidden, grad_mid, seg, table, wait):
    n_seq, rows, kept_count, model = inputs.shape
    slots = table.shape[1]
    token = pl.BlockSpec((1, 1, kept_count, model), lambda r, j: (j, r, 0, 0))
    return pl.pallas_call(
        last_kernel,
        grid=(rows, n_seq),
        in_specs=[
            token, token, token,
            pl.BlockSpec((1, 1, kept_count, 1), lambda r, j: (j, r, 0, 0)),
            pl.BlockSpec((1, slots, 6, model), lambda r, j: (r, 0, 0, 0)),
        ]
        + [ANY] * len(wait),
        out_specs=[token, pl.BlockSpec((1, slots, 2, model), lambda r, j: (r, 0, 0, 0))],
        out_shape=[shape(inputs.shape, BF), shape((rows, slots, 2, model), F32)],
        compiler_params=params(),
        cost_estimate=cost(12),
    )(inputs, grad_hidden, grad_mid, seg, table, *wait)


def mlp_kernel(n_up, n_down, first, n_wait, h_ref, gm_ref, ub_ref, *rest):
    up_refs = rest[:n_up]
    down_refs = rest[n_up : n_up + n_down]
    if first:
        mlp_in = gh_in = None
    else:
        mlp_in, gh_in = rest[n_up + n_down + n_wait : n_up + n_down + n_wait + 2]
    mlp_out, gh_out, own_out, other_out, gub_out, up, down, sum_up, sum_down, sum_bias = rest[-10:]
    step = pl.program_id(0)
    model = h_ref.shape[-1]

    @pl.when(step == 0)
    def _():
        for refs, whole in ((up_refs, up), (down_refs, down)):
            at = 0
            for ref in refs:
                block = ref[...].reshape(-1, model)
                whole[at : at + block.shape[0]] = block
                at += block.shape[0]

    h = h_ref[...]
    gm = gm_ref[...]
    pre = dot_nt(h, up[...]) + ub_ref[0]
    square = pre * pre
    tanh_part = jnp.tanh(GELU_C * pre * (1.0 + GELU_A * square))
    half = 0.5 * (1.0 + tanh_part)
    activated = (pre * half).astype(BF)
    slope = half + 0.5 * pre * (1.0 - tanh_part * tanh_part) * GELU_C * (1.0 + 3.0 * GELU_A * square)
    grad_pre = (dot_nt(gm, down[...]) * slope).astype(BF)
    mlp_term = dot_nn(activated, down[...])
    gh_term = dot_nn(grad_pre, up[...])
    mlp_out[...] = mlp_term if first else mlp_in[...] + mlp_term
    gh_out[...] = gh_term if first else gh_in[...] + gh_term
    up_term = dot_tn(grad_pre, h)
    down_term = dot_tn(activated, gm)
    bias_term = jnp.sum(grad_pre.astype(F32), 0, keepdims=True)

    @pl.when(step == 0)
    def _():
        sum_up[...] = up_term
        sum_down[...] = down_term
        sum_bias[...] = bias_term

    @pl.when(step != 0)
    def _():
        sum_up[...] += up_term
        sum_down[...] += down_term
        sum_bias[...] += bias_term

    @pl.when(step == pl.num_programs(0) - 1)
    def _():
        half_rows = sum_up.shape[0] // 2
        own_out[0] = sum_up[:half_rows].astype(BF)
        own_out[1] = sum_down[:half_rows].astype(BF)
        other_out[0] = sum_up[half_rows:].astype(BF)
        other_out[1] = sum_down[half_rows:].astype(BF)
        gub_out[...] = sum_bias[...]


def mlp_step(hidden, grad_mlp, up_bias, ups, downs, sums, wait):
    count, model = hidden.shape
    chunk = min(512, count)
    width = sum(u.shape[0] * u.shape[1] for u in ups)
    first = sums is None
    own = [] if first else list(sums)
    token = pl.BlockSpec((chunk, model), lambda i: (i, 0))
    weights = [pl.BlockSpec(u.shape, lambda i: (0, 0, 0)) for u in ups + downs]
    grads = pl.BlockSpec((2, width // 2, model), lambda i: (0, 0, 0))
    inputs = 3 + len(ups) + len(downs) + len(wait)
    return pl.pallas_call(
        functools.partial(mlp_kernel, len(ups), len(downs), first, len(wait)),
        grid=(count // chunk,),
        in_specs=[token, token, pl.BlockSpec((1, 1, width), lambda i: (0, 0, 0))]
        + weights
        + [ANY] * len(wait)
        + [token] * len(own),
        out_specs=[token, token, grads, grads, pl.BlockSpec((1, width), lambda i: (0, 0))],
        out_shape=[
            shape((count, model), F32), shape((count, model), F32),
            shape((2, width // 2, model), BF), shape((2, width // 2, model), BF), shape((1, width), F32),
        ],
        scratch_shapes=[
            pltpu.VMEM((width, model), BF), pltpu.VMEM((width, model), BF),
            pltpu.VMEM((width, model), F32), pltpu.VMEM((width, model), F32), pltpu.VMEM((1, width), F32),
        ],
        input_output_aliases={} if first else {inputs: 0, inputs + 1: 1},
        compiler_params=params(),
        cost_estimate=cost(32),
    )(hidden, grad_mlp, up_bias, *ups, *downs, *wait, *own)


def tie(value, *after):
    return lax.optimization_barrier((value,) + after)[0]


def body(
    n_z, n_seq,
    tokens, conditioning, segments, kept, cotangent,
    mod_weight, mod_bias, qkv_weight, query_bias, value_bias, out_weight, out_bias,
    up_weight, up_bias, down_weight, down_bias,
):
    row_count, seq_tokens, model = tokens.shape
    kept_count = kept.shape[1]
    slots = conditioning.shape[1]
    head_size = model // HEADS
    rows = row_count // n_seq
    shard = qkv_weight.shape[0]
    blocks = 2 * n_seq
    devices = n_z * blocks
    width = model // blocks
    part = width // n_z
    flat = n_seq * rows * kept_count
    ff_shard = down_weight.shape[0]
    z_at = lax.axis_index("z")
    core_at = lax.axis_index("core")
    seq_at = lax.axis_index("seq")
    block_at = core_at * n_seq + seq_at
    relative = block_at ^ jnp.arange(blocks)
    z_relative = z_at ^ jnp.arange(n_z)
    seq_relative = seq_at ^ jnp.arange(n_seq)
    core_relative = core_at ^ jnp.arange(2)
    z_ring = (z_at - jnp.arange(n_z)) % n_z
    seq_scalar = seq_at.reshape(1).astype(jnp.int32)
    z_scalar = z_at.reshape(1).astype(jnp.int32)
    mod_shard = 6 * shard

    def over_core(value):
        return lax.ppermute(value, "core", [(0, 1), (1, 0)])

    def over_seq(value, by):
        return lax.ppermute(value, "seq", [(i, i ^ by) for i in range(n_seq)])

    def over_z(value, by):
        return lax.ppermute(value, "z", [(i, i ^ by) for i in range(n_z)])

    def shift_z(value, by):
        return lax.ppermute(value, "z", [(i, (i + by) % n_z) for i in range(n_z)])

    def all_to_all(value):
        return lax.all_to_all(value, EVERY, 0, 0, tiled=True)

    def dense_to_all(value):
        return lax.all_to_all(value, DENSE, 0, 0, tiled=True)

    def to_z(value):
        mine = [lax.dynamic_index_in_dim(value, z_at ^ k, 0, keepdims=False) for k in range(n_z)]
        return [mine[0]] + [over_z(mine[k], k) for k in range(1, n_z)]

    def sum_of(values):
        total = values[0].astype(F32)
        for value in values[1:]:
            total = total + value.astype(F32)
        return total

    def plane(value):
        return [value] + [over_seq(value, j) for j in range(1, n_seq)]

    def seq_to_all(value):
        return lax.all_to_all(value, "seq", 0, 0, tiled=True)

    def gather_seq(value):
        return seq_to_all(jnp.broadcast_to(value[None], (n_seq,) + value.shape))

    def to_rows(value):
        return seq_to_all(value.reshape((n_seq, rows) + value.shape[1:]))

    def from_rows(value):
        return seq_to_all(value).reshape((row_count,) + value.shape[2:])

    first_cols = pack(
        n_z, blocks, qkv_weight, mod_weight, up_weight, (mod_bias, query_bias, value_bias, out_bias, up_bias, down_bias)
    )
    first_got = dense_to_all(first_cols)
    down_got = plane(tie(down_weight, first_cols))

    places = jnp.arange(seq_tokens, dtype=jnp.int32)
    kept = tie(kept, first_cols)
    hits = kept[:, :, None] == places
    pick = hits.astype(BF)
    kept_here = jnp.any(hits, 1)

    def pick_kept(value):
        return jnp.einsum("rkt,rtd->rkd", pick, value, preferred_element_type=F32).astype(BF)

    def put_kept(value, base):
        spread = jnp.einsum("rkt,rkd->rtd", pick, value, preferred_element_type=F32).astype(BF)
        return jnp.where(kept_here[:, :, None], spread, base)

    picked = pick_kept(tokens)
    picked_ct = pick_kept(cotangent)
    inputs = to_rows(tie(picked, first_got))

    cond_float = conditioning.astype(F32).reshape(row_count * slots, model)
    cond_act = (cond_float / (1.0 + jnp.exp(-cond_float))).astype(BF)
    act_other = over_core(cond_act)
    act_pair = jnp.concatenate([jnp.where(core_at == 0, cond_act, act_other), jnp.where(core_at == 0, act_other, cond_act)])
    act_got = [act_pair] + [over_z(act_pair, k) for k in range(1, n_z)]
    act_all = jnp.take(jnp.stack(act_got), z_relative, axis=0).reshape(-1, model)

    numbers = jnp.arange(slots, dtype=jnp.int32)
    query_seg = jnp.sum(jnp.where(hits, segments[:, None, :], 0), -1)
    kept_hits = jnp.sum((query_seg[:, :, None] == numbers).astype(jnp.int32), 1)
    all_hits = jnp.sum((segments[:, :, None] == numbers).astype(jnp.int32), 1)
    small = jnp.concatenate([query_seg, kept_hits, all_hits - kept_hits], -1)
    small_got = plane(small)
    small = jnp.take(jnp.stack(small_got), seq_relative, axis=0)
    sample_counts = jnp.sum(small[:, :, kept_count:], 0).reshape(row_count, 2, slots).transpose(0, 2, 1)
    seg = lax.dynamic_slice_in_dim(small[:, :, :kept_count], seq_at * rows, rows, 1)
    seg_rows = seg.transpose(1, 0, 2).reshape(rows, 1, n_seq * kept_count)
    seg_cols = seg_rows.reshape(rows, n_seq * kept_count, 1)
    seg_tokens = seg.reshape(n_seq, rows, kept_count, 1)

    qkv_rows, z_cols = unpack(tie(first_got, *act_got[1:], *small_got[1:], *down_got[1:], picked), n_z, shard, mod_shard + ff_shard, mod_shard + ff_shard + 4 * shard)
    qkv_got = [qkv_rows] + [over_z(qkv_rows, k) for k in range(1, n_z)]
    (w_own,) = turn(z_scalar, qkv_got, blocks * shard, (0, 3 * width))
    z_got = to_z(tie(z_cols, *qkv_got[1:]))
    mod_cols, up_part, bias_got = turn(z_scalar, z_got, blocks * shard, (0, mod_shard, mod_shard + ff_shard))
    bias_got = bias_got.astype(F32)
    mod_b = bias_got[:, :blocks, :mod_shard].reshape(-1)
    up_b = bias_got[:, :blocks, mod_shard:].reshape(-1)
    query_b, value_b, out_b, down_b = [
        bias_got[:, blocks:, i * shard : (i + 1) * shard].reshape(-1) for i in range(4)
    ]

    mod_part = tie(dot_nt(act_all, mod_cols), inputs).reshape(devices, rows * slots, mod_shard)
    modulation = tie(all_to_all(mod_part), picked_ct).transpose(1, 0, 2).reshape(rows * slots, 6 * model) + mod_b
    table = modulation.reshape(rows, slots, 6, model)

    def token_mod(index):
        value = table[None, :, None, 0, index]
        for slot in range(1, slots):
            value = jnp.where(seg_tokens == slot, table[None, :, None, slot, index], value)
        return value

    hidden_one = (normalize(inputs.astype(F32))[0] * (1.0 + token_mod(1)) + token_mod(0)).astype(BF)

    spread_out = []
    for d in range(devices):
        z, c, s = d % n_z, (d // n_z) // n_seq, (d // n_z) % n_seq
        spread_out.append((d, (z * 2 + c) * n_seq + s))
    out_part = lax.ppermute(out_weight, EVERY, spread_out)
    out_part = tie(out_part, *z_got[1:])
    out_got = [out_part] + [over_z(out_part, k) for k in range(1, n_z)]
    o_own = join(z_scalar, out_got)
    w_all = plane(w_own)
    w_all = w_all + [over_core(w) for w in w_all]

    down_ring = [place(seq_scalar, down_got)]
    up_ring = [gather_seq(tie(up_part, hidden_one))]
    down_ring.append(shift_z(tie(down_ring[0], *out_got[1:]), 1))
    for t in range(2, n_z):
        if t == 2:
            down_ring.append(shift_z(tie(down_ring[1], hidden_one), 1))
            up_ring.append(shift_z(tie(up_ring[0], down_ring[2]), 1))
        else:
            down_ring.append(shift_z(tie(down_ring[-1], up_ring[-1]), 1))
        up_ring.append(shift_z(tie(up_ring[-1], down_ring[-1]) if t > 2 else up_ring[-1], 1))
    while len(up_ring) < n_z:
        up_ring.append(shift_z(up_ring[-1], 1))
    down_other = [over_core(value) for value in down_ring]
    up_other = [over_core(value) for value in up_ring]
    o_all = plane(tie(o_own, hidden_one))
    o_all = o_all + [over_core(o) for o in o_all]

    def by_block(value):
        return jnp.take(value.reshape(blocks, 1, width), relative, axis=0)

    query_b, value_b = by_block(query_b), by_block(value_b)
    up_b = jnp.take(up_b.reshape(n_z, 2, n_seq * ff_shard), core_relative, axis=1)
    up_b = jnp.take(up_b, z_ring, axis=0).reshape(n_z, 1, blocks * ff_shard)

    def pair(value, j):
        return jnp.stack([value[j], value[j + n_seq]])

    saved = []
    for j in range(n_seq):
        saved.append(attn_fwd(
            hidden_one, w_all[j], w_all[j + n_seq], pair(query_b, j), pair(value_b, j), seg_cols, seg_rows, head_size, [],
        ))
    branch_attn, mid, hidden_two = after_attn(
        inputs, seg_tokens, table, out_b.reshape(1, -1), [s[3] for s in saved], o_all, [],
    )
    grad_result = to_rows(tie(picked_ct, up_ring[0]))
    grad_mlp = (grad_result.astype(F32) * token_mod(5)).astype(BF)
    grad_down_bias = jnp.sum(grad_mlp.astype(F32), (0, 1, 2))

    order = list(range(n_z))
    hidden_flat = hidden_two.reshape(flat, model)
    grad_flat = grad_mlp.reshape(flat, model)
    sums = None
    cores, sends, planes, down_sums, grad_up_bias = [], [], [], {}, {}
    ring = []
    for at, t in enumerate(order):
        ups = [up_ring[t], up_other[t]]
        downs = [down_ring[t], down_other[t]]
        if ff_shard % 16:
            ups = [jnp.concatenate([u.reshape(-1, model) for u in ups])[None]]
            downs = [jnp.concatenate([d.reshape(-1, model) for d in downs])[None]]
        wait = []
        if at >= 2:
            wait.extend(sends[at - 2])
        if at >= 3:
            wait.append(planes[at - 3])
        mlp_sum, gh_sum, own, other, grad_up_bias[t] = mlp_step(
            hidden_flat, grad_flat, up_b[t : t + 1], ups, downs, sums, wait
        )
        sums = (mlp_sum, gh_sum)
        cores.append(over_core(other))
        both = (own.astype(F32) + cores[at].astype(F32)).reshape(2, n_seq, ff_shard, model)
        sends.append([both[0].astype(BF)])
        planes.append(seq_to_all(sends[at][0]))
        down_sums[t] = both[1]
        if t and len(ring) == t - 1:
            value = both[1] if t == 1 else both[1] + ring[-1].astype(F32)
            sends[at].append(value.astype(BF))
            ring.append(shift_z(sends[at][1], 1))

    last = n_z - 1
    res, grad_mid, grad_branch, sums_late, grad_out_bias = after_mlp(
        mid, sums[0].reshape(mid.shape), sums[1].reshape(mid.shape), branch_attn, grad_result, seg_tokens, table,
        down_b.reshape(1, -1), sends[last - 1] + [planes[last - 2]],
    )

    def natural_block(value):
        return by_block(value.reshape(-1))

    late_bias = jnp.concatenate([natural_block(grad_out_bias), natural_block(grad_down_bias)], -1)
    late = sums_late.reshape(rows * slots, 4, devices, shard).transpose(2, 0, 1, 3).reshape(devices, rows * slots, -1)
    late = late.astype(BF)
    waits = sends[last] + [planes[last - 1]]
    grad_hidden = None
    w_cores, w_values, w_planes = [], [], []
    for at, j in enumerate([n_seq - 1] + list(range(1, n_seq - 1)) + [0]):
        g_own, g_other, grad_hidden = attn_bwd(
            hidden_one, grad_branch, w_all[j], w_all[j + n_seq], o_all[j], o_all[j + n_seq], saved[j],
            pair(late_bias, j), seg_cols, seg_rows, head_size, grad_hidden, waits,
        )
        waits = []
        if at == 0:
            waits = [planes[last]]
            late = all_to_all(tie(late, g_own)).reshape(-1, 4 * shard)
            res = tie(res, g_own)
            res_mine = [lax.dynamic_index_in_dim(res, seq_at ^ k, 0, keepdims=False) for k in range(n_seq)]
            res_got = [res_mine[0]] + [over_seq(res_mine[k], k) for k in range(1, n_seq)]
            down_last = (down_sums[0] + ring[-1].astype(F32)).astype(BF)
        elif at == 1:
            late_mod = dot_tn(act_all, tie(late, g_own)).astype(BF).reshape(devices, shard, 4 * shard)
            natural = jnp.stack([grad_up_bias[t] for t in range(n_z)]).reshape(n_z, 2, n_seq * ff_shard)
            natural = jnp.take(jnp.take(natural, core_relative, axis=1), z_ring, axis=0).reshape(devices, 1, ff_shard)
            late_got = all_to_all(jnp.concatenate([late_mod, natural.astype(BF)], 1))
            up_bias_grad = jnp.sum(late_got[:, shard].astype(F32), 0)
            up_turned = turn_up(z_scalar, [planes[order.index(t)] for t in range(n_z)])
            up_parts = to_z(up_turned)
            waits = [ring[-1], late, up_turned] + res_got[1:]
        elif at == 2:
            waits = [late_got]
            down_parts = seq_to_all(tie(down_last, g_own))
            down_grad = jnp.sum(down_parts.astype(F32), 0)
        elif at == 3:
            waits = [down_parts] + up_parts[1:]
        w_cores.append(over_core(g_other))
        w_values.append((g_own.astype(F32) + w_cores[at].astype(F32)).astype(BF))
        w_planes.append(over_seq(w_values[at], j) if j else w_values[at])
        if at >= 1:
            waits.append(w_values[at - 1])
        if at == n_seq - 2:
            waits.append(w_values[at])

    grad_x, sums_early = last_step(inputs, grad_hidden, grad_mid, seg_tokens, table, waits)
    grad_mine = [lax.dynamic_index_in_dim(grad_x, seq_at ^ k, 0, keepdims=False) for k in range(n_seq)]
    grad_got = [grad_mine[0]] + [over_seq(grad_mine[k], k) for k in range(1, n_seq)]

    def in_place(got):
        return place(seq_scalar, got).reshape((row_count,) + got[0].shape[1:])

    res_got[0] = tie(res_got[0], grad_x)
    output = put_kept(in_place(res_got), tokens)
    tokens_grad = put_kept(in_place(grad_got), cotangent)

    qkv_parts, out_parts = split_parts(w_planes, n_z)
    qkv_parts = to_z(qkv_parts)
    out_parts = to_z(out_parts)
    back_out = lax.ppermute(sum_of(out_parts).astype(BF), EVERY, [(t, d) for d, t in spread_out]).astype(F32)
    out_grad = back_out[:part]
    small_grads = back_out[part : part + 4, :part]

    early = sums_early.reshape(rows * slots, 2, devices, shard).transpose(2, 0, 1, 3).reshape(devices, rows * slots, -1)
    early = all_to_all(early.astype(BF)).reshape(-1, 2 * shard)
    early_mod = dot_tn(act_all, early).astype(BF).reshape(devices, shard, 2 * shard)
    mod_sums = jnp.concatenate([jnp.sum(sums_early, (0, 1)), jnp.sum(sums_late, (0, 1))]).reshape(devices, 6 * shard)
    mod_sums = mod_sums.astype(BF).reshape(devices, 3, 2 * shard)
    mod_got = all_to_all(jnp.concatenate([early_mod, mod_sums], 1))
    mod_bias_grad = jnp.sum(mod_got[:, shard:].reshape(devices, -1).astype(F32), 0)
    dense_got = dense_to_all(deal(qkv_parts, up_parts, blocks))
    qkv_grad, up_grad = columns(
        [dense_got], [(0, shard, 0, width, 3), (0, shard, 3 * width, ff_shard, n_z)]
    )
    (mod_grad,) = mod_columns(mod_got, late_got, shard)
    return (
        output, tokens_grad, mod_grad, mod_bias_grad, qkv_grad, small_grads[0], small_grads[1],
        out_grad, small_grads[2], up_grad, up_bias_grad, down_grad, small_grads[3], sample_counts,
    )


def solution(mesh):
    n_batch, n_seq = mesh.shape["batch"], mesh.shape["seq"]
    split = Mesh(mesh.devices.reshape(n_batch // 2, 2, n_seq), ("z", "core", "seq"))
    batch = ("z", "core")
    both = ("z", "core", "seq")
    row_split = P(batch, "seq", None)
    matrix = P(both, None)
    vector = P(both)
    return jax.shard_map(
        functools.partial(body, n_batch // 2, n_seq),
        mesh=split,
        in_specs=(
            row_split, P(batch, None, None), P(batch, "seq"), P(batch, "seq"), row_split,
            matrix, vector, matrix, vector, vector, matrix, vector, matrix, vector, matrix, vector,
        ),
        out_specs=(
            row_split, row_split, matrix, vector, matrix, vector, vector,
            matrix, vector, matrix, vector, matrix, vector, P(batch, None, None),
        ),
        check_vma=False,
    )
```

time: 1170 us -> 809 us (0.69)
  Pallas kernels: 144 us -> 358 us
  blocking collectives: 176 us -> 0 us
  local copies, waits for them, and re-layouts: 199 us -> 55.1 us
  matrix products: 160 us -> 18.6 us
  waiting for transfers between devices: 213 us -> 123 us
  other arithmetic: 127 us -> 61.2 us
  starting transfers between devices: 124 us -> 177 us
  between operations: 17.7 us -> 2.3 us
    pallas_call x1 -> x24, Pallas kernels: 88 us -> 311 us  [the longest x4 126 us: mlp_step(): pl.pallas_call(functools.partial(mlp_kernel, len(ups), len(downs), first,...]
    ppermute x36 -> x21, waiting for transfers between devices: 199 us -> 17.8 us  [over_seq(): return lax.ppermute(value, 'seq', [(i, i ^ by) for i in range(n_seq)])]
    unnamed x3 -> x0, blocking collectives: 116 us -> none
    all_to_all x0 -> x15, starting transfers between devices: none -> 76.5 us  [the longest x8 33.6 us: seq_to_all(): return lax.all_to_all(value, 'seq', 0, 0, tiled=True)]
    unnamed x341 -> x149, local copies, waits for them, and re-layouts: 77 us -> 9.33 us
    all_gather x4 -> x0, blocking collectives: 59.7 us -> none  [the longest x2 34.7 us: gather_z(): lax.all_gather(value, 'batch', axis=0, tiled=True, axis_index_groups=z_gr...]
    dot_general x3 -> x0, matrix products: 52.7 us -> none  [the longest x2 49.5 us: dot_nn(): lax.dot_general(a, b, (((1,), (0,)), ((), ())), preferred_element_type=F32)]
    all_to_all x0 -> x15, waiting for transfers between devices: none -> 47 us  [the longest x5 34.6 us: all_to_all(): return lax.all_to_all(value, EVERY, 0, 0, tiled=True)]
  transfers between devices with their start and end apart: 107 -> 93, of which waited for: 26 -> 16; matrix products, arithmetic and copies ran while one was open for 33% -> 15% of each run, Pallas kernels for 12% -> 44%
where the time goes in v2:
time: 809 us; the launch traced here: 795 us
  Pallas kernels  358 us (44%)
  starting transfers between devices  177 us (22%)
  waiting for transfers between devices  123 us (15%)
  other arithmetic  61.2 us (8%)
  local copies, waits for them, and re-layouts  55.1 us (7%)
  matrix products  18.6 us (2%)
    pallas_call x4, Pallas kernels, mlp_step(): pl.pallas_call(functools.partial(mlp_kernel, len(ups), len(downs), first,...  126 us
    pallas_call x4, Pallas kernels, attn_bwd(): pl.pallas_call(functools.partial(attn_bwd_kernel, head_size, first, len(w...  96.4 us
    pallas_call x4, Pallas kernels, attn_fwd(): pl.pallas_call(functools.partial(attn_fwd_kernel, head_size), grid=(rows,...  46.8 us
    ppermute x21, waiting for transfers between devices, over_z(): return lax.ppermute(value, 'z', [(i, i ^ by) for i in range(n_z)])  38.9 us
    ppermute x21, starting transfers between devices, over_z(): return lax.ppermute(value, 'z', [(i, i ^ by) for i in range(n_z)])  34.7 us
    all_to_all x5, waiting for transfers between devices, all_to_all(): return lax.all_to_all(value, EVERY, 0, 0, tiled=True)  34.6 us
    all_to_all x8, starting transfers between devices, seq_to_all(): return lax.all_to_all(value, 'seq', 0, 0, tiled=True)  33.6 us
    all_to_all x5, starting transfers between devices, all_to_all(): return lax.all_to_all(value, EVERY, 0, 0, tiled=True)  28.5 us
  transfers between devices with their start and end apart: 93, of which 16 were waited for; matrix products, arithmetic and copies ran while one was open for 15% of the time, Pallas kernels for 44%

profile of v2, /device:TPU:1, one launch (start us, length us, event | category | flops | bytes accessed | tf_op | source)
XLA Modules:
  0.0 795.0 jit_solution(10665847786814664461)
XLA Ops:
  12.9 6.3 all-to-all-start
  20.3 4.8 convolution_convert_fusion.3
  39.7 8.8 %collective-permute-start.23 = (bf16[36,1152]{1,0:T(8,128)(2,1)S(1)}, bf16[36,1152]{1,0:T(8,128)(2,1)}, u32[]{:S(2)}, u32[]{:S(2)}) collective-permute-start(bf16[36,1152]{1,0:T(8,128)(2,1)S(1)} %copy-done.64), channel_id=1, source_target_pairs={{0,0},{1,8},{2,16},{3,24},{4,1},{5,9},{6,17},{7,25},{8,2},{9,10},{... | collective-permute-start | bytes 248840 | tf_op jit(solution)/shard_map/ppermute | solution.py:854
  64.5 13.2 %collective-permute-done.11.refs_2_ = bf16[288,432]{1,0:T(8,128)(2,1)} collective-permute-done((bf16[288,432]{1,0:T(8,128)(2,1)}, bf16[288,432]{1,0:T(8,128)(2,1)}, u32[]{:S(2)}, u32[]{:S(2)}) %collective-permute-start.11) | collective-permute-done | bytes 248864 | tf_op jit(solution)/shard_map/ppermute | solution.py:747
  79.8 6.6 collective-permute-start.13
  94.8 9.1 %collective-permute-done.14.refs_2_ = bf16[304,360]{1,0:T(8,128)(2,1)S(1)} collective-permute-done((bf16[304,360]{1,0:T(8,128)(2,1)S(1)}, bf16[304,360]{1,0:T(8,128)(2,1)S(1)}, u32[]{:S(2)}, u32[]{:S(2)}) %collective-permute-start.14) | collective-permute-done | bytes 218912 | tf_op jit(solution)/shard_map/ppermute | solution.py:747
  103.9 5.3 collective-permute-start.24
  139.6 4.1 all-to-all-start.2
  144.9 26.5 %all-to-all-done.2 = f32[32,8,216]{2,1,0:T(8,128)S(1)} async-done(((f32[32,8,216]{2,1,0:T(8,128)}), f32[32,8,216]{2,1,0:T(8,128)S(1)}, u32[]{:S(2)}, u32[]{:S(2)}) %all-to-all-start.2) | async-done | bytes 221216 | tf_op jit(solution)/shard_map/all_to_all | solution.py:753
  172.0 9.4 %fusion.5.h_ref = bf16[4,2,128,1152]{3,2,1,0:T(8,128)(2,1)} fusion(bf16[4,2,128,1152]{3,2,1,0:T(8,128)(2,1)S(1)} %all-to-all-done.1.x_ref, f32[2,1152]{1,0:T(2,128)S(1)} %bitcast.188, f32[2,1152]{1,0:T(2,128)S(1)} %bitcast.189, f32[2,1152]{1,0:T(2,128)S(1)} %bitcast.190, f32[2,1152]{1,0:T(2,128)S(1)} %bitcast.191, f32[2,1152]{1,0:T(2,128)S(1)} %bitcast.192, ...), kind=kLoop, calls=%fused_computation.23 | loop fusion | flops 15335424 | bytes 4803584 | tf_op jit(solution)/shard_map/convert_element_type | solution.py:848
  182.6 4.3 all-to-all-start.3
  189.6 11.7 %shard_map.267 = (bf16[2,4,2,128,144]{4,3,2,1,0:T(8,128)(2,1)}, bf16[2,4,2,128,144]{4,3,2,1,0:T(8,128)(2,1)}, bf16[2,4,2,128,144]{4,3,2,1,0:T(8,128)(2,1)}, bf16...) custom-call(bf16[4,2,128,1152]{3,2,1,0:T(8,128)(2,1)} %fusion.5.h_ref, bf16[432,1152]{1,0:T(8,128)(2,1)} %shard_map.266.w_a, ...), custom_call_target="tpu_custom_call" | custom-call | flops 13799999488 | tf_op jit(solution)/shard_map/pallas_call | solution.py:352
  201.5 11.7 %shard_map.270 = (bf16[2,4,2,128,144]{4,3,2,1,0:T(8,128)(2,1)}, bf16[2,4,2,128,144]{4,3,2,1,0:T(8,128)(2,1)}, bf16[2,4,2,128,144]{4,3,2,1,0:T(8,128)(2,1)}, bf16...) custom-call(bf16[4,2,128,1152]{3,2,1,0:T(8,128)(2,1)} %fusion.5.h_ref, bf16[432,1152]{1,0:T(8,128)(2,1)} %collective-permute-done.21.w_a, ...), custom_call_target="tpu_custom_call" | custom-call | flops 13799999488 | tf_op jit(solution)/shard_map/pallas_call | solution.py:352
  213.5 11.7 %shard_map.269 = (bf16[2,4,2,128,144]{4,3,2,1,0:T(8,128)(2,1)}, bf16[2,4,2,128,144]{4,3,2,1,0:T(8,128)(2,1)}, bf16[2,4,2,128,144]{4,3,2,1,0:T(8,128)(2,1)}, bf16...) custom-call(bf16[4,2,128,1152]{3,2,1,0:T(8,128)(2,1)} %fusion.5.h_ref, bf16[432,1152]{1,0:T(8,128)(2,1)} %collective-permute-done.19.w_a, ...), custom_call_target="tpu_custom_call" | custom-call | flops 13799999488 | tf_op jit(solution)/shard_map/pallas_call | solution.py:352
  231.6 11.7 %shard_map.268 = (bf16[2,4,2,128,144]{4,3,2,1,0:T(8,128)(2,1)}, bf16[2,4,2,128,144]{4,3,2,1,0:T(8,128)(2,1)}, bf16[2,4,2,128,144]{4,3,2,1,0:T(8,128)(2,1)}, bf16...) custom-call(bf16[4,2,128,1152]{3,2,1,0:T(8,128)(2,1)} %fusion.5.h_ref, bf16[432,1152]{1,0:T(8,128)(2,1)} %collective-permute-done.17.w_a, ...), custom_call_target="tpu_custom_call" | custom-call | flops 13799999488 | tf_op jit(solution)/shard_map/pallas_call | solution.py:352
  248.5 14.8 %shard_map.272 = (f32[4,2,128,1152]{3,2,1,0:T(8,128)}, f32[4,2,128,1152]{3,2,1,0:T(8,128)}, bf16[4,2,128,1152]{3,2,1,0:T(8,128)(2,1)}) custom-call(bf16[4,2,128,1152]{3,2,1,0:T(8,128)(2,1)} %copy-done, s32[4,2,128,1]{3,2,1,0:T(8,128)} %copy.149.seg_ref, f32[2,4,6,1152]{3,2,1,0:T(8,128)} %copy-done.21, f32[1,1152]{1,0:T(1,128)} %reshape_reshape.21.ob_ref, ...), custom_call_target="tpu_custom_call" | custom-call | flops 17250000896 | tf_op jit(solution)/shard_map/pallas_call | solution.py:511
  263.4 17.0 %collective-permute-done.36.rest_0_ = bf16[4,144,1152]{2,1,0:T(8,128)(2,1)} collective-permute-done((bf16[4,144,1152]{2,1,0:T(8,128)(2,1)}, bf16[4,144,1152]{2,1,0:T(8,128)(2,1)}, u32[]{:S(2)}, u32[]{:S(2)}) %collective-permute-start.36) | collective-permute-done | bytes 1327136 | tf_op jit(solution)/shard_map/ppermute | solution.py:750
  284.8 30.0 %shard_map.274 = (f32[1024,1152]{1,0:T(8,128)}, f32[1024,1152]{1,0:T(8,128)}, bf16[2,576,1152]{2,1,0:T(8,128)(2,1)}, bf16[2,576,1152]{2,1,0:T(8,128)(2,1)}, f32[1,1152]{1,0:T(1,128)}) custom-call(bf16[1024,1152]{1,0:T(8,128)(2,1)} %bitcast.215, bf16[1024,1152]{1,0:T(8,128)(2,1)} %bitcast.169, f32[1,1,1152]{2,1,0:T(1,128)} %slice.258.ub_ref, ...), custom_call_target="tpu_custom_call" | custom-call | flops 36800000000 | tf_op jit(solution)/shard_map/pallas_call | solution.py:683
  318.7 31.8 %shard_map.275 = (f32[1024,1152]{1,0:T(8,128)}, f32[1024,1152]{1,0:T(8,128)}, bf16[2,576,1152]{2,1,0:T(8,128)(2,1)}, bf16[2,576,1152]{2,1,0:T(8,128)(2,1)}, f32[1,1152]{1,0:T(1,128)}) custom-call(bf16[1024,1152]{1,0:T(8,128)(2,1)} %bitcast.216, bf16[1024,1152]{1,0:T(8,128)(2,1)} %bitcast.170, ...), custom_call_target="tpu_custom_call", output_to_operand_aliasing={{0}: (7, {}), {1}: (8, {})} | custom-call | flops 36800000000 | tf_op jit(solution)/shard_map/pallas_call | solution.py:683
  358.3 4.3 all-to-all-start.5
  362.6 31.9 %shard_map.276 = (f32[1024,1152]{1,0:T(8,128)}, f32[1024,1152]{1,0:T(8,128)}, bf16[2,576,1152]{2,1,0:T(8,128)(2,1)}, bf16[2,576,1152]{2,1,0:T(8,128)(2,1)}, f32[1,1152]{1,0:T(1,128)}) custom-call(bf16[1024,1152]{1,0:T(8,128)(2,1)} %bitcast.217, bf16[1024,1152]{1,0:T(8,128)(2,1)} %bitcast.171, ...), custom_call_target="tpu_custom_call", output_to_operand_aliasing={{0}: (8, {}), {1}: (9, {})} | custom-call | flops 36800000000 | tf_op jit(solution)/shard_map/pallas_call | solution.py:683
  403.7 4.3 all-to-all-start.6
  408.1 32.0 %shard_map.277 = (f32[1024,1152]{1,0:T(8,128)}, f32[1024,1152]{1,0:T(8,128)}, bf16[2,576,1152]{2,1,0:T(8,128)(2,1)}, bf16[2,576,1152]{2,1,0:T(8,128)(2,1)}, f32[1,1152]{1,0:T(1,128)}) custom-call(bf16[1024,1152]{1,0:T(8,128)(2,1)} %bitcast.218, bf16[1024,1152]{1,0:T(8,128)(2,1)} %bitcast.172, ...), custom_call_target="tpu_custom_call", output_to_operand_aliasing={{0}: (10, {}), {1}: (11, {})} | custom-call | flops 36800000000 | tf_op jit(solution)/shard_map/pallas_call | solution.py:683
  450.3 4.3 all-to-all-start.7
  454.7 21.3 %shard_map.278 = (bf16[4,2,128,1152]{3,2,1,0:T(8,128)(2,1)}, f32[4,2,128,1152]{3,2,1,0:T(8,128)}, bf16[4,2,128,1152]{3,2,1,0:T(8,128)(2,1)}, f32[2,4,4,1152]{3,2,1,0:T(4,128)}, f32[1,1152]{1,0:T(1,128)}) custom-call(f32[4,2,128,1152]{3,2,1,0:T(8,128)} %get-tuple-element.126.mid_ref, f32[4,2,128,1152]{3,2,1,0:T(8,128)} %bitcast.213, ...), custom_call_target="tpu_custom_call" | custom-call | flops 24149999616 | tf_op jit(solution)/shard_map/pallas_call | solution.py:558
  489.2 4.7 all-to-all-start.9
  493.9 23.6 %shard_map.279 = (bf16[592,1152]{1,0:T(8,128)(2,1)}, bf16[592,1152]{1,0:T(8,128)(2,1)}, f32[4,2,128,1152]{3,2,1,0:T(8,128)}) custom-call(bf16[4,2,128,1152]{3,2,1,0:T(8,128)(2,1)} %fusion.5.h_ref, bf16[4,2,128,1152]{3,2,1,0:T(8,128)(2,1)} %get-tuple-element.152.gb_ref, bf16[432,1152]{1,0:T(8,128)(2,1)} %collective-permute-done.21.w_a, ...), custom_call_target="tpu_custom_call" | custom-call | flops 27599998976 | tf_op jit(solution)/shard_map/pallas_call | solution.py:447
  522.7 6.9 all-to-all-start.8
  529.6 24.3 %shard_map.280 = (bf16[592,1152]{1,0:T(8,128)(2,1)}, bf16[592,1152]{1,0:T(8,128)(2,1)}, f32[4,2,128,1152]{3,2,1,0:T(8,128)}) custom-call(bf16[4,2,128,1152]{3,2,1,0:T(8,128)(2,1)} %fusion.5.h_ref, bf16[4,2,128,1152]{3,2,1,0:T(8,128)(2,1)} %get-tuple-element.152.gb_ref, ...), custom_call_target="tpu_custom_call", output_to_operand_aliasing={{2}: (15, {})} | custom-call | flops 27599998976 | tf_op jit(solution)/shard_map/pallas_call | solution.py:447
  555.7 6.2 all-to-all-start.10
  561.9 5.5 shard_map.281.rest_2_
  571.7 24.3 %shard_map.282 = (bf16[592,1152]{1,0:T(8,128)(2,1)}, bf16[592,1152]{1,0:T(8,128)(2,1)}, f32[4,2,128,1152]{3,2,1,0:T(8,128)}) custom-call(bf16[4,2,128,1152]{3,2,1,0:T(8,128)(2,1)} %fusion.5.h_ref, bf16[4,2,128,1152]{3,2,1,0:T(8,128)(2,1)} %get-tuple-element.152.gb_ref, ...), custom_call_target="tpu_custom_call", output_to_operand_aliasing={{2}: (21, {})} | custom-call | flops 27599998976 | tf_op jit(solution)/shard_map/pallas_call | solution.py:447
  596.0 4.3 all-to-all-start.11
  608.8 7.9 all-to-all-done.11.rest_0_
  625.0 24.3 %shard_map.283 = (bf16[592,1152]{1,0:T(8,128)(2,1)}, bf16[592,1152]{1,0:T(8,128)(2,1)}, f32[4,2,128,1152]{3,2,1,0:T(8,128)}) custom-call(bf16[4,2,128,1152]{3,2,1,0:T(8,128)(2,1)} %fusion.5.h_ref, bf16[4,2,128,1152]{3,2,1,0:T(8,128)(2,1)} %get-tuple-element.152.gb_ref, bf16[432,1152]{1,0:T(8,128)(2,1)} %shard_map.266.w_a, ...), custom_call_target="tpu_custom_call", output_to_operand_aliasing={{2}: (17, {})} | custom-call | flops 27599998976 | tf_op jit(solution)/shard_map/pallas_call | solution.py:447
  650.7 11.8 %shard_map.284 = (bf16[4,2,128,1152]{3,2,1,0:T(8,128)(2,1)}, f32[2,4,2,1152]{3,2,1,0:T(2,128)}) custom-call(bf16[4,2,128,1152]{3,2,1,0:T(8,128)(2,1)} %copy-done, f32[4,2,128,1152]{3,2,1,0:T(8,128)} %get-tuple-element.189.gh_ref, f32[4,2,128,1152]{3,2,1,0:T(8,128)} %get-tuple-element.190.gm_ref, s32[4,2,128,1]{3,2,1,0:T(8,128)} %copy.149.seg_ref, ...), custom_call_target="tpu_custom_call" | custom-call | flops 13799999488 | tf_op jit(solution)/shard_map/pallas_call | solution.py:598
  664.7 4.7 all-to-all-start.12
  679.8 6.7 all-to-all-start.13
  686.6 4.7 broadcast_select_fusion.1
  692.6 5.1 collective-permute-start.69
  697.8 8.1 %all-to-all-done.13.early_ref = bf16[32,39,72]{2,1,0:T(8,128)(2,1)S(1)} async-done(((bf16[32,39,72]{2,1,0:T(8,128)(2,1)}), bf16[32,39,72]{2,1,0:T(8,128)(2,1)S(1)}, u32[]{:S(2)}, u32[]{:S(2)}) %all-to-all-start.13) | async-done | bytes 179744 | tf_op jit(solution)/shard_map/all_to_all | solution.py:753
  715.5 17.7 %collective-permute-done.68.refs_1_ = bf16[592,1152]{1,0:T(8,128)(2,1)S(1)} collective-permute-done((bf16[592,1152]{1,0:T(8,128)(2,1)}, bf16[592,1152]{1,0:T(8,128)(2,1)S(1)}, u32[]{:S(2)}, u32[]{:S(2)}) %collective-permute-start.68) | collective-permute-done | bytes 1364000 | tf_op jit(solution)/shard_map/ppermute | solution.py:744
  734.3 4.4 shard_map.288
  749.8 8.3 %collective-permute-start.77 = (bf16[40,1152]{1,0:T(8,128)(2,1)S(1)}, bf16[40,1152]{1,0:T(8,128)(2,1)S(1)}, u32[]{:S(2)}, u32[]{:S(2)}) collective-permute-start(bf16[40,1152]{1,0:T(8,128)(2,1)S(1)} %fusion.13), channel_id=1, source_target_pairs={{0,0},{8,1},{16,2},{24,3},{1,4},{9,5},{17,6},{25,7},{2,8},{10,9},{... | collective-permute-start | bytes 276488 | tf_op jit(solution)/shard_map/ppermute | solution.py:996
  760.1 8.9 %collective-permute-done.72.refs_2_ = bf16[288,432]{1,0:T(8,128)(2,1)S(1)} collective-permute-done((bf16[288,432]{1,0:T(8,128)(2,1)S(1)}, bf16[288,432]{1,0:T(8,128)(2,1)S(1)}, u32[]{:S(2)}, u32[]{:S(2)}) %collective-permute-start.72) | collective-permute-done | bytes 248864 | tf_op jit(solution)/shard_map/ppermute | solution.py:747
  773.0 8.2 %all-to-all-start.14 = ((bf16[8,36,1008]{2,1,0:T(8,128)(2,1)}), bf16[8,36,1008]{2,1,0:T(8,128)(2,1)S(1)}, u32[]{:S(2)}, u32[]{:S(2)}) async-start(bf16[8,36,1008]{2,1,0:T(8,128)(2,1)} %shard_map.289), calls=%async_computation.14 | async-start | bytes 1310720 | tf_op jit(solution)/shard_map/all_to_all | solution.py:756
  781.2 4.7 broadcast_select_fusion
  787.1 4.5 all-to-all-done.14.refs_0_
  (486 shorter events, 226.2 us)
Async XLA Ops:
  10.3 39.2 %collective-permute-start.7 = (bf16[144,1152]{1,0:T(8,128)(2,1)S(1)}, bf16[144,1152]{1,0:T(8,128)(2,1)S(1)}, u32[]{:S(2)}, u32[]{:S(2)}) collective-permute-start(bf16[144,1152]{1,0:T(8,128)(2,1)S(1)} %copy-done.47), channel_id=1, source_target_pairs={{0,1},{1,0},{2,3},{3,2},{4,5},{5,4},{6,7},{7,6},{8,9},{9,8},{10,11... | collective-permute-start | bytes 995336 | tf_op jit(solution)/shard_map/ppermute | solution.py:744
  11.7 37.8 %collective-permute-start.8 = (bf16[144,1152]{1,0:T(8,128)(2,1)S(1)}, bf16[144,1152]{1,0:T(8,128)(2,1)S(1)}, u32[]{:S(2)}, u32[]{:S(2)}) collective-permute-start(bf16[144,1152]{1,0:T(8,128)(2,1)S(1)} %copy-done.47), channel_id=1, source_target_pairs={{0,2},{1,3},{2,0},{3,1},{4,6},{5,7},{6,4},{7,5},{8,10},{9,11},{10,... | collective-permute-start | bytes 995336 | tf_op jit(solution)/shard_map/ppermute | solution.py:744
  12.9 36.6 %all-to-all-start = ((bf16[8,40,1872]{2,1,0:T(8,128)(2,1)}), bf16[8,40,1872]{2,1,0:T(8,128)(2,1)}, u32[]{:S(2)}, u32[]{:S(2)}) async-start(bf16[8,40,1872]{2,1,0:T(8,128)(2,1)} %shard_map.263), calls=%async_computation | async-start | bytes 2457600 | tf_op jit(solution)/shard_map/all_to_all | solution.py:756
  39.7 52.3 %collective-permute-start.23 = (bf16[36,1152]{1,0:T(8,128)(2,1)S(1)}, bf16[36,1152]{1,0:T(8,128)(2,1)}, u32[]{:S(2)}, u32[]{:S(2)}) collective-permute-start(bf16[36,1152]{1,0:T(8,128)(2,1)S(1)} %copy-done.64), channel_id=1, source_target_pairs={{0,0},{1,8},{2,16},{3,24},{4,1},{5,9},{6,17},{7,25},{8,2},{9,10},{... | collective-permute-start | bytes 248840 | tf_op jit(solution)/shard_map/ppermute | solution.py:854
  59.7 78.9 %all-to-all-start.1 = ((bf16[4,2,128,1152]{3,2,1,0:T(8,128)(2,1)}), bf16[4,2,128,1152]{3,2,1,0:T(8,128)(2,1)S(1)}, u32[]{:S(2)}, u32[]{:S(2)}) async-start(bf16[4,2,128,1152]{3,2,1,0:T(8,128)(2,1)} %bitcast.168), calls=%async_computation.1 | async-start | bytes 4718592 | tf_op jit(solution)/shard_map/all_to_all | solution.py:772
  91.5 43.6 %collective-permute-start.21 = (bf16[432,1152]{1,0:T(8,128)(2,1)}, bf16[432,1152]{1,0:T(8,128)(2,1)}, u32[]{:S(2)}, u32[]{:S(2)}) collective-permute-start(bf16[432,1152]{1,0:T(8,128)(2,1)} %shard_map.266.w_a), channel_id=1, source_target_pairs={{0,3},{1,2},{2,1},{3,0},{4,7},{5,6},{6,5},{7,4},{8,11},{9,10},{10,... | collective-permute-start | bytes 2985992 | tf_op jit(solution)/shard_map/ppermute | solution.py:744
  91.9 46.1 %collective-permute-start.19 = (bf16[432,1152]{1,0:T(8,128)(2,1)}, bf16[432,1152]{1,0:T(8,128)(2,1)}, u32[]{:S(2)}, u32[]{:S(2)}) collective-permute-start(bf16[432,1152]{1,0:T(8,128)(2,1)} %shard_map.266.w_a), channel_id=1, source_target_pairs={{0,2},{1,3},{2,0},{3,1},{4,6},{5,7},{6,4},{7,5},{8,10},{9,11},{10,... | collective-permute-start | bytes 2985992 | tf_op jit(solution)/shard_map/ppermute | solution.py:744
  94.8 43.3 %collective-permute-start.17 = (bf16[432,1152]{1,0:T(8,128)(2,1)}, bf16[432,1152]{1,0:T(8,128)(2,1)}, u32[]{:S(2)}, u32[]{:S(2)}) collective-permute-start(bf16[432,1152]{1,0:T(8,128)(2,1)} %shard_map.266.w_a), channel_id=1, source_target_pairs={{0,1},{1,0},{2,3},{3,2},{4,5},{5,4},{6,7},{7,6},{8,9},{9,8},{10,11... | collective-permute-start | bytes 2985992 | tf_op jit(solution)/shard_map/ppermute | solution.py:744
  129.8 58.6 %collective-permute-start.16 = (bf16[432,1152]{1,0:T(8,128)(2,1)}, bf16[432,1152]{1,0:T(8,128)(2,1)}, u32[]{:S(2)}, u32[]{:S(2)}) collective-permute-start(bf16[432,1152]{1,0:T(8,128)(2,1)} %shard_map.266.w_a), channel_id=1, source_target_pairs={{0,4},{4,0},{1,5},{5,1},{2,6},{6,2},{3,7},{7,3},{8,12},{12,8},{9,1... | collective-permute-start | bytes 2985992 | tf_op jit(solution)/shard_map/ppermute | solution.py:741
  132.6 54.3 %collective-permute-start.34 = (bf16[4,144,1152]{2,1,0:T(8,128)(2,1)}, bf16[4,144,1152]{2,1,0:T(8,128)(2,1)}, u32[]{:S(2)}, u32[]{:S(2)}) collective-permute-start(bf16[4,144,1152]{2,1,0:T(8,128)(2,1)} %shard_map.273.rest_2_), channel_id=1, source_target_pairs={{0,8},{8,16},{16,24},{24,0},{1,9},{9,17},{17,25},{25,1},{2,10},{10... | collective-permute-start | bytes 3981320 | tf_op jit(solution)/shard_map/ppermute | solution.py:750
  135.1 66.2 %collective-permute-start.22 = (bf16[432,1152]{1,0:T(8,128)(2,1)}, bf16[432,1152]{1,0:T(8,128)(2,1)}, u32[]{:S(2)}, u32[]{:S(2)}) collective-permute-start(bf16[432,1152]{1,0:T(8,128)(2,1)} %collective-permute-done.21.w_a), channel_id=1, source_target_pairs={{0,4},{4,0},{1,5},{5,1},{2,6},{6,2},{3,7},{7,3},{8,12},{12,8},{9,1... | collective-permute-start | bytes 2985992 | tf_op jit(solution)/shard_map/ppermute | solution.py:741
  138.1 75.1 %collective-permute-start.20 = (bf16[432,1152]{1,0:T(8,128)(2,1)}, bf16[432,1152]{1,0:T(8,128)(2,1)}, u32[]{:S(2)}, u32[]{:S(2)}) collective-permute-start(bf16[432,1152]{1,0:T(8,128)(2,1)} %collective-permute-done.19.w_a), channel_id=1, source_target_pairs={{0,4},{4,0},{1,5},{5,1},{2,6},{6,2},{3,7},{7,3},{8,12},{12,8},{9,1... | collective-permute-start | bytes 2985992 | tf_op jit(solution)/shard_map/ppermute | solution.py:741
  138.1 90.8 %collective-permute-start.18 = (bf16[432,1152]{1,0:T(8,128)(2,1)}, bf16[432,1152]{1,0:T(8,128)(2,1)}, u32[]{:S(2)}, u32[]{:S(2)}) collective-permute-start(bf16[432,1152]{1,0:T(8,128)(2,1)} %collective-permute-done.17.w_a), channel_id=1, source_target_pairs={{0,4},{4,0},{1,5},{5,1},{2,6},{6,2},{3,7},{7,3},{8,12},{12,8},{9,1... | collective-permute-start | bytes 2985992 | tf_op jit(solution)/shard_map/ppermute | solution.py:741
  182.6 42.7 %all-to-all-start.3 = ((bf16[4,144,1152]{2,1,0:T(8,128)(2,1)}), bf16[4,144,1152]{2,1,0:T(8,128)(2,1)}, u32[]{:S(2)}, u32[]{:S(2)}) async-start(bf16[4,144,1152]{2,1,0:T(8,128)(2,1)} %broadcast_in_dim.255), calls=%async_computation.3 | async-start | bytes 2654208 | tf_op jit(solution)/shard_map/all_to_all | solution.py:772
  187.0 44.0 %collective-permute-start.27 = (bf16[144,1152]{1,0:T(8,128)(2,1)S(1)}, bf16[144,1152]{1,0:T(8,128)(2,1)}, u32[]{:S(2)}, u32[]{:S(2)}) collective-permute-start(bf16[144,1152]{1,0:T(8,128)(2,1)S(1)} %copy-done.48), channel_id=1, source_target_pairs={{0,1},{1,0},{2,3},{3,2},{4,5},{5,4},{6,7},{7,6},{8,9},{9,8},{10,11... | collective-permute-start | bytes 995336 | tf_op jit(solution)/shard_map/ppermute | solution.py:744
  188.4 42.6 %collective-permute-start.28 = (bf16[144,1152]{1,0:T(8,128)(2,1)S(1)}, bf16[144,1152]{1,0:T(8,128)(2,1)S(1)}, u32[]{:S(2)}, u32[]{:S(2)}) collective-permute-start(bf16[144,1152]{1,0:T(8,128)(2,1)S(1)} %copy-done.48), channel_id=1, source_target_pairs={{0,2},{1,3},{2,0},{3,1},{4,6},{5,7},{6,4},{7,5},{8,10},{9,11},{10,... | collective-permute-start | bytes 995336 | tf_op jit(solution)/shard_map/ppermute | solution.py:744
  225.2 56.1 %all-to-all-start.4 = ((bf16[4,2,128,1152]{3,2,1,0:T(8,128)(2,1)}), bf16[4,2,128,1152]{3,2,1,0:T(8,128)(2,1)S(1)}, u32[]{:S(2)}, u32[]{:S(2)}) async-start(bf16[4,2,128,1152]{3,2,1,0:T(8,128)(2,1)} %bitcast.30), calls=%async_computation.4 | async-start | bytes 4718592 | tf_op jit(solution)/shard_map/all_to_all | solution.py:772
  244.9 39.6 %collective-permute-start.45 = (bf16[4,144,1152]{2,1,0:T(8,128)(2,1)}, bf16[4,144,1152]{2,1,0:T(8,128)(2,1)}, u32[]{:S(2)}, u32[]{:S(2)}) collective-permute-start(bf16[4,144,1152]{2,1,0:T(8,128)(2,1)} %shard_map.273.rest_2_), channel_id=1, source_target_pairs={{0,4},{4,0},{1,5},{5,1},{2,6},{6,2},{3,7},{7,3},{8,12},{12,8},{9,1... | collective-permute-start | bytes 3981320 | tf_op jit(solution)/shard_map/ppermute | solution.py:741
  247.1 70.7 %collective-permute-start.43 = (bf16[4,144,1152]{2,1,0:T(8,128)(2,1)}, bf16[4,144,1152]{2,1,0:T(8,128)(2,1)}, u32[]{:S(2)}, u32[]{:S(2)}) collective-permute-start(bf16[4,144,1152]{2,1,0:T(8,128)(2,1)} %collective-permute-done.34.rest_2_), channel_id=1, source_target_pairs={{0,4},{4,0},{1,5},{5,1},{2,6},{6,2},{3,7},{7,3},{8,12},{12,8},{9,1... | collective-permute-start | bytes 3981320 | tf_op jit(solution)/shard_map/ppermute | solution.py:741
  247.2 37.7 %collective-permute-start.44 = (bf16[4,144,1152]{2,1,0:T(8,128)(2,1)}, bf16[4,144,1152]{2,1,0:T(8,128)(2,1)}, u32[]{:S(2)}, u32[]{:S(2)}) collective-permute-start(bf16[4,144,1152]{2,1,0:T(8,128)(2,1)} %all-to-all-done.3.rest_0_), channel_id=1, source_target_pairs={{0,4},{4,0},{1,5},{5,1},{2,6},{6,2},{3,7},{7,3},{8,12},{12,8},{9,1... | collective-permute-start | bytes 3981320 | tf_op jit(solution)/shard_map/ppermute | solution.py:741
  263.2 99.4 %collective-permute-start.49 = (bf16[4,144,1152]{2,1,0:T(8,128)(2,1)}, bf16[4,144,1152]{2,1,0:T(8,128)(2,1)}, u32[]{:S(2)}, u32[]{:S(2)}) collective-permute-start(bf16[4,144,1152]{2,1,0:T(8,128)(2,1)} %collective-permute-done.35.rest_2_), channel_id=1, source_target_pairs={{0,4},{4,0},{1,5},{5,1},{2,6},{6,2},{3,7},{7,3},{8,12},{12,8},{9,1... | collective-permute-start | bytes 3981320 | tf_op jit(solution)/shard_map/ppermute | solution.py:741
  280.4 38.3 %collective-permute-start.42 = (bf16[4,144,1152]{2,1,0:T(8,128)(2,1)}, bf16[4,144,1152]{2,1,0:T(8,128)(2,1)}, u32[]{:S(2)}, u32[]{:S(2)}) collective-permute-start(bf16[4,144,1152]{2,1,0:T(8,128)(2,1)} %collective-permute-done.36.rest_0_), channel_id=1, source_target_pairs={{0,4},{4,0},{1,5},{5,1},{2,6},{6,2},{3,7},{7,3},{8,12},{12,8},{9,1... | collective-permute-start | bytes 3981320 | tf_op jit(solution)/shard_map/ppermute | solution.py:741
  314.9 37.0 %collective-permute-start.47 = (bf16[2,576,1152]{2,1,0:T(8,128)(2,1)}, bf16[2,576,1152]{2,1,0:T(8,128)(2,1)}, u32[]{:S(2)}, u32[]{:S(2)}) collective-permute-start(bf16[2,576,1152]{2,1,0:T(8,128)(2,1)} %get-tuple-element.141), channel_id=1, source_target_pairs={{0,4},{4,0},{1,5},{5,1},{2,6},{6,2},{3,7},{7,3},{8,12},{12,8},{9,1... | collective-permute-start | bytes 7962632 | tf_op jit(solution)/shard_map/ppermute | solution.py:741
  317.8 44.8 %collective-permute-start.48 = (bf16[4,144,1152]{2,1,0:T(8,128)(2,1)}, bf16[4,144,1152]{2,1,0:T(8,128)(2,1)}, u32[]{:S(2)}, u32[]{:S(2)}) collective-permute-start(bf16[4,144,1152]{2,1,0:T(8,128)(2,1)} %collective-permute-done.37.rest_0_), channel_id=1, source_target_pairs={{0,4},{4,0},{1,5},{5,1},{2,6},{6,2},{3,7},{7,3},{8,12},{12,8},{9,1... | collective-permute-start | bytes 3981320 | tf_op jit(solution)/shard_map/ppermute | solution.py:741
  350.5 45.0 %collective-permute-start.46 = (bf16[2,576,1152]{2,1,0:T(8,128)(2,1)}, bf16[2,576,1152]{2,1,0:T(8,128)(2,1)}, u32[]{:S(2)}, u32[]{:S(2)}) collective-permute-start(bf16[2,576,1152]{2,1,0:T(8,128)(2,1)} %get-tuple-element.139), channel_id=1, source_target_pairs={{0,4},{4,0},{1,5},{5,1},{2,6},{6,2},{3,7},{7,3},{8,12},{12,8},{9,1... | collective-permute-start | bytes 7962632 | tf_op jit(solution)/shard_map/ppermute | solution.py:741
  351.5 43.9 %collective-permute-start.39 = (bf16[4,144,1152]{2,1,0:T(8,128)(2,1)}, bf16[4,144,1152]{2,1,0:T(8,128)(2,1)}, u32[]{:S(2)}, u32[]{:S(2)}) collective-permute-start(bf16[4,144,1152]{2,1,0:T(8,128)(2,1)} %collective-permute-done.37.rest_0_), channel_id=1, source_target_pairs={{0,8},{8,16},{16,24},{24,0},{1,9},{9,17},{17,25},{25,1},{2,10},{10... | collective-permute-start | bytes 3981320 | tf_op jit(solution)/shard_map/ppermute | solution.py:750
  351.9 56.1 %collective-permute-start.41 = (bf16[4,144,1152]{2,1,0:T(8,128)(2,1)}, bf16[4,144,1152]{2,1,0:T(8,128)(2,1)}, u32[]{:S(2)}, u32[]{:S(2)}) collective-permute-start(bf16[4,144,1152]{2,1,0:T(8,128)(2,1)} %collective-permute-done.38.rest_2_), channel_id=1, source_target_pairs={{0,4},{4,0},{1,5},{5,1},{2,6},{6,2},{3,7},{7,3},{8,12},{12,8},{9,1... | collective-permute-start | bytes 3981320 | tf_op jit(solution)/shard_map/ppermute | solution.py:741
  358.3 45.4 %all-to-all-start.5 = ((bf16[4,144,1152]{2,1,0:T(8,128)(2,1)}), bf16[4,144,1152]{2,1,0:T(8,128)(2,1)}, u32[]{:S(2)}, u32[]{:S(2)}) async-start(bf16[4,144,1152]{2,1,0:T(8,128)(2,1)} %bitcast.35.rest_4_), calls=%async_computation.5 | async-start | bytes 2654208 | tf_op jit(solution)/shard_map/all_to_all | solution.py:772
  394.6 48.4 %collective-permute-start.50 = (bf16[2,576,1152]{2,1,0:T(8,128)(2,1)}, bf16[2,576,1152]{2,1,0:T(8,128)(2,1)}, u32[]{:S(2)}, u32[]{:S(2)}) collective-permute-start(bf16[2,576,1152]{2,1,0:T(8,128)(2,1)} %get-tuple-element.150), channel_id=1, source_target_pairs={{0,4},{4,0},{1,5},{5,1},{2,6},{6,2},{3,7},{7,3},{8,12},{12,8},{9,1... | collective-permute-start | bytes 7962632 | tf_op jit(solution)/shard_map/ppermute | solution.py:741
  400.4 46.2 %collective-permute-start.51 = (bf16[4,144,1152]{2,1,0:T(8,128)(2,1)}, bf16[4,144,1152]{2,1,0:T(8,128)(2,1)}, u32[]{:S(2)}, u32[]{:S(2)}) collective-permute-start(bf16[4,144,1152]{2,1,0:T(8,128)(2,1)} %bitcast.34.rest_5_), channel_id=1, source_target_pairs={{0,8},{8,16},{16,24},{24,0},{1,9},{9,17},{17,25},{25,1},{2,10},{10... | collective-permute-start | bytes 3981320 | tf_op jit(solution)/shard_map/ppermute | solution.py:750
  403.7 46.6 %all-to-all-start.6 = ((bf16[4,144,1152]{2,1,0:T(8,128)(2,1)}), bf16[4,144,1152]{2,1,0:T(8,128)(2,1)}, u32[]{:S(2)}, u32[]{:S(2)}) async-start(bf16[4,144,1152]{2,1,0:T(8,128)(2,1)} %bitcast.33.rest_4_), calls=%async_computation.6 | async-start | bytes 2654208 | tf_op jit(solution)/shard_map/all_to_all | solution.py:772
  440.1 42.8 %collective-permute-start.52 = (bf16[2,576,1152]{2,1,0:T(8,128)(2,1)}, bf16[2,576,1152]{2,1,0:T(8,128)(2,1)}, u32[]{:S(2)}, u32[]{:S(2)}) collective-permute-start(bf16[2,576,1152]{2,1,0:T(8,128)(2,1)} %get-tuple-element.159), channel_id=1, source_target_pairs={{0,4},{4,0},{1,5},{5,1},{2,6},{6,2},{3,7},{7,3},{8,12},{12,8},{9,1... | collective-permute-start | bytes 7962632 | tf_op jit(solution)/shard_map/ppermute | solution.py:741
  449.4 37.1 %collective-permute-start.53 = (bf16[4,144,1152]{2,1,0:T(8,128)(2,1)}, bf16[4,144,1152]{2,1,0:T(8,128)(2,1)}, u32[]{:S(2)}, u32[]{:S(2)}) collective-permute-start(bf16[4,144,1152]{2,1,0:T(8,128)(2,1)} %add_convert_fusion.7.rest_1_), channel_id=1, source_target_pairs={{0,8},{8,16},{16,24},{24,0},{1,9},{9,17},{17,25},{25,1},{2,10},{10... | collective-permute-start | bytes 3981320 | tf_op jit(solution)/shard_map/ppermute | solution.py:750
  450.3 38.9 %all-to-all-start.7 = ((bf16[4,144,1152]{2,1,0:T(8,128)(2,1)}), bf16[4,144,1152]{2,1,0:T(8,128)(2,1)}, u32[]{:S(2)}, u32[]{:S(2)}) async-start(bf16[4,144,1152]{2,1,0:T(8,128)(2,1)} %bitcast.38.rest_0_), calls=%async_computation.7 | async-start | bytes 2654208 | tf_op jit(solution)/shard_map/all_to_all | solution.py:772
  489.2 78.2 %collective-permute-start.55 = (bf16[4,144,1152]{2,1,0:T(8,128)(2,1)}, bf16[4,144,1152]{2,1,0:T(8,128)(2,1)}, u32[]{:S(2)}, u32[]{:S(2)}) collective-permute-start(bf16[4,144,1152]{2,1,0:T(8,128)(2,1)} %add_convert_fusion.6.rest_1_), channel_id=1, source_target_pairs={{0,8},{8,16},{16,24},{24,0},{1,9},{9,17},{17,25},{25,1},{2,10},{10... | collective-permute-start | bytes 3981320 | tf_op jit(solution)/shard_map/ppermute | solution.py:750
  517.5 52.8 %collective-permute-start.59 = (bf16[592,1152]{1,0:T(8,128)(2,1)}, bf16[592,1152]{1,0:T(8,128)(2,1)S(1)}, u32[]{:S(2)}, u32[]{:S(2)}) collective-permute-start(bf16[592,1152]{1,0:T(8,128)(2,1)} %get-tuple-element.184), channel_id=1, source_target_pairs={{0,4},{4,0},{1,5},{5,1},{2,6},{6,2},{3,7},{7,3},{8,12},{12,8},{9,1... | collective-permute-start | bytes 4091912 | tf_op jit(solution)/shard_map/ppermute | solution.py:741
  519.8 51.9 %collective-permute-start.56 = (bf16[2,128,1152]{2,1,0:T(8,128)(2,1)}, bf16[2,128,1152]{2,1,0:T(8,128)(2,1)}, u32[]{:S(2)}, u32[]{:S(2)}) collective-permute-start(bf16[2,128,1152]{2,1,0:T(8,128)(2,1)} %get-tuple-element.281), channel_id=1, source_target_pairs={{0,1},{1,0},{2,3},{3,2},{4,5},{5,4},{6,7},{7,6},{8,9},{9,8},{10,11... | collective-permute-start | bytes 1769480 | tf_op jit(solution)/shard_map/ppermute | solution.py:744
  521.5 50.2 %collective-permute-start.57 = (bf16[2,128,1152]{2,1,0:T(8,128)(2,1)}, bf16[2,128,1152]{2,1,0:T(8,128)(2,1)}, u32[]{:S(2)}, u32[]{:S(2)}) collective-permute-start(bf16[2,128,1152]{2,1,0:T(8,128)(2,1)} %get-tuple-element.280), channel_id=1, source_target_pairs={{0,2},{1,3},{2,0},{3,1},{4,6},{5,7},{6,4},{7,5},{8,10},{9,11},{10,... | collective-permute-start | bytes 1769480 | tf_op jit(solution)/shard_map/ppermute | solution.py:744
  522.7 49.0 %collective-permute-start.58 = (bf16[2,128,1152]{2,1,0:T(8,128)(2,1)}, bf16[2,128,1152]{2,1,0:T(8,128)(2,1)}, u32[]{:S(2)}, u32[]{:S(2)}) collective-permute-start(bf16[2,128,1152]{2,1,0:T(8,128)(2,1)} %get-tuple-element.279), channel_id=1, source_target_pairs={{0,3},{1,2},{2,1},{3,0},{4,7},{5,6},{6,5},{7,4},{8,11},{9,10},{10,... | collective-permute-start | bytes 1769480 | tf_op jit(solution)/shard_map/ppermute | solution.py:744
  555.7 40.3 %all-to-all-start.10 = ((bf16[32,37,144]{2,1,0:T(8,128)(2,1)}), bf16[32,37,144]{2,1,0:T(8,128)(2,1)S(1)}, u32[]{:S(2)}, u32[]{:S(2)}) async-start(bf16[32,37,144]{2,1,0:T(8,128)(2,1)} %pad_maximum_fusion), calls=%async_computation.10 | async-start | bytes 1310720 | tf_op jit(solution)/shard_map/all_to_all | solution.py:753
  567.4 50.3 %collective-permute-start.54 = (bf16[592,1152]{1,0:T(8,128)(2,1)}, bf16[592,1152]{1,0:T(8,128)(2,1)}, u32[]{:S(2)}, u32[]{:S(2)}) collective-permute-start(bf16[592,1152]{1,0:T(8,128)(2,1)} %get-tuple-element.179), channel_id=1, source_target_pairs={{0,4},{4,0},{1,5},{5,1},{2,6},{6,2},{3,7},{7,3},{8,12},{12,8},{9,1... | collective-permute-start | bytes 4091912 | tf_op jit(solution)/shard_map/ppermute | solution.py:741
  604.6 46.1 %collective-permute-start.61 = (bf16[288,576]{1,0:T(8,128)(2,1)}, bf16[288,576]{1,0:T(8,128)(2,1)}, u32[]{:S(2)}, u32[]{:S(2)}) collective-permute-start(bf16[288,576]{1,0:T(8,128)(2,1)} %get-tuple-element.286), channel_id=1, source_target_pairs={{0,8},{8,0},{16,24},{24,16},{1,9},{9,1},{17,25},{25,17},{2,10},{10... | collective-permute-start | bytes 995336 | tf_op jit(solution)/shard_map/ppermute | solution.py:747
  605.8 44.9 %collective-permute-start.62 = (bf16[288,576]{1,0:T(8,128)(2,1)}, bf16[288,576]{1,0:T(8,128)(2,1)}, u32[]{:S(2)}, u32[]{:S(2)}) collective-permute-start(bf16[288,576]{1,0:T(8,128)(2,1)} %get-tuple-element.285), channel_id=1, source_target_pairs={{0,16},{8,24},{16,0},{24,8},{1,17},{9,25},{17,1},{25,9},{2,18},{10... | collective-permute-start | bytes 995336 | tf_op jit(solution)/shard_map/ppermute | solution.py:747
  608.0 42.6 %collective-permute-start.63 = (bf16[288,576]{1,0:T(8,128)(2,1)S(1)}, bf16[288,576]{1,0:T(8,128)(2,1)}, u32[]{:S(2)}, u32[]{:S(2)}) collective-permute-start(bf16[288,576]{1,0:T(8,128)(2,1)S(1)} %get-tuple-element.284), channel_id=1, source_target_pairs={{0,24},{8,16},{16,8},{24,0},{1,25},{9,17},{17,9},{25,1},{2,26},{10... | collective-permute-start | bytes 995336 | tf_op jit(solution)/shard_map/ppermute | solution.py:747
  617.7 97.7 %collective-permute-start.67 = (bf16[592,1152]{1,0:T(8,128)(2,1)}, bf16[592,1152]{1,0:T(8,128)(2,1)}, u32[]{:S(2)}, u32[]{:S(2)}) collective-permute-start(bf16[592,1152]{1,0:T(8,128)(2,1)} %add_convert_fusion.3.rest_6_), channel_id=1, source_target_pairs={{0,3},{1,2},{2,1},{3,0},{4,7},{5,6},{6,5},{7,4},{8,11},{9,10},{10,... | collective-permute-start | bytes 4091912 | tf_op jit(solution)/shard_map/ppermute | solution.py:744
  649.2 63.5 %collective-permute-start.70 = (bf16[592,1152]{1,0:T(8,128)(2,1)}, bf16[592,1152]{1,0:T(8,128)(2,1)}, u32[]{:S(2)}, u32[]{:S(2)}) collective-permute-start(bf16[592,1152]{1,0:T(8,128)(2,1)} %get-tuple-element.196), channel_id=1, source_target_pairs={{0,4},{4,0},{1,5},{5,1},{2,6},{6,2},{3,7},{7,3},{8,12},{12,8},{9,1... | collective-permute-start | bytes 4091912 | tf_op jit(solution)/shard_map/ppermute | solution.py:741
  691.2 41.9 %collective-permute-start.68 = (bf16[592,1152]{1,0:T(8,128)(2,1)}, bf16[592,1152]{1,0:T(8,128)(2,1)S(1)}, u32[]{:S(2)}, u32[]{:S(2)}) collective-permute-start(bf16[592,1152]{1,0:T(8,128)(2,1)} %add_convert_fusion.4.rest_1_), channel_id=1, source_target_pairs={{0,1},{1,0},{2,3},{3,2},{4,5},{5,4},{6,7},{7,6},{8,9},{9,8},{10,11... | collective-permute-start | bytes 4091912 | tf_op jit(solution)/shard_map/ppermute | solution.py:744
  692.6 40.6 %collective-permute-start.69 = (bf16[592,1152]{1,0:T(8,128)(2,1)}, bf16[592,1152]{1,0:T(8,128)(2,1)}, u32[]{:S(2)}, u32[]{:S(2)}) collective-permute-start(bf16[592,1152]{1,0:T(8,128)(2,1)} %add_convert_fusion.2.rest_2_.rest_4_), channel_id=1, source_target_pairs={{0,2},{1,3},{2,0},{3,1},{4,6},{5,7},{6,4},{7,5},{8,10},{9,11},{10,... | collective-permute-start | bytes 4091912 | tf_op jit(solution)/shard_map/ppermute | solution.py:744
  (114 other events, 2324.3 us)

commit v3 on v2

--- a/solution.py
+++ b/solution.py
@@ -16,6 +16,7 @@
 F32 = jnp.float32
 VMEM = 58 * 1024 * 1024
 ANY = pl.BlockSpec(memory_space=pl.ANY)
+SMEM = pl.BlockSpec(memory_space=pltpu.SMEM)
 EVERY = ("z", "core", "seq")
 DENSE = ("core", "seq")
 
@@ -151,24 +152,28 @@
     )(z_at, *got)
 
 
-def join_kernel(n_z, at_ref, *refs):
-    got, (out, held) = refs[:n_z], refs[n_z:]
+def turn_w_kernel(n_z, at_ref, *refs):
+    got, out_got = refs[:n_z], refs[n_z : 2 * n_z]
+    w_out, held, out_held = refs[2 * n_z :]
     for k in range(n_z):
         held[at_ref[0] ^ k] = got[k][...]
-    out[...] = jnp.concatenate([held[z].astype(F32) for z in range(n_z)], 0).astype(BF)
-
-
-def join(z_at, got):
+        out_held[at_ref[0] ^ k] = out_got[k][...]
+    columns_part = jnp.concatenate([held[z].astype(F32).T for z in range(n_z)], 1)
+    rows = [out_held[z].astype(F32) for z in range(n_z)]
+    w_out[...] = jnp.concatenate([columns_part] + rows, 0).astype(BF)
+
+
+def turn_w(z_at, got, out_got):
     n_z = len(got)
-    rows, model = got[0].shape
-    return pl.pallas_call(
-        functools.partial(join_kernel, n_z),
-        in_specs=[pl.BlockSpec(memory_space=pltpu.SMEM)] + [pl.BlockSpec(memory_space=pltpu.VMEM)] * n_z,
-        out_shape=shape((n_z * rows, model), BF),
-        scratch_shapes=[pltpu.VMEM((n_z, rows, model), BF)],
+    rows, lanes = got[0].shape
+    return pl.pallas_call(
+        functools.partial(turn_w_kernel, n_z),
+        in_specs=[SMEM] + [pl.BlockSpec(memory_space=pltpu.VMEM)] * (2 * n_z),
+        out_shape=shape((lanes + n_z * out_got[0].shape[0], rows * n_z), BF),
+        scratch_shapes=[pltpu.VMEM((n_z, rows, lanes), BF), pltpu.VMEM((n_z,) + out_got[0].shape, BF)],
         compiler_params=params(),
         cost_estimate=cost(3),
-    )(z_at, *got)
+    )(z_at, *got, *out_got)
 
 
 def split_kernel(n_z, width, n_in, *refs):
@@ -319,7 +324,7 @@
     scale = head_size ** (-0.5)
     part = q_out.shape[1:]
     for n, w_ref in enumerate((w_a, w_b)):
-        qkv = dot_nt(h, w_ref[...])
+        qkv = dot_nt(h, w_ref[: 3 * width])
         q = (qkv[:, :width] + qb_ref[n]).astype(BF)
         k = qkv[:, width : 2 * width].astype(BF)
         v = (qkv[:, 2 * width :] + vb_ref[n]).astype(BF)
@@ -365,7 +370,7 @@
     )(hidden, w_a, w_b, query_bias, value_bias, seg_col, seg_row, *wait)
 
 
-def attn_bwd_kernel(head_size, first, n_wait, h_ref, gb_ref, w_a, w_b, o_a, o_b, q_ref, k_ref, v_ref, att_ref, lse_ref,
+def attn_bwd_kernel(head_size, first, n_wait, h_ref, gb_ref, w_a, w_b, q_ref, k_ref, v_ref, att_ref, lse_ref,
                     bias_ref, segc_ref, segr_ref, *rest):
     g_a, g_b, gh_out, sum_qkv, sum_out, sum_bias = rest[-6:]
     gh_in = None if first else rest[n_wait]
@@ -378,8 +383,8 @@
     allowed = segc_ref[0] == segr_ref[0]
     scale = head_size ** (-0.5)
     total = None
-    for n, (w_ref, o_ref) in enumerate(((w_a, o_a), (w_b, o_b))):
-        grad_att = dot_nt(gb, o_ref[...]).astype(BF)
+    for n, w_ref in enumerate((w_a, w_b)):
+        grad_att = dot_nt(gb, w_ref[3 * width :]).astype(BF)
         q = q_ref[n].reshape(length, width)
         k = k_ref[n].reshape(length, width)
         v = v_ref[n].reshape(length, width)
@@ -396,7 +401,7 @@
             gk.append(dot_nn(grad_score, q[:, cut]) * scale)
             gv.append(dot_nn(prob.astype(BF), grad_att[:, cut]))
         grad_qkv = jnp.concatenate(gq + gk + gv, -1).astype(BF)
-        term = dot_nn(grad_qkv, w_ref[...])
+        term = dot_nn(grad_qkv, w_ref[: 3 * width])
         total = term if total is None else total + term
         term_qkv = dot_tn(grad_qkv, h)
         term_out = dot_tn(att, gb)
@@ -431,7 +436,7 @@
             g_ref[4 * width :] = jnp.broadcast_to(biases, (16, model)).astype(BF)
 
 
-def attn_bwd(hidden, grad_branch, w_a, w_b, o_a, o_b, saved, bias, seg_col, seg_row, head_size, grad_hidden, wait):
+def attn_bwd(hidden, grad_branch, w_a, w_b, saved, bias, seg_col, seg_row, head_size, grad_hidden, wait):
     q, k, v, att, lse = saved
     n_seq, rows, kept_count, model = hidden.shape
     width = q.shape[-1]
@@ -441,14 +446,13 @@
     token = pl.BlockSpec((n_seq, 1, kept_count, model), lambda r: (0, r, 0, 0))
     part = pl.BlockSpec((2, n_seq, 1, kept_count, width), lambda r: (0, 0, r, 0, 0))
     weight = pl.BlockSpec(w_a.shape, lambda r: (0, 0))
-    out_weight = pl.BlockSpec(o_a.shape, lambda r: (0, 0))
     out = pl.BlockSpec((4 * width + 16, model), lambda r: (0, 0))
     own = [] if first else [grad_hidden]
     return pl.pallas_call(
         functools.partial(attn_bwd_kernel, head_size, first, len(wait)),
         grid=(rows,),
         in_specs=[
-            token, token, weight, weight, out_weight, out_weight, part, part, part, part,
+            token, token, weight, weight, part, part, part, part,
             pl.BlockSpec((2, 1, heads, length), lambda r: (0, r, 0, 0)),
             pl.BlockSpec((2, 1, 2 * width), lambda r: (0, 0, 0)),
             pl.BlockSpec((1, length, 1), lambda r: (r, 0, 0)),
@@ -457,100 +461,140 @@
         + [ANY] * len(wait)
         + [token] * len(own),
         out_specs=[out, out, token],
-        out_shape=[shape((4 * width + 16, model), BF)] * 2 + [shape(hidden.shape, F32)],
         scratch_shapes=[
             pltpu.VMEM((2, 3 * width, model), F32),
             pltpu.VMEM((2, width, model), F32),
             pltpu.VMEM((2, 1, 3 * width), F32),
         ],
-        input_output_aliases={} if first else {14 + len(wait): 2},
+        out_shape=[shape((4 * width + 16, model), BF)] * 2 + [shape(hidden.shape, F32)],
+        input_output_aliases={} if first else {12 + len(wait): 2},
         compiler_params=params(),
         cost_estimate=cost(24),
-    )(hidden, grad_branch, w_a, w_b, o_a, o_b, q, k, v, att, lse, bias, seg_col, seg_row, *wait, *own)
-
-
-def pick_slot(table_ref, seg, index):
-    value = table_ref[0, 0, index : index + 1, :]
-    for slot in range(1, table_ref.shape[1]):
-        value = jnp.where(seg == slot, table_ref[0, slot, index : index + 1, :], value)
-    return value
-
-
-def add_slots(out_ref, index, seg, value, start):
-    for slot in range(out_ref.shape[1]):
-        part = jnp.sum(jnp.where(seg == slot, value, 0.0), 0, keepdims=True)
-        at = (0, slot, slice(index, index + 1))
-        out_ref[at] = jnp.where(start, 0.0, out_ref[at]) + part
-
-
-def after_attn_kernel(n_blocks, width, x_ref, seg_ref, table_ref, ob_ref, *rest):
-    att_refs = rest[: n_blocks // 2]
-    w_refs = rest[n_blocks // 2 : n_blocks // 2 + n_blocks]
+    )(hidden, grad_branch, w_a, w_b, q, k, v, att, lse, bias, seg_col, seg_row, *wait, *own)
+
+
+def pick_slot(table_ref, ends, seg, index):
+    first, last = ends
+    low = table_ref[0, first, index : index + 1, :]
+    return jnp.where(seg == last, table_ref[0, last, index : index + 1, :], low)
+
+
+def add_slots(out_ref, ends, seg, values, start):
+    first, last = ends
+
+    @pl.when(start)
+    def _():
+        out_ref[...] = jnp.zeros_like(out_ref)
+
+    @pl.when(first == last)
+    def _():
+        for index, value in enumerate(values):
+            out_ref[0, first, index : index + 1] += jnp.sum(value, 0, keepdims=True)
+
+    @pl.when(first != last)
+    def _():
+        for index, value in enumerate(values):
+            out_ref[0, first, index : index + 1] += jnp.sum(jnp.where(seg == first, value, 0.0), 0, keepdims=True)
+            out_ref[0, last, index : index + 1] += jnp.sum(jnp.where(seg == last, value, 0.0), 0, keepdims=True)
+
+
+def ends_of(ends_ref):
+    row, part = pl.program_id(0), pl.program_id(1)
+    return ends_ref[0, part, row], ends_ref[1, part, row]
+
+
+def before_attn_kernel(ends_ref, x_ref, seg_ref, table_ref, out_ref):
+    ends, seg = ends_of(ends_ref), seg_ref[0, 0]
+    normed, _ = normalize(x_ref[0, 0].astype(F32))
+    out_ref[0, 0] = (normed * (1.0 + pick_slot(table_ref, ends, seg, 1)) + pick_slot(table_ref, ends, seg, 0)).astype(BF)
+
+
+def before_attn(ends, inputs, seg, table):
+    n_seq, rows, kept_count, model = inputs.shape
+    slots = table.shape[1]
+    token = pl.BlockSpec((1, 1, kept_count, model), lambda r, j: (j, r, 0, 0))
+    return pl.pallas_call(
+        before_attn_kernel,
+        grid=(rows, n_seq),
+        in_specs=[
+            SMEM, token,
+            pl.BlockSpec((1, 1, kept_count, 1), lambda r, j: (j, r, 0, 0)),
+            pl.BlockSpec((1, slots, 6, model), lambda r, j: (r, 0, 0, 0)),
+        ],
+        out_specs=token,
+        out_shape=shape(inputs.shape, BF),
+        compiler_params=params(),
+        cost_estimate=cost(5),
+    )(ends, inputs, seg, table)
+
+
+def after_attn_kernel(n_seq, width, out_at, ends_ref, x_ref, seg_ref, table_ref, ob_ref, *rest):
+    att_refs, w_refs = rest[:n_seq], rest[n_seq : 3 * n_seq]
     br_out, mid_out, h2_out = rest[-3:]
     kept_count, model = x_ref.shape[2:]
-    seg = seg_ref[0, 0]
+    ends, seg = ends_of(ends_ref), seg_ref[0, 0]
     branch = ob_ref[...]
-    for j in range(n_blocks // 2):
+    for j in range(n_seq):
         for n in range(2):
-            w = w_refs[j + n * (n_blocks // 2)][...]
+            w = w_refs[j + n * n_seq][pl.ds(out_at, width)]
             branch = branch + dot_nn(att_refs[j][n].reshape(kept_count, width), w)
-    mid = x_ref[0, 0].astype(F32) + pick_slot(table_ref, seg, 2) * branch
+    mid = x_ref[0, 0].astype(F32) + pick_slot(table_ref, ends, seg, 2) * branch
     normed, _ = normalize(mid)
     br_out[0, 0] = branch
     mid_out[0, 0] = mid
-    h2_out[0, 0] = (normed * (1.0 + pick_slot(table_ref, seg, 4)) + pick_slot(table_ref, seg, 3)).astype(BF)
-
-
-def after_attn(inputs, seg, table, out_bias, atts, weights, wait):
+    h2_out[0, 0] = (normed * (1.0 + pick_slot(table_ref, ends, seg, 4)) + pick_slot(table_ref, ends, seg, 3)).astype(BF)
+
+
+def after_attn(ends, inputs, seg, table, out_bias, weights, atts):
     n_seq, rows, kept_count, model = inputs.shape
     width = atts[0].shape[-1]
     slots = table.shape[1]
     token = pl.BlockSpec((1, 1, kept_count, model), lambda r, j: (j, r, 0, 0))
     part = pl.BlockSpec((2, 1, 1, kept_count, width), lambda r, j: (0, j, r, 0, 0))
-    weight = pl.BlockSpec((width, model), lambda r, j: (0, 0))
-    return pl.pallas_call(
-        functools.partial(after_attn_kernel, len(weights), width),
+    if width % 16 == 0:
+        weight, out_at = pl.BlockSpec((width, model), lambda r, j: (3, 0)), 0
+    else:
+        weight, out_at = pl.BlockSpec((4 * width, model), lambda r, j: (0, 0)), 3 * width
+    return pl.pallas_call(
+        functools.partial(after_attn_kernel, n_seq, width, out_at),
         grid=(rows, n_seq),
         in_specs=[
-            token,
+            SMEM, token,
             pl.BlockSpec((1, 1, kept_count, 1), lambda r, j: (j, r, 0, 0)),
             pl.BlockSpec((1, slots, 6, model), lambda r, j: (r, 0, 0, 0)),
             pl.BlockSpec((1, model), lambda r, j: (0, 0)),
         ]
         + [part] * len(atts)
-        + [weight] * len(weights)
-        + [ANY] * len(wait),
+        + [weight] * len(weights),
         out_specs=[token] * 3,
         out_shape=[shape(inputs.shape, F32), shape(inputs.shape, F32), shape(inputs.shape, BF)],
         compiler_params=params(),
-        cost_estimate=cost(15),
-    )(inputs, seg, table, out_bias, *atts, *weights, *wait)
-
-
-def after_mlp_kernel(mid_ref, mlp_ref, gh_ref, br_ref, ct_ref, seg_ref, table_ref, db_ref, *rest):
+        cost_estimate=cost(11),
+    )(ends, inputs, seg, table, out_bias, *atts, *weights)
+
+
+def after_mlp_kernel(ends_ref, mid_ref, mlp_ref, gh_ref, br_ref, ct_ref, seg_ref, table_ref, db_ref, *rest):
     res_out, gm_out, gb_out, sums_out, obias_out = rest[-5:]
-    seg = seg_ref[0, 0]
+    ends, seg = ends_of(ends_ref), seg_ref[0, 0]
     step = pl.program_id(1)
     mid = mid_ref[0, 0]
     branch_mlp = mlp_ref[0, 0] + db_ref[...]
     grad_hidden = gh_ref[0, 0]
     grad_result = ct_ref[0, 0].astype(F32)
-    res_out[0, 0] = (mid + pick_slot(table_ref, seg, 5) * branch_mlp).astype(BF)
+    res_out[0, 0] = (mid + pick_slot(table_ref, ends, seg, 5) * branch_mlp).astype(BF)
     normed, inv = normalize(mid)
-    grad_mid = grad_result + norm_back(grad_hidden * (1.0 + pick_slot(table_ref, seg, 4)), normed, inv)
+    grad_mid = grad_result + norm_back(grad_hidden * (1.0 + pick_slot(table_ref, ends, seg, 4)), normed, inv)
     gm_out[0, 0] = grad_mid
-    grad_branch = (grad_mid * pick_slot(table_ref, seg, 2)).astype(BF)
+    grad_branch = (grad_mid * pick_slot(table_ref, ends, seg, 2)).astype(BF)
     gb_out[0, 0] = grad_branch
-    add_slots(sums_out, 0, seg, grad_mid * br_ref[0, 0], step == 0)
-    add_slots(sums_out, 1, seg, grad_hidden, step == 0)
-    add_slots(sums_out, 2, seg, grad_hidden * normed, step == 0)
-    add_slots(sums_out, 3, seg, grad_result * branch_mlp, step == 0)
+    values = [grad_mid * br_ref[0, 0], grad_hidden, grad_hidden * normed, grad_result * branch_mlp]
+    add_slots(sums_out, ends, seg, values, step == 0)
     start = jnp.logical_and(step == 0, pl.program_id(0) == 0)
     part = jnp.sum(grad_branch.astype(F32), 0, keepdims=True)
     obias_out[...] = jnp.where(start, 0.0, obias_out[...]) + part
 
 
-def after_mlp(mid, mlp, grad_hidden, branch, cotangent, seg, table, down_bias, wait):
+def after_mlp(ends, mid, mlp, grad_hidden, branch, cotangent, seg, table, down_bias, wait):
     n_seq, rows, kept_count, model = mid.shape
     slots = table.shape[1]
     token = pl.BlockSpec((1, 1, kept_count, model), lambda r, j: (j, r, 0, 0))
@@ -559,7 +603,7 @@
         after_mlp_kernel,
         grid=(rows, n_seq),
         in_specs=[
-            token, token, token, token, token,
+            SMEM, token, token, token, token, token,
             pl.BlockSpec((1, 1, kept_count, 1), lambda r, j: (j, r, 0, 0)),
             pl.BlockSpec((1, slots, 6, model), lambda r, j: (r, 0, 0, 0)),
             vector,
@@ -575,23 +619,21 @@
             shape((rows, slots, 4, model), F32), shape((1, model), F32),
         ],
         compiler_params=params(),
-        cost_estimate=cost(21),
-    )(mid, mlp, grad_hidden, branch, cotangent, seg, table, down_bias, *wait)
-
-
-def last_kernel(x_ref, gh_ref, gm_ref, seg_ref, table_ref, *rest):
+        cost_estimate=cost(13),
+    )(ends, mid, mlp, grad_hidden, branch, cotangent, seg, table, down_bias, *wait)
+
+
+def last_kernel(ends_ref, x_ref, gh_ref, gm_ref, seg_ref, table_ref, *rest):
     gx_out, sums_out = rest[-2:]
-    seg = seg_ref[0, 0]
-    step = pl.program_id(1)
+    ends, seg = ends_of(ends_ref), seg_ref[0, 0]
     grad_hidden = gh_ref[0, 0]
     normed, inv = normalize(x_ref[0, 0].astype(F32))
-    back = norm_back(grad_hidden * (1.0 + pick_slot(table_ref, seg, 1)), normed, inv)
+    back = norm_back(grad_hidden * (1.0 + pick_slot(table_ref, ends, seg, 1)), normed, inv)
     gx_out[0, 0] = (gm_ref[0, 0] + back).astype(BF)
-    add_slots(sums_out, 0, seg, grad_hidden, step == 0)
-    add_slots(sums_out, 1, seg, grad_hidden * normed, step == 0)
-
-
-def last_step(inputs, grad_hidden, grad_mid, seg, table, wait):
+    add_slots(sums_out, ends, seg, [grad_hidden, grad_hidden * normed], pl.program_id(1) == 0)
+
+
+def last_step(ends, inputs, grad_hidden, grad_mid, seg, table, wait):
     n_seq, rows, kept_count, model = inputs.shape
     slots = table.shape[1]
     token = pl.BlockSpec((1, 1, kept_count, model), lambda r, j: (j, r, 0, 0))
@@ -599,7 +641,7 @@
         last_kernel,
         grid=(rows, n_seq),
         in_specs=[
-            token, token, token,
+            SMEM, token, token, token,
             pl.BlockSpec((1, 1, kept_count, 1), lambda r, j: (j, r, 0, 0)),
             pl.BlockSpec((1, slots, 6, model), lambda r, j: (r, 0, 0, 0)),
         ]
@@ -607,8 +649,8 @@
         out_specs=[token, pl.BlockSpec((1, slots, 2, model), lambda r, j: (r, 0, 0, 0))],
         out_shape=[shape(inputs.shape, BF), shape((rows, slots, 2, model), F32)],
         compiler_params=params(),
-        cost_estimate=cost(12),
-    )(inputs, grad_hidden, grad_mid, seg, table, *wait)
+        cost_estimate=cost(8),
+    )(ends, inputs, grad_hidden, grad_mid, seg, table, *wait)
 
 
 def mlp_kernel(n_up, n_down, first, n_wait, h_ref, gm_ref, ub_ref, *rest):
@@ -672,7 +714,7 @@
 
 def mlp_step(hidden, grad_mlp, up_bias, ups, downs, sums, wait):
     count, model = hidden.shape
-    chunk = min(512, count)
+    chunk = min(1024, count)
     width = sum(u.shape[0] * u.shape[1] for u in ups)
     first = sums is None
     own = [] if first else list(sums)
@@ -784,7 +826,13 @@
         n_z, blocks, qkv_weight, mod_weight, up_weight, (mod_bias, query_bias, value_bias, out_bias, up_bias, down_bias)
     )
     first_got = dense_to_all(first_cols)
+    spread_out = []
+    for d in range(devices):
+        z, c, s = d % n_z, (d // n_z) // n_seq, (d // n_z) % n_seq
+        spread_out.append((d, (z * 2 + c) * n_seq + s))
     down_got = plane(tie(down_weight, first_cols))
+    out_part = lax.ppermute(tie(out_weight, first_cols), EVERY, spread_out)
+    out_got = [out_part] + [over_z(out_part, k) for k in range(1, n_z)]
 
     places = jnp.arange(seq_tokens, dtype=jnp.int32)
     kept = tie(kept, first_cols)
@@ -822,12 +870,13 @@
     seg_rows = seg.transpose(1, 0, 2).reshape(rows, 1, n_seq * kept_count)
     seg_cols = seg_rows.reshape(rows, n_seq * kept_count, 1)
     seg_tokens = seg.reshape(n_seq, rows, kept_count, 1)
-
-    qkv_rows, z_cols = unpack(tie(first_got, *act_got[1:], *small_got[1:], *down_got[1:], picked), n_z, shard, mod_shard + ff_shard, mod_shard + ff_shard + 4 * shard)
+    ends = jnp.stack([seg[:, :, 0], seg[:, :, -1]])
+
+    qkv_rows, z_cols = unpack(tie(first_got, *act_got[1:], *small_got[1:], *out_got[1:], *down_got[1:], picked), n_z, shard, mod_shard + ff_shard, mod_shard + ff_shard + 4 * shard)
     qkv_got = [qkv_rows] + [over_z(qkv_rows, k) for k in range(1, n_z)]
-    (w_own,) = turn(z_scalar, qkv_got, blocks * shard, (0, 3 * width))
+    w_own = turn_w(z_scalar, qkv_got, out_got)
     z_got = to_z(tie(z_cols, *qkv_got[1:]))
-    mod_cols, up_part, bias_got = turn(z_scalar, z_got, blocks * shard, (0, mod_shard, mod_shard + ff_shard))
+    mod_cols, up_part, bias_got = turn(tie(z_scalar, w_own), z_got, blocks * shard, (0, mod_shard, mod_shard + ff_shard))
     bias_got = bias_got.astype(F32)
     mod_b = bias_got[:, :blocks, :mod_shard].reshape(-1)
     up_b = bias_got[:, :blocks, mod_shard:].reshape(-1)
@@ -845,22 +894,14 @@
             value = jnp.where(seg_tokens == slot, table[None, :, None, slot, index], value)
         return value
 
-    hidden_one = (normalize(inputs.astype(F32))[0] * (1.0 + token_mod(1)) + token_mod(0)).astype(BF)
-
-    spread_out = []
-    for d in range(devices):
-        z, c, s = d % n_z, (d // n_z) // n_seq, (d // n_z) % n_seq
-        spread_out.append((d, (z * 2 + c) * n_seq + s))
-    out_part = lax.ppermute(out_weight, EVERY, spread_out)
-    out_part = tie(out_part, *z_got[1:])
-    out_got = [out_part] + [over_z(out_part, k) for k in range(1, n_z)]
-    o_own = join(z_scalar, out_got)
+    hidden_one = before_attn(ends, inputs, seg_tokens, table)
+
     w_all = plane(w_own)
     w_all = w_all + [over_core(w) for w in w_all]
 
     down_ring = [place(seq_scalar, down_got)]
     up_ring = [gather_seq(tie(up_part, hidden_one))]
-    down_ring.append(shift_z(tie(down_ring[0], *out_got[1:]), 1))
+    down_ring.append(shift_z(tie(down_ring[0], *z_got[1:]), 1))
     for t in range(2, n_z):
         if t == 2:
             down_ring.append(shift_z(tie(down_ring[1], hidden_one), 1))
@@ -872,8 +913,6 @@
         up_ring.append(shift_z(up_ring[-1], 1))
     down_other = [over_core(value) for value in down_ring]
     up_other = [over_core(value) for value in up_ring]
-    o_all = plane(tie(o_own, hidden_one))
-    o_all = o_all + [over_core(o) for o in o_all]
 
     def by_block(value):
         return jnp.take(value.reshape(blocks, 1, width), relative, axis=0)
@@ -891,7 +930,7 @@
             hidden_one, w_all[j], w_all[j + n_seq], pair(query_b, j), pair(value_b, j), seg_cols, seg_rows, head_size, [],
         ))
     branch_attn, mid, hidden_two = after_attn(
-        inputs, seg_tokens, table, out_b.reshape(1, -1), [s[3] for s in saved], o_all, [],
+        ends, inputs, seg_tokens, table, out_b.reshape(1, -1), w_all, [s[3] for s in saved],
     )
     grad_result = to_rows(tie(picked_ct, up_ring[0]))
     grad_mlp = (grad_result.astype(F32) * token_mod(5)).astype(BF)
@@ -930,7 +969,7 @@
 
     last = n_z - 1
     res, grad_mid, grad_branch, sums_late, grad_out_bias = after_mlp(
-        mid, sums[0].reshape(mid.shape), sums[1].reshape(mid.shape), branch_attn, grad_result, seg_tokens, table,
+        ends, mid, sums[0].reshape(mid.shape), sums[1].reshape(mid.shape), branch_attn, grad_result, seg_tokens, table,
         down_b.reshape(1, -1), sends[last - 1] + [planes[last - 2]],
     )
 
@@ -945,7 +984,7 @@
     w_cores, w_values, w_planes = [], [], []
     for at, j in enumerate([n_seq - 1] + list(range(1, n_seq - 1)) + [0]):
         g_own, g_other, grad_hidden = attn_bwd(
-            hidden_one, grad_branch, w_all[j], w_all[j + n_seq], o_all[j], o_all[j + n_seq], saved[j],
+            hidden_one, grad_branch, w_all[j], w_all[j + n_seq], saved[j],
             pair(late_bias, j), seg_cols, seg_rows, head_size, grad_hidden, waits,
         )
         waits = []
@@ -979,7 +1018,7 @@
         if at == n_seq - 2:
             waits.append(w_values[at])
 
-    grad_x, sums_early = last_step(inputs, grad_hidden, grad_mid, seg_tokens, table, waits)
+    grad_x, sums_early = last_step(ends, inputs, grad_hidden, grad_mid, seg_tokens, table, waits)
     grad_mine = [lax.dynamic_index_in_dim(grad_x, seq_at ^ k, 0, keepdims=False) for k in range(n_seq)]
     grad_got = [grad_mine[0]] + [over_seq(grad_mine[k], k) for k in range(1, n_seq)]
 

time: 809 us -> 780 us (0.964)
  Pallas kernels: 358 us -> 345 us
  waiting for transfers between devices: 123 us -> 110 us
  other arithmetic: 61.2 us -> 52.1 us
    pallas_call x4, Pallas kernels: 126 us -> 115 us  [mlp_step(): pl.pallas_call(functools.partial(mlp_kernel, len(ups), len(downs), first,...]
    convert_element_type x1 -> x0, other arithmetic: 9.38 us -> none  [body(): (normalize(inputs.astype(F32))[0] * (1.0 + token_mod(1)) + token_mod(0))....]
    ppermute x25 -> x21, starting transfers between devices: 17.2 us -> 20.7 us  [over_core(): return lax.ppermute(value, 'core', [(0, 1), (1, 0)])]
    ppermute x21 -> x18, starting transfers between devices: 25.5 us -> 24.4 us  [over_seq(): return lax.ppermute(value, 'seq', [(i, i ^ by) for i in range(n_seq)])]
    ppermute x21 -> x18, waiting for transfers between devices: 17.8 us -> 17.5 us  [over_seq(): return lax.ppermute(value, 'seq', [(i, i ^ by) for i in range(n_seq)])]
    pallas_call x4 -> x5, Pallas kernels: 49.7 us -> 49.5 us  [the longest x1 16 us: after_mlp(): pl.pallas_call(after_mlp_kernel, grid=(rows, n_seq), in_specs=[SMEM, toke...]
  transfers between devices with their start and end apart: 93 -> 86, of which waited for: 16 -> 18; matrix products, arithmetic and copies ran while one was open for 15% -> 15% of each run, Pallas kernels for 44% -> 43%
where the time goes in v3:
time: 780 us; the launch traced here: 765 us
  Pallas kernels  345 us (44%)
  starting transfers between devices  179 us (23%)
  waiting for transfers between devices  110 us (14%)
  local copies, waits for them, and re-layouts  58.1 us (7%)
  other arithmetic  52.1 us (7%)
  matrix products  18.6 us (2%)
    pallas_call x4, Pallas kernels, mlp_step(): pl.pallas_call(functools.partial(mlp_kernel, len(ups), len(downs), first,...  115 us
    pallas_call x4, Pallas kernels, attn_bwd(): pl.pallas_call(functools.partial(attn_bwd_kernel, head_size, first, len(w...  96.7 us
    pallas_call x4, Pallas kernels, attn_fwd(): pl.pallas_call(functools.partial(attn_fwd_kernel, head_size), grid=(rows,...  47.9 us
    all_to_all x8, starting transfers between devices, seq_to_all(): return lax.all_to_all(value, 'seq', 0, 0, tiled=True)  34.5 us
    ppermute x21, waiting for transfers between devices, over_z(): return lax.ppermute(value, 'z', [(i, i ^ by) for i in range(n_z)])  32.4 us
    ppermute x21, starting transfers between devices, over_z(): return lax.ppermute(value, 'z', [(i, i ^ by) for i in range(n_z)])  31.8 us
    all_to_all x5, waiting for transfers between devices, all_to_all(): return lax.all_to_all(value, EVERY, 0, 0, tiled=True)  30.6 us
    all_to_all x5, starting transfers between devices, all_to_all(): return lax.all_to_all(value, EVERY, 0, 0, tiled=True)  30.1 us
  transfers between devices with their start and end apart: 86, of which 18 were waited for; matrix products, arithmetic and copies ran while one was open for 15% of the time, Pallas kernels for 43%

profile of v3, /device:TPU:1, one launch (start us, length us, event | category | flops | bytes accessed | tf_op | source)
XLA Modules:
  0.0 764.8 jit_solution(9875008876984574619)
XLA Ops:
  10.2 5.4 all-to-all-start
  18.6 4.8 convolution_convert_fusion.3
  40.7 6.4 collective-permute-done.4
  52.5 4.6 collective-permute-done.9.refs_6_
  67.6 4.3 all-to-all-start.1
  72.3 5.9 collective-permute-done.16.refs_3_
  80.3 10.1 %collective-permute-start.17 = (bf16[304,360]{1,0:T(8,128)(2,1)S(1)}, bf16[304,360]{1,0:T(8,128)(2,1)S(1)}, u32[]{:S(2)}, u32[]{:S(2)}) collective-permute-start(bf16[304,360]{1,0:T(8,128)(2,1)S(1)} %get-tuple-element.293), channel_id=1, source_target_pairs={{0,8},{8,0},{16,24},{24,16},{1,9},{9,1},{17,25},{25,17},{2,10},{10... | collective-permute-start | bytes 656648 | tf_op jit(solution)/shard_map/ppermute | solution.py:789
  102.0 9.8 %collective-permute-start.20 = (bf16[576,1152]{1,0:T(8,128)(2,1)}, bf16[576,1152]{1,0:T(8,128)(2,1)}, u32[]{:S(2)}, u32[]{:S(2)}) collective-permute-start(bf16[576,1152]{1,0:T(8,128)(2,1)} %shard_map.265.w_a.rest_4_), channel_id=1, source_target_pairs={{0,4},{4,0},{1,5},{5,1},{2,6},{6,2},{3,7},{7,3},{8,12},{12,8},{9,1... | collective-permute-start | bytes 3981320 | tf_op jit(solution)/shard_map/ppermute | solution.py:783
  130.0 7.6 all-to-all-start.2
  139.9 22.5 %all-to-all-done.2 = f32[32,8,216]{2,1,0:T(8,128)S(1)} async-done(((f32[32,8,216]{2,1,0:T(8,128)}), f32[32,8,216]{2,1,0:T(8,128)S(1)}, u32[]{:S(2)}, u32[]{:S(2)}) %all-to-all-start.2) | async-done | bytes 221216 | tf_op jit(solution)/shard_map/all_to_all | solution.py:795
  163.6 7.3 shard_map.267.h_ref
  172.0 4.6 all-to-all-start.3
  178.1 12.0 %shard_map.268 = (bf16[2,4,2,128,144]{4,3,2,1,0:T(8,128)(2,1)}, bf16[2,4,2,128,144]{4,3,2,1,0:T(8,128)(2,1)}, bf16[2,4,2,128,144]{4,3,2,1,0:T(8,128)(2,1)}, bf16...) custom-call(bf16[4,2,128,1152]{3,2,1,0:T(8,128)(2,1)} %shard_map.267.h_ref, bf16[576,1152]{1,0:T(8,128)(2,1)} %shard_map.265.w_a.rest_4_, ...), custom_call_target="tpu_custom_call" | custom-call | flops 13799999488 | tf_op jit(solution)/shard_map/pallas_call | solution.py:357
  192.3 12.0 %shard_map.271 = (bf16[2,4,2,128,144]{4,3,2,1,0:T(8,128)(2,1)}, bf16[2,4,2,128,144]{4,3,2,1,0:T(8,128)(2,1)}, bf16[2,4,2,128,144]{4,3,2,1,0:T(8,128)(2,1)}, bf16...) custom-call(bf16[4,2,128,1152]{3,2,1,0:T(8,128)(2,1)} %shard_map.267.h_ref, ...), custom_call_target="tpu_custom_call" | custom-call | flops 13799999488 | tf_op jit(solution)/shard_map/pallas_call | solution.py:357
  205.3 11.9 %shard_map.270 = (bf16[2,4,2,128,144]{4,3,2,1,0:T(8,128)(2,1)}, bf16[2,4,2,128,144]{4,3,2,1,0:T(8,128)(2,1)}, bf16[2,4,2,128,144]{4,3,2,1,0:T(8,128)(2,1)}, bf16...) custom-call(bf16[4,2,128,1152]{3,2,1,0:T(8,128)(2,1)} %shard_map.267.h_ref, ...), custom_call_target="tpu_custom_call" | custom-call | flops 13799999488 | tf_op jit(solution)/shard_map/pallas_call | solution.py:357
  224.1 12.0 %shard_map.269 = (bf16[2,4,2,128,144]{4,3,2,1,0:T(8,128)(2,1)}, bf16[2,4,2,128,144]{4,3,2,1,0:T(8,128)(2,1)}, bf16[2,4,2,128,144]{4,3,2,1,0:T(8,128)(2,1)}, bf16...) custom-call(bf16[4,2,128,1152]{3,2,1,0:T(8,128)(2,1)} %shard_map.267.h_ref, ...), custom_call_target="tpu_custom_call" | custom-call | flops 13799999488 | tf_op jit(solution)/shard_map/pallas_call | solution.py:357
  237.0 13.1 %shard_map.272 = (f32[4,2,128,1152]{3,2,1,0:T(8,128)}, f32[4,2,128,1152]{3,2,1,0:T(8,128)}, bf16[4,2,128,1152]{3,2,1,0:T(8,128)(2,1)}) custom-call(s32[2,4,2]{2,1,0:T(4,128)} %pad_add_fusion.2.ends_ref, bf16[4,2,128,1152]{3,2,1,0:T(8,128)(2,1)} %copy-done.12, s32[4,2,128,1]{3,2,1,0:T(8,128)} %copy.173.seg_ref, ...), custom_call_target="tpu_custom_call" | custom-call | flops 12650000384 | tf_op jit(solution)/shard_map/pallas_call | solution.py:558
  250.2 5.8 collective-permute-done.29.rest_0_
  260.9 8.5 %collective-permute-start.30 = (bf16[4,144,1152]{2,1,0:T(8,128)(2,1)}, bf16[4,144,1152]{2,1,0:T(8,128)(2,1)}, u32[]{:S(2)}, u32[]{:S(2)}) collective-permute-start(bf16[4,144,1152]{2,1,0:T(8,128)(2,1)} %collective-permute-done.29.rest_0_), channel_id=1, source_target_pairs={{0,8},{8,16},{16,24},{24,0},{1,9},{9,17},{17,25},{25,1},{2,10},{10... | collective-permute-start | bytes 3981320 | tf_op jit(solution)/shard_map/ppermute | solution.py:792
  269.4 26.8 %shard_map.274 = (f32[1024,1152]{1,0:T(8,128)}, f32[1024,1152]{1,0:T(8,128)}, bf16[2,576,1152]{2,1,0:T(8,128)(2,1)}, bf16[2,576,1152]{2,1,0:T(8,128)(2,1)}, f32[1,1152]{1,0:T(1,128)}) custom-call(bf16[1024,1152]{1,0:T(8,128)(2,1)} %bitcast.186, bf16[1024,1152]{1,0:T(8,128)(2,1)} %bitcast.146, f32[1,1,1152]{2,1,0:T(1,128)} %slice.234.ub_ref, ...), custom_call_target="tpu_custom_call" | custom-call | flops 36800000000 | tf_op jit(solution)/shard_map/pallas_call | solution.py:725
  297.7 4.6 collective-permute-done.30.rest_0_
  303.1 29.4 %shard_map.275 = (f32[1024,1152]{1,0:T(8,128)}, f32[1024,1152]{1,0:T(8,128)}, bf16[2,576,1152]{2,1,0:T(8,128)(2,1)}, bf16[2,576,1152]{2,1,0:T(8,128)(2,1)}, f32[1,1152]{1,0:T(1,128)}) custom-call(bf16[1024,1152]{1,0:T(8,128)(2,1)} %bitcast.187, bf16[1024,1152]{1,0:T(8,128)(2,1)} %bitcast.147, ...), custom_call_target="tpu_custom_call", output_to_operand_aliasing={{0}: (7, {}), {1}: (8, {})} | custom-call | flops 36800000000 | tf_op jit(solution)/shard_map/pallas_call | solution.py:725
  341.7 4.3 all-to-all-start.5
  346.1 29.5 %shard_map.276 = (f32[1024,1152]{1,0:T(8,128)}, f32[1024,1152]{1,0:T(8,128)}, bf16[2,576,1152]{2,1,0:T(8,128)(2,1)}, bf16[2,576,1152]{2,1,0:T(8,128)(2,1)}, f32[1,1152]{1,0:T(1,128)}) custom-call(bf16[1024,1152]{1,0:T(8,128)(2,1)} %bitcast.188, bf16[1024,1152]{1,0:T(8,128)(2,1)} %bitcast.148, ...), custom_call_target="tpu_custom_call", output_to_operand_aliasing={{0}: (8, {}), {1}: (9, {})} | custom-call | flops 36800000000 | tf_op jit(solution)/shard_map/pallas_call | solution.py:725
  385.9 29.4 %shard_map.277 = (f32[1024,1152]{1,0:T(8,128)}, f32[1024,1152]{1,0:T(8,128)}, bf16[2,576,1152]{2,1,0:T(8,128)(2,1)}, bf16[2,576,1152]{2,1,0:T(8,128)(2,1)}, f32[1,1152]{1,0:T(1,128)}) custom-call(bf16[1024,1152]{1,0:T(8,128)(2,1)} %bitcast.189, bf16[1024,1152]{1,0:T(8,128)(2,1)} %bitcast.149, ...), custom_call_target="tpu_custom_call", output_to_operand_aliasing={{0}: (10, {}), {1}: (11, {})} | custom-call | flops 36800000000 | tf_op jit(solution)/shard_map/pallas_call | solution.py:725
  431.1 16.0 %shard_map.278 = (bf16[4,2,128,1152]{3,2,1,0:T(8,128)(2,1)}, f32[4,2,128,1152]{3,2,1,0:T(8,128)}, bf16[4,2,128,1152]{3,2,1,0:T(8,128)(2,1)}, f32[2,4,4,1152]{3,2,1,0:T(4,128)}, f32[1,1152]{1,0:T(1,128)}) custom-call(s32[2,4,2]{2,1,0:T(4,128)} %pad_add_fusion.2.ends_ref, f32[4,2,128,1152]{3,2,1,0:T(8,128)} %get-tuple-element.126.mid_ref, ...), custom_call_target="tpu_custom_call" | custom-call | flops 14949999616 | tf_op jit(solution)/shard_map/pallas_call | solution.py:602
  461.5 4.6 all-to-all-start.9
  466.1 23.6 %shard_map.279 = (bf16[592,1152]{1,0:T(8,128)(2,1)}, bf16[592,1152]{1,0:T(8,128)(2,1)}, f32[4,2,128,1152]{3,2,1,0:T(8,128)}) custom-call(bf16[4,2,128,1152]{3,2,1,0:T(8,128)(2,1)} %shard_map.267.h_ref, bf16[4,2,128,1152]{3,2,1,0:T(8,128)(2,1)} %get-tuple-element.152.gb_ref, bf16[576,1152]{1,0:T(8,128)(2,1)} %collective-permute-done.25.w_a.rest_7_, ...), custom_call_target="tpu_custom_call" | custom-call | flops 27599998976 | tf_op jit(solution)/shard_map/pallas_call | solution.py:451
  495.8 5.0 all-to-all-start.8
  500.8 24.4 %shard_map.280 = (bf16[592,1152]{1,0:T(8,128)(2,1)}, bf16[592,1152]{1,0:T(8,128)(2,1)}, f32[4,2,128,1152]{3,2,1,0:T(8,128)}) custom-call(bf16[4,2,128,1152]{3,2,1,0:T(8,128)(2,1)} %shard_map.267.h_ref, bf16[4,2,128,1152]{3,2,1,0:T(8,128)(2,1)} %get-tuple-element.152.gb_ref, ...), custom_call_target="tpu_custom_call", output_to_operand_aliasing={{2}: (13, {})} | custom-call | flops 27599998976 | tf_op jit(solution)/shard_map/pallas_call | solution.py:451
  527.0 6.1 all-to-all-start.10
  533.1 5.5 shard_map.281.rest_2_
  543.0 24.3 %shard_map.282 = (bf16[592,1152]{1,0:T(8,128)(2,1)}, bf16[592,1152]{1,0:T(8,128)(2,1)}, f32[4,2,128,1152]{3,2,1,0:T(8,128)}) custom-call(bf16[4,2,128,1152]{3,2,1,0:T(8,128)(2,1)} %shard_map.267.h_ref, bf16[4,2,128,1152]{3,2,1,0:T(8,128)(2,1)} %get-tuple-element.152.gb_ref, ...), custom_call_target="tpu_custom_call", output_to_operand_aliasing={{2}: (19, {})} | custom-call | flops 27599998976 | tf_op jit(solution)/shard_map/pallas_call | solution.py:451
  579.9 8.0 %all-to-all-done.11.rest_0_ = bf16[4,144,1152]{2,1,0:T(8,128)(2,1)S(1)} async-done(((bf16[4,144,1152]{2,1,0:T(8,128)(2,1)}), bf16[4,144,1152]{2,1,0:T(8,128)(2,1)S(1)}, u32[]{:S(2)}, u32[]{:S(2)}) %all-to-all-start.11) | async-done | bytes 1327136 | tf_op jit(solution)/shard_map/all_to_all | solution.py:814
  596.3 24.3 %shard_map.283 = (bf16[592,1152]{1,0:T(8,128)(2,1)}, bf16[592,1152]{1,0:T(8,128)(2,1)}, f32[4,2,128,1152]{3,2,1,0:T(8,128)}) custom-call(bf16[4,2,128,1152]{3,2,1,0:T(8,128)(2,1)} %shard_map.267.h_ref, bf16[4,2,128,1152]{3,2,1,0:T(8,128)(2,1)} %get-tuple-element.152.gb_ref, ...), custom_call_target="tpu_custom_call", output_to_operand_aliasing={{2}: (15, {})} | custom-call | flops 27599998976 | tf_op jit(solution)/shard_map/pallas_call | solution.py:451
  622.1 9.9 %shard_map.284 = (bf16[4,2,128,1152]{3,2,1,0:T(8,128)(2,1)}, f32[2,4,2,1152]{3,2,1,0:T(2,128)}) custom-call(s32[2,4,2]{2,1,0:T(4,128)} %pad_add_fusion.2.ends_ref, bf16[4,2,128,1152]{3,2,1,0:T(8,128)(2,1)} %copy-done.12, f32[4,2,128,1152]{3,2,1,0:T(8,128)} %get-tuple-element.189.gh_ref, f32[4,2,128,1152]{3,2,1,0:T(8,128)} %get-tuple-element.190.gm_ref, ...), custom_call_target="tpu_custom_call" | custom-call | flops 9200000000 | tf_op jit(solution)/shard_map/pallas_call | solution.py:640
  634.2 4.8 all-to-all-start.12
  649.4 6.7 all-to-all-start.13
  656.2 4.7 broadcast_select_fusion.1
  662.2 5.1 collective-permute-start.62
  667.4 8.1 %all-to-all-done.13.early_ref = bf16[32,39,72]{2,1,0:T(8,128)(2,1)S(1)} async-done(((bf16[32,39,72]{2,1,0:T(8,128)(2,1)}), bf16[32,39,72]{2,1,0:T(8,128)(2,1)S(1)}, u32[]{:S(2)}, u32[]{:S(2)}) %all-to-all-start.13) | async-done | bytes 179744 | tf_op jit(solution)/shard_map/all_to_all | solution.py:795
  685.0 17.4 %collective-permute-done.61.refs_1_ = bf16[592,1152]{1,0:T(8,128)(2,1)S(1)} collective-permute-done((bf16[592,1152]{1,0:T(8,128)(2,1)}, bf16[592,1152]{1,0:T(8,128)(2,1)S(1)}, u32[]{:S(2)}, u32[]{:S(2)}) %collective-permute-start.61) | collective-permute-done | bytes 1364000 | tf_op jit(solution)/shard_map/ppermute | solution.py:786
  703.6 4.4 shard_map.288
  719.4 8.3 %collective-permute-start.70 = (bf16[40,1152]{1,0:T(8,128)(2,1)S(1)}, bf16[40,1152]{1,0:T(8,128)(2,1)S(1)}, u32[]{:S(2)}, u32[]{:S(2)}) collective-permute-start(bf16[40,1152]{1,0:T(8,128)(2,1)S(1)} %fusion.7), channel_id=1, source_target_pairs={{0,0},{8,1},{16,2},{24,3},{1,4},{9,5},{17,6},{25,7},{2,8},{10,9},{... | collective-permute-start | bytes 276488 | tf_op jit(solution)/shard_map/ppermute | solution.py:1035
  729.4 9.2 %collective-permute-done.65.refs_2_ = bf16[288,432]{1,0:T(8,128)(2,1)S(1)} collective-permute-done((bf16[288,432]{1,0:T(8,128)(2,1)S(1)}, bf16[288,432]{1,0:T(8,128)(2,1)S(1)}, u32[]{:S(2)}, u32[]{:S(2)}) %collective-permute-start.65) | collective-permute-done | bytes 248864 | tf_op jit(solution)/shard_map/ppermute | solution.py:789
  742.6 8.1 %all-to-all-start.14 = ((bf16[8,36,1008]{2,1,0:T(8,128)(2,1)}), bf16[8,36,1008]{2,1,0:T(8,128)(2,1)S(1)}, u32[]{:S(2)}, u32[]{:S(2)}) async-start(bf16[8,36,1008]{2,1,0:T(8,128)(2,1)} %shard_map.289), calls=%async_computation.14 | async-start | bytes 1310720 | tf_op jit(solution)/shard_map/all_to_all | solution.py:798
  750.8 4.7 broadcast_select_fusion
  756.7 4.5 all-to-all-done.14.refs_0_
  (451 shorter events, 232.1 us)
Async XLA Ops:
  10.2 47.5 %all-to-all-start = ((bf16[8,40,1872]{2,1,0:T(8,128)(2,1)}), bf16[8,40,1872]{2,1,0:T(8,128)(2,1)S(1)}, u32[]{:S(2)}, u32[]{:S(2)}) async-start(bf16[8,40,1872]{2,1,0:T(8,128)(2,1)} %shard_map.263), calls=%async_computation | async-start | bytes 2457600 | tf_op jit(solution)/shard_map/all_to_all | solution.py:798
  15.8 41.3 %collective-permute-start.11 = (bf16[144,1152]{1,0:T(8,128)(2,1)S(1)}, bf16[144,1152]{1,0:T(8,128)(2,1)S(1)}, u32[]{:S(2)}, u32[]{:S(2)}) collective-permute-start(bf16[144,1152]{1,0:T(8,128)(2,1)S(1)} %copy-done.47), channel_id=1, source_target_pairs={{0,1},{1,0},{2,3},{3,2},{4,5},{5,4},{6,7},{7,6},{8,9},{9,8},{10,11... | collective-permute-start | bytes 995336 | tf_op jit(solution)/shard_map/ppermute | solution.py:786
  67.6 61.4 %all-to-all-start.1 = ((bf16[4,2,128,1152]{3,2,1,0:T(8,128)(2,1)}), bf16[4,2,128,1152]{3,2,1,0:T(8,128)(2,1)S(1)}, u32[]{:S(2)}, u32[]{:S(2)}) async-start(bf16[4,2,128,1152]{3,2,1,0:T(8,128)(2,1)} %bitcast.12), calls=%async_computation.1 | async-start | bytes 4718592 | tf_op jit(solution)/shard_map/all_to_all | solution.py:814
  95.8 80.8 %collective-permute-start.25 = (bf16[576,1152]{1,0:T(8,128)(2,1)}, bf16[576,1152]{1,0:T(8,128)(2,1)}, u32[]{:S(2)}, u32[]{:S(2)}) collective-permute-start(bf16[576,1152]{1,0:T(8,128)(2,1)} %shard_map.265.w_a.rest_4_), channel_id=1, source_target_pairs={{0,3},{1,2},{2,1},{3,0},{4,7},{5,6},{6,5},{7,4},{8,11},{9,10},{10,... | collective-permute-start | bytes 3981320 | tf_op jit(solution)/shard_map/ppermute | solution.py:786
  99.3 77.8 %collective-permute-start.23 = (bf16[576,1152]{1,0:T(8,128)(2,1)}, bf16[576,1152]{1,0:T(8,128)(2,1)}, u32[]{:S(2)}, u32[]{:S(2)}) collective-permute-start(bf16[576,1152]{1,0:T(8,128)(2,1)} %shard_map.265.w_a.rest_4_), channel_id=1, source_target_pairs={{0,2},{1,3},{2,0},{3,1},{4,6},{5,7},{6,4},{7,5},{8,10},{9,11},{10,... | collective-permute-start | bytes 3981320 | tf_op jit(solution)/shard_map/ppermute | solution.py:786
  100.5 76.7 %collective-permute-start.21 = (bf16[576,1152]{1,0:T(8,128)(2,1)}, bf16[576,1152]{1,0:T(8,128)(2,1)}, u32[]{:S(2)}, u32[]{:S(2)}) collective-permute-start(bf16[576,1152]{1,0:T(8,128)(2,1)} %shard_map.265.w_a.rest_4_), channel_id=1, source_target_pairs={{0,1},{1,0},{2,3},{3,2},{4,5},{5,4},{6,7},{7,6},{8,9},{9,8},{10,11... | collective-permute-start | bytes 3981320 | tf_op jit(solution)/shard_map/ppermute | solution.py:786
  102.0 75.6 %collective-permute-start.20 = (bf16[576,1152]{1,0:T(8,128)(2,1)}, bf16[576,1152]{1,0:T(8,128)(2,1)}, u32[]{:S(2)}, u32[]{:S(2)}) collective-permute-start(bf16[576,1152]{1,0:T(8,128)(2,1)} %shard_map.265.w_a.rest_4_), channel_id=1, source_target_pairs={{0,4},{4,0},{1,5},{5,1},{2,6},{6,2},{3,7},{7,3},{8,12},{12,8},{9,1... | collective-permute-start | bytes 3981320 | tf_op jit(solution)/shard_map/ppermute | solution.py:783
  122.0 55.7 %collective-permute-start.27 = (bf16[4,144,1152]{2,1,0:T(8,128)(2,1)}, bf16[4,144,1152]{2,1,0:T(8,128)(2,1)}, u32[]{:S(2)}, u32[]{:S(2)}) collective-permute-start(bf16[4,144,1152]{2,1,0:T(8,128)(2,1)} %shard_map.273.rest_2_), channel_id=1, source_target_pairs={{0,8},{8,16},{16,24},{24,0},{1,9},{9,17},{17,25},{25,1},{2,10},{10... | collective-permute-start | bytes 3981320 | tf_op jit(solution)/shard_map/ppermute | solution.py:792
  130.0 32.4 %all-to-all-start.2 = ((f32[32,8,216]{2,1,0:T(8,128)}), f32[32,8,216]{2,1,0:T(8,128)S(1)}, u32[]{:S(2)}, u32[]{:S(2)}) async-start(f32[32,8,216]{2,1,0:T(8,128)} %bitcast.25), calls=%async_computation.2 | async-start | bytes 524288 | tf_op jit(solution)/shard_map/all_to_all | solution.py:795
  172.0 45.3 %all-to-all-start.3 = ((bf16[4,144,1152]{2,1,0:T(8,128)(2,1)}), bf16[4,144,1152]{2,1,0:T(8,128)(2,1)}, u32[]{:S(2)}, u32[]{:S(2)}) async-start(bf16[4,144,1152]{2,1,0:T(8,128)(2,1)} %broadcast_in_dim.160), calls=%async_computation.3 | async-start | bytes 2654208 | tf_op jit(solution)/shard_map/all_to_all | solution.py:814
  176.6 84.3 %collective-permute-start.38 = (bf16[4,144,1152]{2,1,0:T(8,128)(2,1)}, bf16[4,144,1152]{2,1,0:T(8,128)(2,1)}, u32[]{:S(2)}, u32[]{:S(2)}) collective-permute-start(bf16[4,144,1152]{2,1,0:T(8,128)(2,1)} %shard_map.273.rest_2_), channel_id=1, source_target_pairs={{0,4},{4,0},{1,5},{5,1},{2,6},{6,2},{3,7},{7,3},{8,12},{12,8},{9,1... | collective-permute-start | bytes 3981320 | tf_op jit(solution)/shard_map/ppermute | solution.py:783
  177.6 46.5 %collective-permute-start.22 = (bf16[576,1152]{1,0:T(8,128)(2,1)}, bf16[576,1152]{1,0:T(8,128)(2,1)}, u32[]{:S(2)}, u32[]{:S(2)}) collective-permute-start(bf16[576,1152]{1,0:T(8,128)(2,1)} %collective-permute-done.21.w_a.rest_5_), channel_id=1, source_target_pairs={{0,4},{4,0},{1,5},{5,1},{2,6},{6,2},{3,7},{7,3},{8,12},{12,8},{9,1... | collective-permute-start | bytes 3981320 | tf_op jit(solution)/shard_map/ppermute | solution.py:783
  177.7 124.5 %collective-permute-start.36 = (bf16[4,144,1152]{2,1,0:T(8,128)(2,1)}, bf16[4,144,1152]{2,1,0:T(8,128)(2,1)}, u32[]{:S(2)}, u32[]{:S(2)}) collective-permute-start(bf16[4,144,1152]{2,1,0:T(8,128)(2,1)} %collective-permute-done.27.rest_2_), channel_id=1, source_target_pairs={{0,4},{4,0},{1,5},{5,1},{2,6},{6,2},{3,7},{7,3},{8,12},{12,8},{9,1... | collective-permute-start | bytes 3981320 | tf_op jit(solution)/shard_map/ppermute | solution.py:783
  191.2 32.9 %collective-permute-start.28 = (bf16[4,144,1152]{2,1,0:T(8,128)(2,1)}, bf16[4,144,1152]{2,1,0:T(8,128)(2,1)}, u32[]{:S(2)}, u32[]{:S(2)}) collective-permute-start(bf16[4,144,1152]{2,1,0:T(8,128)(2,1)} %collective-permute-done.27.rest_2_), channel_id=1, source_target_pairs={{0,8},{8,16},{16,24},{24,0},{1,9},{9,17},{17,25},{25,1},{2,10},{10... | collective-permute-start | bytes 3981320 | tf_op jit(solution)/shard_map/ppermute | solution.py:792
  217.3 40.4 %all-to-all-start.4 = ((bf16[4,2,128,1152]{3,2,1,0:T(8,128)(2,1)}), bf16[4,2,128,1152]{3,2,1,0:T(8,128)(2,1)S(1)}, u32[]{:S(2)}, u32[]{:S(2)}) async-start(bf16[4,2,128,1152]{3,2,1,0:T(8,128)(2,1)} %bitcast.32), calls=%async_computation.4 | async-start | bytes 4718592 | tf_op jit(solution)/shard_map/all_to_all | solution.py:814
  236.1 33.3 %collective-permute-start.37 = (bf16[4,144,1152]{2,1,0:T(8,128)(2,1)}, bf16[4,144,1152]{2,1,0:T(8,128)(2,1)}, u32[]{:S(2)}, u32[]{:S(2)}) collective-permute-start(bf16[4,144,1152]{2,1,0:T(8,128)(2,1)} %all-to-all-done.3.rest_0_), channel_id=1, source_target_pairs={{0,4},{4,0},{1,5},{5,1},{2,6},{6,2},{3,7},{7,3},{8,12},{12,8},{9,1... | collective-permute-start | bytes 3981320 | tf_op jit(solution)/shard_map/ppermute | solution.py:783
  250.0 96.0 %collective-permute-start.42 = (bf16[4,144,1152]{2,1,0:T(8,128)(2,1)}, bf16[4,144,1152]{2,1,0:T(8,128)(2,1)}, u32[]{:S(2)}, u32[]{:S(2)}) collective-permute-start(bf16[4,144,1152]{2,1,0:T(8,128)(2,1)} %collective-permute-done.28.rest_2_), channel_id=1, source_target_pairs={{0,4},{4,0},{1,5},{5,1},{2,6},{6,2},{3,7},{7,3},{8,12},{12,8},{9,1... | collective-permute-start | bytes 3981320 | tf_op jit(solution)/shard_map/ppermute | solution.py:783
  255.9 47.1 %collective-permute-start.35 = (bf16[4,144,1152]{2,1,0:T(8,128)(2,1)}, bf16[4,144,1152]{2,1,0:T(8,128)(2,1)}, u32[]{:S(2)}, u32[]{:S(2)}) collective-permute-start(bf16[4,144,1152]{2,1,0:T(8,128)(2,1)} %collective-permute-done.29.rest_0_), channel_id=1, source_target_pairs={{0,4},{4,0},{1,5},{5,1},{2,6},{6,2},{3,7},{7,3},{8,12},{12,8},{9,1... | collective-permute-start | bytes 3981320 | tf_op jit(solution)/shard_map/ppermute | solution.py:783
  260.9 41.3 %collective-permute-start.30 = (bf16[4,144,1152]{2,1,0:T(8,128)(2,1)}, bf16[4,144,1152]{2,1,0:T(8,128)(2,1)}, u32[]{:S(2)}, u32[]{:S(2)}) collective-permute-start(bf16[4,144,1152]{2,1,0:T(8,128)(2,1)} %collective-permute-done.29.rest_0_), channel_id=1, source_target_pairs={{0,8},{8,16},{16,24},{24,0},{1,9},{9,17},{17,25},{25,1},{2,10},{10... | collective-permute-start | bytes 3981320 | tf_op jit(solution)/shard_map/ppermute | solution.py:792
  296.2 38.0 %collective-permute-start.40 = (bf16[2,576,1152]{2,1,0:T(8,128)(2,1)}, bf16[2,576,1152]{2,1,0:T(8,128)(2,1)}, u32[]{:S(2)}, u32[]{:S(2)}) collective-permute-start(bf16[2,576,1152]{2,1,0:T(8,128)(2,1)} %get-tuple-element.141), channel_id=1, source_target_pairs={{0,4},{4,0},{1,5},{5,1},{2,6},{6,2},{3,7},{7,3},{8,12},{12,8},{9,1... | collective-permute-start | bytes 7962632 | tf_op jit(solution)/shard_map/ppermute | solution.py:783
  302.3 43.8 %collective-permute-start.41 = (bf16[4,144,1152]{2,1,0:T(8,128)(2,1)}, bf16[4,144,1152]{2,1,0:T(8,128)(2,1)}, u32[]{:S(2)}, u32[]{:S(2)}) collective-permute-start(bf16[4,144,1152]{2,1,0:T(8,128)(2,1)} %collective-permute-done.30.rest_0_), channel_id=1, source_target_pairs={{0,4},{4,0},{1,5},{5,1},{2,6},{6,2},{3,7},{7,3},{8,12},{12,8},{9,1... | collective-permute-start | bytes 3981320 | tf_op jit(solution)/shard_map/ppermute | solution.py:783
  332.5 44.0 %collective-permute-start.39 = (bf16[2,576,1152]{2,1,0:T(8,128)(2,1)}, bf16[2,576,1152]{2,1,0:T(8,128)(2,1)}, u32[]{:S(2)}, u32[]{:S(2)}) collective-permute-start(bf16[2,576,1152]{2,1,0:T(8,128)(2,1)} %get-tuple-element.139), channel_id=1, source_target_pairs={{0,4},{4,0},{1,5},{5,1},{2,6},{6,2},{3,7},{7,3},{8,12},{12,8},{9,1... | collective-permute-start | bytes 7962632 | tf_op jit(solution)/shard_map/ppermute | solution.py:783
  334.2 42.2 %collective-permute-start.32 = (bf16[4,144,1152]{2,1,0:T(8,128)(2,1)}, bf16[4,144,1152]{2,1,0:T(8,128)(2,1)}, u32[]{:S(2)}, u32[]{:S(2)}) collective-permute-start(bf16[4,144,1152]{2,1,0:T(8,128)(2,1)} %collective-permute-done.30.rest_0_), channel_id=1, source_target_pairs={{0,8},{8,16},{16,24},{24,0},{1,9},{9,17},{17,25},{25,1},{2,10},{10... | collective-permute-start | bytes 3981320 | tf_op jit(solution)/shard_map/ppermute | solution.py:792
  334.2 51.6 %collective-permute-start.34 = (bf16[4,144,1152]{2,1,0:T(8,128)(2,1)}, bf16[4,144,1152]{2,1,0:T(8,128)(2,1)}, u32[]{:S(2)}, u32[]{:S(2)}) collective-permute-start(bf16[4,144,1152]{2,1,0:T(8,128)(2,1)} %collective-permute-done.31.rest_2_), channel_id=1, source_target_pairs={{0,4},{4,0},{1,5},{5,1},{2,6},{6,2},{3,7},{7,3},{8,12},{12,8},{9,1... | collective-permute-start | bytes 3981320 | tf_op jit(solution)/shard_map/ppermute | solution.py:783
  341.7 39.8 %all-to-all-start.5 = ((bf16[4,144,1152]{2,1,0:T(8,128)(2,1)}), bf16[4,144,1152]{2,1,0:T(8,128)(2,1)}, u32[]{:S(2)}, u32[]{:S(2)}) async-start(bf16[4,144,1152]{2,1,0:T(8,128)(2,1)} %bitcast.37.rest_4_), calls=%async_computation.5 | async-start | bytes 2654208 | tf_op jit(solution)/shard_map/all_to_all | solution.py:814
  375.6 42.2 %collective-permute-start.43 = (bf16[2,576,1152]{2,1,0:T(8,128)(2,1)}, bf16[2,576,1152]{2,1,0:T(8,128)(2,1)}, u32[]{:S(2)}, u32[]{:S(2)}) collective-permute-start(bf16[2,576,1152]{2,1,0:T(8,128)(2,1)} %get-tuple-element.150), channel_id=1, source_target_pairs={{0,4},{4,0},{1,5},{5,1},{2,6},{6,2},{3,7},{7,3},{8,12},{12,8},{9,1... | collective-permute-start | bytes 7962632 | tf_op jit(solution)/shard_map/ppermute | solution.py:783
  381.5 40.0 %collective-permute-start.44 = (bf16[4,144,1152]{2,1,0:T(8,128)(2,1)}, bf16[4,144,1152]{2,1,0:T(8,128)(2,1)}, u32[]{:S(2)}, u32[]{:S(2)}) collective-permute-start(bf16[4,144,1152]{2,1,0:T(8,128)(2,1)} %bitcast.36.rest_5_), channel_id=1, source_target_pairs={{0,8},{8,16},{16,24},{24,0},{1,9},{9,17},{17,25},{25,1},{2,10},{10... | collective-permute-start | bytes 3981320 | tf_op jit(solution)/shard_map/ppermute | solution.py:792
  381.5 45.3 %all-to-all-start.6 = ((bf16[4,144,1152]{2,1,0:T(8,128)(2,1)}), bf16[4,144,1152]{2,1,0:T(8,128)(2,1)}, u32[]{:S(2)}, u32[]{:S(2)}) async-start(bf16[4,144,1152]{2,1,0:T(8,128)(2,1)} %bitcast.35.rest_4_), calls=%async_computation.6 | async-start | bytes 2654208 | tf_op jit(solution)/shard_map/all_to_all | solution.py:814
  415.3 38.5 %collective-permute-start.45 = (bf16[2,576,1152]{2,1,0:T(8,128)(2,1)}, bf16[2,576,1152]{2,1,0:T(8,128)(2,1)}, u32[]{:S(2)}, u32[]{:S(2)}) collective-permute-start(bf16[2,576,1152]{2,1,0:T(8,128)(2,1)} %get-tuple-element.159), channel_id=1, source_target_pairs={{0,4},{4,0},{1,5},{5,1},{2,6},{6,2},{3,7},{7,3},{8,12},{12,8},{9,1... | collective-permute-start | bytes 7962632 | tf_op jit(solution)/shard_map/ppermute | solution.py:783
  424.2 33.3 %collective-permute-start.46 = (bf16[4,144,1152]{2,1,0:T(8,128)(2,1)}, bf16[4,144,1152]{2,1,0:T(8,128)(2,1)}, u32[]{:S(2)}, u32[]{:S(2)}) collective-permute-start(bf16[4,144,1152]{2,1,0:T(8,128)(2,1)} %add_convert_fusion.7.rest_1_), channel_id=1, source_target_pairs={{0,8},{8,16},{16,24},{24,0},{1,9},{9,17},{17,25},{25,1},{2,10},{10... | collective-permute-start | bytes 3981320 | tf_op jit(solution)/shard_map/ppermute | solution.py:792
  426.8 34.6 %all-to-all-start.7 = ((bf16[4,144,1152]{2,1,0:T(8,128)(2,1)}), bf16[4,144,1152]{2,1,0:T(8,128)(2,1)}, u32[]{:S(2)}, u32[]{:S(2)}) async-start(bf16[4,144,1152]{2,1,0:T(8,128)(2,1)} %bitcast.40.rest_0_), calls=%async_computation.7 | async-start | bytes 2654208 | tf_op jit(solution)/shard_map/all_to_all | solution.py:814
  460.2 78.5 %collective-permute-start.48 = (bf16[4,144,1152]{2,1,0:T(8,128)(2,1)}, bf16[4,144,1152]{2,1,0:T(8,128)(2,1)}, u32[]{:S(2)}, u32[]{:S(2)}) collective-permute-start(bf16[4,144,1152]{2,1,0:T(8,128)(2,1)} %add_convert_fusion.6.rest_1_), channel_id=1, source_target_pairs={{0,8},{8,16},{16,24},{24,0},{1,9},{9,17},{17,25},{25,1},{2,10},{10... | collective-permute-start | bytes 3981320 | tf_op jit(solution)/shard_map/ppermute | solution.py:792
  461.5 34.4 %all-to-all-start.9 = ((bf16[4,144,1152]{2,1,0:T(8,128)(2,1)}), bf16[4,144,1152]{2,1,0:T(8,128)(2,1)}, u32[]{:S(2)}, u32[]{:S(2)}) async-start(bf16[4,144,1152]{2,1,0:T(8,128)(2,1)} %bitcast.42.rest_0_), calls=%async_computation.9 | async-start | bytes 2654208 | tf_op jit(solution)/shard_map/all_to_all | solution.py:814
  489.7 51.8 %collective-permute-start.52 = (bf16[592,1152]{1,0:T(8,128)(2,1)}, bf16[592,1152]{1,0:T(8,128)(2,1)S(1)}, u32[]{:S(2)}, u32[]{:S(2)}) collective-permute-start(bf16[592,1152]{1,0:T(8,128)(2,1)} %get-tuple-element.184), channel_id=1, source_target_pairs={{0,4},{4,0},{1,5},{5,1},{2,6},{6,2},{3,7},{7,3},{8,12},{12,8},{9,1... | collective-permute-start | bytes 4091912 | tf_op jit(solution)/shard_map/ppermute | solution.py:783
  492.9 50.1 %collective-permute-start.49 = (bf16[2,128,1152]{2,1,0:T(8,128)(2,1)}, bf16[2,128,1152]{2,1,0:T(8,128)(2,1)}, u32[]{:S(2)}, u32[]{:S(2)}) collective-permute-start(bf16[2,128,1152]{2,1,0:T(8,128)(2,1)} %get-tuple-element.281), channel_id=1, source_target_pairs={{0,1},{1,0},{2,3},{3,2},{4,5},{5,4},{6,7},{7,6},{8,9},{9,8},{10,11... | collective-permute-start | bytes 1769480 | tf_op jit(solution)/shard_map/ppermute | solution.py:786
  494.6 48.4 %collective-permute-start.50 = (bf16[2,128,1152]{2,1,0:T(8,128)(2,1)}, bf16[2,128,1152]{2,1,0:T(8,128)(2,1)}, u32[]{:S(2)}, u32[]{:S(2)}) collective-permute-start(bf16[2,128,1152]{2,1,0:T(8,128)(2,1)} %get-tuple-element.280), channel_id=1, source_target_pairs={{0,2},{1,3},{2,0},{3,1},{4,6},{5,7},{6,4},{7,5},{8,10},{9,11},{10,... | collective-permute-start | bytes 1769480 | tf_op jit(solution)/shard_map/ppermute | solution.py:786
  495.8 47.2 %collective-permute-start.51 = (bf16[2,128,1152]{2,1,0:T(8,128)(2,1)}, bf16[2,128,1152]{2,1,0:T(8,128)(2,1)}, u32[]{:S(2)}, u32[]{:S(2)}) collective-permute-start(bf16[2,128,1152]{2,1,0:T(8,128)(2,1)} %get-tuple-element.279), channel_id=1, source_target_pairs={{0,3},{1,2},{2,1},{3,0},{4,7},{5,6},{6,5},{7,4},{8,11},{9,10},{10,... | collective-permute-start | bytes 1769480 | tf_op jit(solution)/shard_map/ppermute | solution.py:786
  527.0 40.4 %all-to-all-start.10 = ((bf16[32,37,144]{2,1,0:T(8,128)(2,1)}), bf16[32,37,144]{2,1,0:T(8,128)(2,1)S(1)}, u32[]{:S(2)}, u32[]{:S(2)}) async-start(bf16[32,37,144]{2,1,0:T(8,128)(2,1)} %pad_maximum_fusion), calls=%async_computation.10 | async-start | bytes 1310720 | tf_op jit(solution)/shard_map/all_to_all | solution.py:795
  538.7 50.4 %collective-permute-start.47 = (bf16[592,1152]{1,0:T(8,128)(2,1)}, bf16[592,1152]{1,0:T(8,128)(2,1)}, u32[]{:S(2)}, u32[]{:S(2)}) collective-permute-start(bf16[592,1152]{1,0:T(8,128)(2,1)} %get-tuple-element.179), channel_id=1, source_target_pairs={{0,4},{4,0},{1,5},{5,1},{2,6},{6,2},{3,7},{7,3},{8,12},{12,8},{9,1... | collective-permute-start | bytes 4091912 | tf_op jit(solution)/shard_map/ppermute | solution.py:783
  575.8 46.3 %collective-permute-start.54 = (bf16[288,576]{1,0:T(8,128)(2,1)}, bf16[288,576]{1,0:T(8,128)(2,1)}, u32[]{:S(2)}, u32[]{:S(2)}) collective-permute-start(bf16[288,576]{1,0:T(8,128)(2,1)} %get-tuple-element.286), channel_id=1, source_target_pairs={{0,8},{8,0},{16,24},{24,16},{1,9},{9,1},{17,25},{25,17},{2,10},{10... | collective-permute-start | bytes 995336 | tf_op jit(solution)/shard_map/ppermute | solution.py:789
  577.0 45.1 %collective-permute-start.55 = (bf16[288,576]{1,0:T(8,128)(2,1)}, bf16[288,576]{1,0:T(8,128)(2,1)}, u32[]{:S(2)}, u32[]{:S(2)}) collective-permute-start(bf16[288,576]{1,0:T(8,128)(2,1)} %get-tuple-element.285), channel_id=1, source_target_pairs={{0,16},{8,24},{16,0},{24,8},{1,17},{9,25},{17,1},{25,9},{2,18},{10... | collective-permute-start | bytes 995336 | tf_op jit(solution)/shard_map/ppermute | solution.py:789
  579.2 42.9 %collective-permute-start.56 = (bf16[288,576]{1,0:T(8,128)(2,1)S(1)}, bf16[288,576]{1,0:T(8,128)(2,1)}, u32[]{:S(2)}, u32[]{:S(2)}) collective-permute-start(bf16[288,576]{1,0:T(8,128)(2,1)S(1)} %get-tuple-element.284), channel_id=1, source_target_pairs={{0,24},{8,16},{16,8},{24,0},{1,25},{9,17},{17,9},{25,1},{2,26},{10... | collective-permute-start | bytes 995336 | tf_op jit(solution)/shard_map/ppermute | solution.py:789
  589.1 96.0 %collective-permute-start.60 = (bf16[592,1152]{1,0:T(8,128)(2,1)}, bf16[592,1152]{1,0:T(8,128)(2,1)}, u32[]{:S(2)}, u32[]{:S(2)}) collective-permute-start(bf16[592,1152]{1,0:T(8,128)(2,1)} %add_convert_fusion.3.rest_6_), channel_id=1, source_target_pairs={{0,3},{1,2},{2,1},{3,0},{4,7},{5,6},{6,5},{7,4},{8,11},{9,10},{10,... | collective-permute-start | bytes 4091912 | tf_op jit(solution)/shard_map/ppermute | solution.py:786
  620.6 61.7 %collective-permute-start.63 = (bf16[592,1152]{1,0:T(8,128)(2,1)}, bf16[592,1152]{1,0:T(8,128)(2,1)}, u32[]{:S(2)}, u32[]{:S(2)}) collective-permute-start(bf16[592,1152]{1,0:T(8,128)(2,1)} %get-tuple-element.196), channel_id=1, source_target_pairs={{0,4},{4,0},{1,5},{5,1},{2,6},{6,2},{3,7},{7,3},{8,12},{12,8},{9,1... | collective-permute-start | bytes 4091912 | tf_op jit(solution)/shard_map/ppermute | solution.py:783
  644.6 34.4 %collective-permute-start.59 = (bf16[2,128,1152]{2,1,0:T(8,128)(2,1)}, bf16[2,128,1152]{2,1,0:T(8,128)(2,1)}, u32[]{:S(2)}, u32[]{:S(2)}) collective-permute-start(bf16[2,128,1152]{2,1,0:T(8,128)(2,1)} %get-tuple-element.275), channel_id=1, source_target_pairs={{0,3},{1,2},{2,1},{3,0},{4,7},{5,6},{6,5},{7,4},{8,11},{9,10},{10,... | collective-permute-start | bytes 1769480 | tf_op jit(solution)/shard_map/ppermute | solution.py:786
  660.9 41.6 %collective-permute-start.61 = (bf16[592,1152]{1,0:T(8,128)(2,1)}, bf16[592,1152]{1,0:T(8,128)(2,1)S(1)}, u32[]{:S(2)}, u32[]{:S(2)}) collective-permute-start(bf16[592,1152]{1,0:T(8,128)(2,1)} %add_convert_fusion.4.rest_1_), channel_id=1, source_target_pairs={{0,1},{1,0},{2,3},{3,2},{4,5},{5,4},{6,7},{7,6},{8,9},{9,8},{10,11... | collective-permute-start | bytes 4091912 | tf_op jit(solution)/shard_map/ppermute | solution.py:786
  662.2 40.2 %collective-permute-start.62 = (bf16[592,1152]{1,0:T(8,128)(2,1)}, bf16[592,1152]{1,0:T(8,128)(2,1)}, u32[]{:S(2)}, u32[]{:S(2)}) collective-permute-start(bf16[592,1152]{1,0:T(8,128)(2,1)} %add_convert_fusion.2.rest_2_.rest_4_), channel_id=1, source_target_pairs={{0,2},{1,3},{2,0},{3,1},{4,6},{5,7},{6,4},{7,5},{8,10},{9,11},{10,... | collective-permute-start | bytes 4091912 | tf_op jit(solution)/shard_map/ppermute | solution.py:786
  719.4 36.1 %collective-permute-start.70 = (bf16[40,1152]{1,0:T(8,128)(2,1)S(1)}, bf16[40,1152]{1,0:T(8,128)(2,1)S(1)}, u32[]{:S(2)}, u32[]{:S(2)}) collective-permute-start(bf16[40,1152]{1,0:T(8,128)(2,1)S(1)} %fusion.7), channel_id=1, source_target_pairs={{0,0},{8,1},{16,2},{24,3},{1,4},{9,5},{17,6},{25,7},{2,8},{10,9},{... | collective-permute-start | bytes 276488 | tf_op jit(solution)/shard_map/ppermute | solution.py:1035
  (100 other events, 1716.5 us)

commit v4 on v3

--- a/solution.py
+++ b/solution.py
@@ -1019,15 +1019,11 @@
             waits.append(w_values[at])
 
     grad_x, sums_early = last_step(ends, inputs, grad_hidden, grad_mid, seg_tokens, table, waits)
-    grad_mine = [lax.dynamic_index_in_dim(grad_x, seq_at ^ k, 0, keepdims=False) for k in range(n_seq)]
-    grad_got = [grad_mine[0]] + [over_seq(grad_mine[k], k) for k in range(1, n_seq)]
-
     def in_place(got):
         return place(seq_scalar, got).reshape((row_count,) + got[0].shape[1:])
 
     res_got[0] = tie(res_got[0], grad_x)
     output = put_kept(in_place(res_got), tokens)
-    tokens_grad = put_kept(in_place(grad_got), cotangent)
 
     qkv_parts, out_parts = split_parts(w_planes, n_z)
     qkv_parts = to_z(qkv_parts)
@@ -1038,10 +1034,12 @@
 
     early = sums_early.reshape(rows * slots, 2, devices, shard).transpose(2, 0, 1, 3).reshape(devices, rows * slots, -1)
     early = all_to_all(early.astype(BF)).reshape(-1, 2 * shard)
+    grad_got = from_rows(tie(grad_x, early))
+    tokens_grad = put_kept(grad_got, cotangent)
     early_mod = dot_tn(act_all, early).astype(BF).reshape(devices, shard, 2 * shard)
     mod_sums = jnp.concatenate([jnp.sum(sums_early, (0, 1)), jnp.sum(sums_late, (0, 1))]).reshape(devices, 6 * shard)
     mod_sums = mod_sums.astype(BF).reshape(devices, 3, 2 * shard)
-    mod_got = all_to_all(jnp.concatenate([early_mod, mod_sums], 1))
+    mod_got = all_to_all(jnp.concatenate([tie(early_mod, grad_got), mod_sums], 1))
     mod_bias_grad = jnp.sum(mod_got[:, shard:].reshape(devices, -1).astype(F32), 0)
     dense_got = dense_to_all(deal(qkv_parts, up_parts, blocks))
     qkv_grad, up_grad = columns(

time: 780 us -> 756 us (0.969)
  starting transfers between devices: 179 us -> 166 us
    ppermute x18 -> x15, waiting for transfers between devices: 17.5 us -> 0.04 us  [over_seq(): return lax.ppermute(value, 'seq', [(i, i ^ by) for i in range(n_seq)])]
    ppermute x21, waiting for transfers between devices: 32.4 us -> 42 us  [over_z(): return lax.ppermute(value, 'z', [(i, i ^ by) for i in range(n_z)])]
    ppermute x18 -> x15, starting transfers between devices: 24.4 us -> 16.5 us  [over_seq(): return lax.ppermute(value, 'seq', [(i, i ^ by) for i in range(n_seq)])]
    all_to_all x8 -> x9, starting transfers between devices: 34.5 us -> 37.3 us  [seq_to_all(): return lax.all_to_all(value, 'seq', 0, 0, tiled=True)]
  transfers between devices with their start and end apart: 86 -> 84, of which waited for: 18 -> 19; matrix products, arithmetic and copies ran while one was open for 15% -> 15% of each run, Pallas kernels for 43% -> 45%
where the time goes in v4:
time: 756 us; the launch traced here: 745 us
  Pallas kernels  341 us (45%)
  starting transfers between devices  166 us (22%)
  waiting for transfers between devices  106 us (14%)
  local copies, waits for them, and re-layouts  55.2 us (7%)
  other arithmetic  54.3 us (7%)
  matrix products  19.2 us (3%)
    pallas_call x4, Pallas kernels, mlp_step(): pl.pallas_call(functools.partial(mlp_kernel, len(ups), len(downs), first,...  115 us
    pallas_call x4, Pallas kernels, attn_bwd(): pl.pallas_call(functools.partial(attn_bwd_kernel, head_size, first, len(w...  96.6 us
    pallas_call x4, Pallas kernels, attn_fwd(): pl.pallas_call(functools.partial(attn_fwd_kernel, head_size), grid=(rows,...  47.8 us
    ppermute x21, waiting for transfers between devices, over_z(): return lax.ppermute(value, 'z', [(i, i ^ by) for i in range(n_z)])  42 us
    all_to_all x5, waiting for transfers between devices, all_to_all(): return lax.all_to_all(value, EVERY, 0, 0, tiled=True)  37.7 us
    all_to_all x9, starting transfers between devices, seq_to_all(): return lax.all_to_all(value, 'seq', 0, 0, tiled=True)  37.3 us
    ppermute x21, starting transfers between devices, over_z(): return lax.ppermute(value, 'z', [(i, i ^ by) for i in range(n_z)])  31.4 us
    all_to_all x5, starting transfers between devices, all_to_all(): return lax.all_to_all(value, EVERY, 0, 0, tiled=True)  28.5 us
  transfers between devices with their start and end apart: 84, of which 19 were waited for; matrix products, arithmetic and copies ran while one was open for 15% of the time, Pallas kernels for 45%

profile of v4, /device:TPU:1, one launch (start us, length us, event | category | flops | bytes accessed | tf_op | source)
XLA Modules:
  0.0 744.5 jit_solution(1608807393886095600)
XLA Ops:
  10.2 5.4 all-to-all-start
  18.6 4.8 convolution_convert_fusion.3
  40.7 6.3 collective-permute-done.4
  48.6 4.0 collective-permute-done.10.refs_7_
  52.7 4.7 collective-permute-done.9.refs_6_
  72.3 6.6 collective-permute-done.16.refs_3_
  81.0 9.6 %collective-permute-start.17 = (bf16[304,360]{1,0:T(8,128)(2,1)S(1)}, bf16[304,360]{1,0:T(8,128)(2,1)S(1)}, u32[]{:S(2)}, u32[]{:S(2)}) collective-permute-start(bf16[304,360]{1,0:T(8,128)(2,1)S(1)} %get-tuple-element.293), channel_id=1, source_target_pairs={{0,8},{8,0},{16,24},{24,16},{1,9},{9,1},{17,25},{25,17},{2,10},{10... | collective-permute-start | bytes 656648 | tf_op jit(solution)/shard_map/ppermute | solution.py:789
  101.8 10.3 %collective-permute-start.20 = (bf16[576,1152]{1,0:T(8,128)(2,1)}, bf16[576,1152]{1,0:T(8,128)(2,1)}, u32[]{:S(2)}, u32[]{:S(2)}) collective-permute-start(bf16[576,1152]{1,0:T(8,128)(2,1)} %shard_map.265.w_a.rest_4_), channel_id=1, source_target_pairs={{0,4},{4,0},{1,5},{5,1},{2,6},{6,2},{3,7},{7,3},{8,12},{12,8},{9,1... | collective-permute-start | bytes 3981320 | tf_op jit(solution)/shard_map/ppermute | solution.py:783
  130.0 7.7 %all-to-all-start.2 = ((f32[32,8,216]{2,1,0:T(8,128)}), f32[32,8,216]{2,1,0:T(8,128)S(1)}, u32[]{:S(2)}, u32[]{:S(2)}) async-start(f32[32,8,216]{2,1,0:T(8,128)} %bitcast.25), calls=%async_computation.2 | async-start | bytes 524288 | tf_op jit(solution)/shard_map/all_to_all | solution.py:795
  139.9 22.2 %all-to-all-done.2 = f32[32,8,216]{2,1,0:T(8,128)S(1)} async-done(((f32[32,8,216]{2,1,0:T(8,128)}), f32[32,8,216]{2,1,0:T(8,128)S(1)}, u32[]{:S(2)}, u32[]{:S(2)}) %all-to-all-start.2) | async-done | bytes 221216 | tf_op jit(solution)/shard_map/all_to_all | solution.py:795
  163.2 7.2 shard_map.267.h_ref
  171.6 4.6 all-to-all-start.3
  177.7 11.9 %shard_map.268 = (bf16[2,4,2,128,144]{4,3,2,1,0:T(8,128)(2,1)}, bf16[2,4,2,128,144]{4,3,2,1,0:T(8,128)(2,1)}, bf16[2,4,2,128,144]{4,3,2,1,0:T(8,128)(2,1)}, bf16...) custom-call(bf16[4,2,128,1152]{3,2,1,0:T(8,128)(2,1)} %shard_map.267.h_ref, bf16[576,1152]{1,0:T(8,128)(2,1)} %shard_map.265.w_a.rest_4_, ...), custom_call_target="tpu_custom_call" | custom-call | flops 13799999488 | tf_op jit(solution)/shard_map/pallas_call | solution.py:357
  191.8 11.9 %shard_map.271 = (bf16[2,4,2,128,144]{4,3,2,1,0:T(8,128)(2,1)}, bf16[2,4,2,128,144]{4,3,2,1,0:T(8,128)(2,1)}, bf16[2,4,2,128,144]{4,3,2,1,0:T(8,128)(2,1)}, bf16...) custom-call(bf16[4,2,128,1152]{3,2,1,0:T(8,128)(2,1)} %shard_map.267.h_ref, ...), custom_call_target="tpu_custom_call" | custom-call | flops 13799999488 | tf_op jit(solution)/shard_map/pallas_call | solution.py:357
  204.9 12.0 %shard_map.270 = (bf16[2,4,2,128,144]{4,3,2,1,0:T(8,128)(2,1)}, bf16[2,4,2,128,144]{4,3,2,1,0:T(8,128)(2,1)}, bf16[2,4,2,128,144]{4,3,2,1,0:T(8,128)(2,1)}, bf16...) custom-call(bf16[4,2,128,1152]{3,2,1,0:T(8,128)(2,1)} %shard_map.267.h_ref, ...), custom_call_target="tpu_custom_call" | custom-call | flops 13799999488 | tf_op jit(solution)/shard_map/pallas_call | solution.py:357
  223.5 12.0 %shard_map.269 = (bf16[2,4,2,128,144]{4,3,2,1,0:T(8,128)(2,1)}, bf16[2,4,2,128,144]{4,3,2,1,0:T(8,128)(2,1)}, bf16[2,4,2,128,144]{4,3,2,1,0:T(8,128)(2,1)}, bf16...) custom-call(bf16[4,2,128,1152]{3,2,1,0:T(8,128)(2,1)} %shard_map.267.h_ref, ...), custom_call_target="tpu_custom_call" | custom-call | flops 13799999488 | tf_op jit(solution)/shard_map/pallas_call | solution.py:357
  236.5 13.0 %shard_map.272 = (f32[4,2,128,1152]{3,2,1,0:T(8,128)}, f32[4,2,128,1152]{3,2,1,0:T(8,128)}, bf16[4,2,128,1152]{3,2,1,0:T(8,128)(2,1)}) custom-call(s32[2,4,2]{2,1,0:T(4,128)} %pad_add_fusion.2.ends_ref, bf16[4,2,128,1152]{3,2,1,0:T(8,128)(2,1)} %copy-done.12, s32[4,2,128,1]{3,2,1,0:T(8,128)} %copy.173.seg_ref, ...), custom_call_target="tpu_custom_call" | custom-call | flops 12650000384 | tf_op jit(solution)/shard_map/pallas_call | solution.py:558
  249.6 5.7 collective-permute-done.29.rest_0_
  260.4 8.5 %collective-permute-start.30 = (bf16[4,144,1152]{2,1,0:T(8,128)(2,1)}, bf16[4,144,1152]{2,1,0:T(8,128)(2,1)}, u32[]{:S(2)}, u32[]{:S(2)}) collective-permute-start(bf16[4,144,1152]{2,1,0:T(8,128)(2,1)} %collective-permute-done.29.rest_0_), channel_id=1, source_target_pairs={{0,8},{8,16},{16,24},{24,0},{1,9},{9,17},{17,25},{25,1},{2,10},{10... | collective-permute-start | bytes 3981320 | tf_op jit(solution)/shard_map/ppermute | solution.py:792
  268.9 26.8 %shard_map.274 = (f32[1024,1152]{1,0:T(8,128)}, f32[1024,1152]{1,0:T(8,128)}, bf16[2,576,1152]{2,1,0:T(8,128)(2,1)}, bf16[2,576,1152]{2,1,0:T(8,128)(2,1)}, f32[1,1152]{1,0:T(1,128)}) custom-call(bf16[1024,1152]{1,0:T(8,128)(2,1)} %bitcast.178, bf16[1024,1152]{1,0:T(8,128)(2,1)} %bitcast.139, f32[1,1,1152]{2,1,0:T(1,128)} %slice.234.ub_ref, ...), custom_call_target="tpu_custom_call" | custom-call | flops 36800000000 | tf_op jit(solution)/shard_map/pallas_call | solution.py:725
  297.2 4.6 collective-permute-done.30.rest_0_
  302.5 29.4 %shard_map.275 = (f32[1024,1152]{1,0:T(8,128)}, f32[1024,1152]{1,0:T(8,128)}, bf16[2,576,1152]{2,1,0:T(8,128)(2,1)}, bf16[2,576,1152]{2,1,0:T(8,128)(2,1)}, f32[1,1152]{1,0:T(1,128)}) custom-call(bf16[1024,1152]{1,0:T(8,128)(2,1)} %bitcast.179, bf16[1024,1152]{1,0:T(8,128)(2,1)} %bitcast.140, ...), custom_call_target="tpu_custom_call", output_to_operand_aliasing={{0}: (7, {}), {1}: (8, {})} | custom-call | flops 36800000000 | tf_op jit(solution)/shard_map/pallas_call | solution.py:725
  341.3 4.3 all-to-all-start.5
  345.6 29.5 %shard_map.276 = (f32[1024,1152]{1,0:T(8,128)}, f32[1024,1152]{1,0:T(8,128)}, bf16[2,576,1152]{2,1,0:T(8,128)(2,1)}, bf16[2,576,1152]{2,1,0:T(8,128)(2,1)}, f32[1,1152]{1,0:T(1,128)}) custom-call(bf16[1024,1152]{1,0:T(8,128)(2,1)} %bitcast.180, bf16[1024,1152]{1,0:T(8,128)(2,1)} %bitcast.141, ...), custom_call_target="tpu_custom_call", output_to_operand_aliasing={{0}: (8, {}), {1}: (9, {})} | custom-call | flops 36800000000 | tf_op jit(solution)/shard_map/pallas_call | solution.py:725
  380.9 4.3 all-to-all-start.6
  385.3 29.4 %shard_map.277 = (f32[1024,1152]{1,0:T(8,128)}, f32[1024,1152]{1,0:T(8,128)}, bf16[2,576,1152]{2,1,0:T(8,128)(2,1)}, bf16[2,576,1152]{2,1,0:T(8,128)(2,1)}, f32[1,1152]{1,0:T(1,128)}) custom-call(bf16[1024,1152]{1,0:T(8,128)(2,1)} %bitcast.181, bf16[1024,1152]{1,0:T(8,128)(2,1)} %bitcast.142, ...), custom_call_target="tpu_custom_call", output_to_operand_aliasing={{0}: (10, {}), {1}: (11, {})} | custom-call | flops 36800000000 | tf_op jit(solution)/shard_map/pallas_call | solution.py:725
  426.9 4.3 all-to-all-start.7
  431.3 16.0 %shard_map.278 = (bf16[4,2,128,1152]{3,2,1,0:T(8,128)(2,1)}, f32[4,2,128,1152]{3,2,1,0:T(8,128)}, bf16[4,2,128,1152]{3,2,1,0:T(8,128)(2,1)}, f32[2,4,4,1152]{3,2,1,0:T(4,128)}, f32[1,1152]{1,0:T(1,128)}) custom-call(s32[2,4,2]{2,1,0:T(4,128)} %pad_add_fusion.2.ends_ref, f32[4,2,128,1152]{3,2,1,0:T(8,128)} %get-tuple-element.128.mid_ref, ...), custom_call_target="tpu_custom_call" | custom-call | flops 14949999616 | tf_op jit(solution)/shard_map/pallas_call | solution.py:602
  461.6 4.7 all-to-all-start.9
  466.3 23.6 %shard_map.279 = (bf16[592,1152]{1,0:T(8,128)(2,1)}, bf16[592,1152]{1,0:T(8,128)(2,1)}, f32[4,2,128,1152]{3,2,1,0:T(8,128)}) custom-call(bf16[4,2,128,1152]{3,2,1,0:T(8,128)(2,1)} %shard_map.267.h_ref, bf16[4,2,128,1152]{3,2,1,0:T(8,128)(2,1)} %get-tuple-element.154.gb_ref, bf16[576,1152]{1,0:T(8,128)(2,1)} %collective-permute-done.25.w_a.rest_7_, ...), custom_call_target="tpu_custom_call" | custom-call | flops 27599998976 | tf_op jit(solution)/shard_map/pallas_call | solution.py:451
  495.8 5.2 all-to-all-start.8
  501.0 24.4 %shard_map.280 = (bf16[592,1152]{1,0:T(8,128)(2,1)}, bf16[592,1152]{1,0:T(8,128)(2,1)}, f32[4,2,128,1152]{3,2,1,0:T(8,128)}) custom-call(bf16[4,2,128,1152]{3,2,1,0:T(8,128)(2,1)} %shard_map.267.h_ref, bf16[4,2,128,1152]{3,2,1,0:T(8,128)(2,1)} %get-tuple-element.154.gb_ref, ...), custom_call_target="tpu_custom_call", output_to_operand_aliasing={{2}: (13, {})} | custom-call | flops 27599998976 | tf_op jit(solution)/shard_map/pallas_call | solution.py:451
  528.5 6.1 all-to-all-start.10
  534.7 5.5 shard_map.281.rest_2_
  544.6 24.3 %shard_map.282 = (bf16[592,1152]{1,0:T(8,128)(2,1)}, bf16[592,1152]{1,0:T(8,128)(2,1)}, f32[4,2,128,1152]{3,2,1,0:T(8,128)}) custom-call(bf16[4,2,128,1152]{3,2,1,0:T(8,128)(2,1)} %shard_map.267.h_ref, bf16[4,2,128,1152]{3,2,1,0:T(8,128)(2,1)} %get-tuple-element.154.gb_ref, ...), custom_call_target="tpu_custom_call", output_to_operand_aliasing={{2}: (19, {})} | custom-call | flops 27599998976 | tf_op jit(solution)/shard_map/pallas_call | solution.py:451
  582.9 7.2 all-to-all-done.11.rest_0_
  599.6 24.3 %shard_map.283 = (bf16[592,1152]{1,0:T(8,128)(2,1)}, bf16[592,1152]{1,0:T(8,128)(2,1)}, f32[4,2,128,1152]{3,2,1,0:T(8,128)}) custom-call(bf16[4,2,128,1152]{3,2,1,0:T(8,128)(2,1)} %shard_map.267.h_ref, bf16[4,2,128,1152]{3,2,1,0:T(8,128)(2,1)} %get-tuple-element.154.gb_ref, ...), custom_call_target="tpu_custom_call", output_to_operand_aliasing={{2}: (15, {})} | custom-call | flops 27599998976 | tf_op jit(solution)/shard_map/pallas_call | solution.py:451
  626.3 9.9 %shard_map.284 = (bf16[4,2,128,1152]{3,2,1,0:T(8,128)(2,1)}, f32[2,4,2,1152]{3,2,1,0:T(2,128)}) custom-call(s32[2,4,2]{2,1,0:T(4,128)} %pad_add_fusion.2.ends_ref, bf16[4,2,128,1152]{3,2,1,0:T(8,128)(2,1)} %copy-done.12, f32[4,2,128,1152]{3,2,1,0:T(8,128)} %get-tuple-element.191.gh_ref, f32[4,2,128,1152]{3,2,1,0:T(8,128)} %get-tuple-element.192.gm_ref, ...), custom_call_target="tpu_custom_call" | custom-call | flops 9200000000 | tf_op jit(solution)/shard_map/pallas_call | solution.py:640
  638.4 4.8 all-to-all-start.12
  646.4 5.4 broadcast_select_fusion.1
  651.9 5.0 all-to-all-done.12
  663.7 4.4 shard_map.287
  680.4 6.4 collective-permute-start.67
  693.4 4.8 all-to-all-start.14
  699.5 5.5 collective-permute-done.61.refs_1_
  705.0 8.2 %collective-permute-done.62.refs_2_ = bf16[288,432]{1,0:T(8,128)(2,1)} collective-permute-done((bf16[288,432]{1,0:T(8,128)(2,1)}, bf16[288,432]{1,0:T(8,128)(2,1)}, u32[]{:S(2)}, u32[]{:S(2)}) %collective-permute-start.62) | collective-permute-done | bytes 248864 | tf_op jit(solution)/shard_map/ppermute | solution.py:789
  716.3 10.5 %all-to-all-done.14.early_ref = bf16[32,39,72]{2,1,0:T(8,128)(2,1)S(1)} async-done(((bf16[32,39,72]{2,1,0:T(8,128)(2,1)}), bf16[32,39,72]{2,1,0:T(8,128)(2,1)S(1)}, u32[]{:S(2)}, u32[]{:S(2)}) %all-to-all-start.14) | async-done | bytes 179744 | tf_op jit(solution)/shard_map/all_to_all | solution.py:795
  730.5 4.7 broadcast_select_fusion
  (425 shorter events, 230.2 us)
Async XLA Ops:
  10.2 47.9 %all-to-all-start = ((bf16[8,40,1872]{2,1,0:T(8,128)(2,1)}), bf16[8,40,1872]{2,1,0:T(8,128)(2,1)S(1)}, u32[]{:S(2)}, u32[]{:S(2)}) async-start(bf16[8,40,1872]{2,1,0:T(8,128)(2,1)} %shard_map.263), calls=%async_computation | async-start | bytes 2457600 | tf_op jit(solution)/shard_map/all_to_all | solution.py:798
  15.8 41.7 %collective-permute-start.11 = (bf16[144,1152]{1,0:T(8,128)(2,1)S(1)}, bf16[144,1152]{1,0:T(8,128)(2,1)S(1)}, u32[]{:S(2)}, u32[]{:S(2)}) collective-permute-start(bf16[144,1152]{1,0:T(8,128)(2,1)S(1)} %copy-done.43), channel_id=1, source_target_pairs={{0,1},{1,0},{2,3},{3,2},{4,5},{5,4},{6,7},{7,6},{8,9},{9,8},{10,11... | collective-permute-start | bytes 995336 | tf_op jit(solution)/shard_map/ppermute | solution.py:786
  68.0 60.9 %all-to-all-start.1 = ((bf16[4,2,128,1152]{3,2,1,0:T(8,128)(2,1)}), bf16[4,2,128,1152]{3,2,1,0:T(8,128)(2,1)S(1)}, u32[]{:S(2)}, u32[]{:S(2)}) async-start(bf16[4,2,128,1152]{3,2,1,0:T(8,128)(2,1)} %bitcast.12), calls=%async_computation.1 | async-start | bytes 4718592 | tf_op jit(solution)/shard_map/all_to_all | solution.py:814
  96.0 80.3 %collective-permute-start.25 = (bf16[576,1152]{1,0:T(8,128)(2,1)}, bf16[576,1152]{1,0:T(8,128)(2,1)}, u32[]{:S(2)}, u32[]{:S(2)}) collective-permute-start(bf16[576,1152]{1,0:T(8,128)(2,1)} %shard_map.265.w_a.rest_4_), channel_id=1, source_target_pairs={{0,3},{1,2},{2,1},{3,0},{4,7},{5,6},{6,5},{7,4},{8,11},{9,10},{10,... | collective-permute-start | bytes 3981320 | tf_op jit(solution)/shard_map/ppermute | solution.py:786
  97.9 78.8 %collective-permute-start.23 = (bf16[576,1152]{1,0:T(8,128)(2,1)}, bf16[576,1152]{1,0:T(8,128)(2,1)}, u32[]{:S(2)}, u32[]{:S(2)}) collective-permute-start(bf16[576,1152]{1,0:T(8,128)(2,1)} %shard_map.265.w_a.rest_4_), channel_id=1, source_target_pairs={{0,2},{1,3},{2,0},{3,1},{4,6},{5,7},{6,4},{7,5},{8,10},{9,11},{10,... | collective-permute-start | bytes 3981320 | tf_op jit(solution)/shard_map/ppermute | solution.py:786
  100.5 76.3 %collective-permute-start.21 = (bf16[576,1152]{1,0:T(8,128)(2,1)}, bf16[576,1152]{1,0:T(8,128)(2,1)}, u32[]{:S(2)}, u32[]{:S(2)}) collective-permute-start(bf16[576,1152]{1,0:T(8,128)(2,1)} %shard_map.265.w_a.rest_4_), channel_id=1, source_target_pairs={{0,1},{1,0},{2,3},{3,2},{4,5},{5,4},{6,7},{7,6},{8,9},{9,8},{10,11... | collective-permute-start | bytes 3981320 | tf_op jit(solution)/shard_map/ppermute | solution.py:786
  101.8 75.4 %collective-permute-start.20 = (bf16[576,1152]{1,0:T(8,128)(2,1)}, bf16[576,1152]{1,0:T(8,128)(2,1)}, u32[]{:S(2)}, u32[]{:S(2)}) collective-permute-start(bf16[576,1152]{1,0:T(8,128)(2,1)} %shard_map.265.w_a.rest_4_), channel_id=1, source_target_pairs={{0,4},{4,0},{1,5},{5,1},{2,6},{6,2},{3,7},{7,3},{8,12},{12,8},{9,1... | collective-permute-start | bytes 3981320 | tf_op jit(solution)/shard_map/ppermute | solution.py:783
  122.4 55.0 %collective-permute-start.27 = (bf16[4,144,1152]{2,1,0:T(8,128)(2,1)}, bf16[4,144,1152]{2,1,0:T(8,128)(2,1)}, u32[]{:S(2)}, u32[]{:S(2)}) collective-permute-start(bf16[4,144,1152]{2,1,0:T(8,128)(2,1)} %shard_map.273.rest_2_), channel_id=1, source_target_pairs={{0,8},{8,16},{16,24},{24,0},{1,9},{9,17},{17,25},{25,1},{2,10},{10... | collective-permute-start | bytes 3981320 | tf_op jit(solution)/shard_map/ppermute | solution.py:792
  130.0 32.1 %all-to-all-start.2 = ((f32[32,8,216]{2,1,0:T(8,128)}), f32[32,8,216]{2,1,0:T(8,128)S(1)}, u32[]{:S(2)}, u32[]{:S(2)}) async-start(f32[32,8,216]{2,1,0:T(8,128)} %bitcast.25), calls=%async_computation.2 | async-start | bytes 524288 | tf_op jit(solution)/shard_map/all_to_all | solution.py:795
  171.6 45.3 %all-to-all-start.3 = ((bf16[4,144,1152]{2,1,0:T(8,128)(2,1)}), bf16[4,144,1152]{2,1,0:T(8,128)(2,1)}, u32[]{:S(2)}, u32[]{:S(2)}) async-start(bf16[4,144,1152]{2,1,0:T(8,128)(2,1)} %broadcast_in_dim.160), calls=%async_computation.3 | async-start | bytes 2654208 | tf_op jit(solution)/shard_map/all_to_all | solution.py:814
  176.2 84.1 %collective-permute-start.38 = (bf16[4,144,1152]{2,1,0:T(8,128)(2,1)}, bf16[4,144,1152]{2,1,0:T(8,128)(2,1)}, u32[]{:S(2)}, u32[]{:S(2)}) collective-permute-start(bf16[4,144,1152]{2,1,0:T(8,128)(2,1)} %shard_map.273.rest_2_), channel_id=1, source_target_pairs={{0,4},{4,0},{1,5},{5,1},{2,6},{6,2},{3,7},{7,3},{8,12},{12,8},{9,1... | collective-permute-start | bytes 3981320 | tf_op jit(solution)/shard_map/ppermute | solution.py:783
  177.2 46.3 %collective-permute-start.22 = (bf16[576,1152]{1,0:T(8,128)(2,1)}, bf16[576,1152]{1,0:T(8,128)(2,1)}, u32[]{:S(2)}, u32[]{:S(2)}) collective-permute-start(bf16[576,1152]{1,0:T(8,128)(2,1)} %collective-permute-done.21.w_a.rest_5_), channel_id=1, source_target_pairs={{0,4},{4,0},{1,5},{5,1},{2,6},{6,2},{3,7},{7,3},{8,12},{12,8},{9,1... | collective-permute-start | bytes 3981320 | tf_op jit(solution)/shard_map/ppermute | solution.py:783
  177.3 124.4 %collective-permute-start.36 = (bf16[4,144,1152]{2,1,0:T(8,128)(2,1)}, bf16[4,144,1152]{2,1,0:T(8,128)(2,1)}, u32[]{:S(2)}, u32[]{:S(2)}) collective-permute-start(bf16[4,144,1152]{2,1,0:T(8,128)(2,1)} %collective-permute-done.27.rest_2_), channel_id=1, source_target_pairs={{0,4},{4,0},{1,5},{5,1},{2,6},{6,2},{3,7},{7,3},{8,12},{12,8},{9,1... | collective-permute-start | bytes 3981320 | tf_op jit(solution)/shard_map/ppermute | solution.py:783
  190.8 32.8 %collective-permute-start.28 = (bf16[4,144,1152]{2,1,0:T(8,128)(2,1)}, bf16[4,144,1152]{2,1,0:T(8,128)(2,1)}, u32[]{:S(2)}, u32[]{:S(2)}) collective-permute-start(bf16[4,144,1152]{2,1,0:T(8,128)(2,1)} %collective-permute-done.27.rest_2_), channel_id=1, source_target_pairs={{0,8},{8,16},{16,24},{24,0},{1,9},{9,17},{17,25},{25,1},{2,10},{10... | collective-permute-start | bytes 3981320 | tf_op jit(solution)/shard_map/ppermute | solution.py:792
  216.9 40.3 %all-to-all-start.4 = ((bf16[4,2,128,1152]{3,2,1,0:T(8,128)(2,1)}), bf16[4,2,128,1152]{3,2,1,0:T(8,128)(2,1)S(1)}, u32[]{:S(2)}, u32[]{:S(2)}) async-start(bf16[4,2,128,1152]{3,2,1,0:T(8,128)(2,1)} %bitcast.32), calls=%async_computation.4 | async-start | bytes 4718592 | tf_op jit(solution)/shard_map/all_to_all | solution.py:814
  235.5 33.4 %collective-permute-start.37 = (bf16[4,144,1152]{2,1,0:T(8,128)(2,1)}, bf16[4,144,1152]{2,1,0:T(8,128)(2,1)}, u32[]{:S(2)}, u32[]{:S(2)}) collective-permute-start(bf16[4,144,1152]{2,1,0:T(8,128)(2,1)} %all-to-all-done.3.rest_0_), channel_id=1, source_target_pairs={{0,4},{4,0},{1,5},{5,1},{2,6},{6,2},{3,7},{7,3},{8,12},{12,8},{9,1... | collective-permute-start | bytes 3981320 | tf_op jit(solution)/shard_map/ppermute | solution.py:783
  249.5 96.0 %collective-permute-start.42 = (bf16[4,144,1152]{2,1,0:T(8,128)(2,1)}, bf16[4,144,1152]{2,1,0:T(8,128)(2,1)}, u32[]{:S(2)}, u32[]{:S(2)}) collective-permute-start(bf16[4,144,1152]{2,1,0:T(8,128)(2,1)} %collective-permute-done.28.rest_2_), channel_id=1, source_target_pairs={{0,4},{4,0},{1,5},{5,1},{2,6},{6,2},{3,7},{7,3},{8,12},{12,8},{9,1... | collective-permute-start | bytes 3981320 | tf_op jit(solution)/shard_map/ppermute | solution.py:783
  255.3 47.2 %collective-permute-start.35 = (bf16[4,144,1152]{2,1,0:T(8,128)(2,1)}, bf16[4,144,1152]{2,1,0:T(8,128)(2,1)}, u32[]{:S(2)}, u32[]{:S(2)}) collective-permute-start(bf16[4,144,1152]{2,1,0:T(8,128)(2,1)} %collective-permute-done.29.rest_0_), channel_id=1, source_target_pairs={{0,4},{4,0},{1,5},{5,1},{2,6},{6,2},{3,7},{7,3},{8,12},{12,8},{9,1... | collective-permute-start | bytes 3981320 | tf_op jit(solution)/shard_map/ppermute | solution.py:783
  260.4 41.3 %collective-permute-start.30 = (bf16[4,144,1152]{2,1,0:T(8,128)(2,1)}, bf16[4,144,1152]{2,1,0:T(8,128)(2,1)}, u32[]{:S(2)}, u32[]{:S(2)}) collective-permute-start(bf16[4,144,1152]{2,1,0:T(8,128)(2,1)} %collective-permute-done.29.rest_0_), channel_id=1, source_target_pairs={{0,8},{8,16},{16,24},{24,0},{1,9},{9,17},{17,25},{25,1},{2,10},{10... | collective-permute-start | bytes 3981320 | tf_op jit(solution)/shard_map/ppermute | solution.py:792
  295.7 38.0 %collective-permute-start.40 = (bf16[2,576,1152]{2,1,0:T(8,128)(2,1)}, bf16[2,576,1152]{2,1,0:T(8,128)(2,1)}, u32[]{:S(2)}, u32[]{:S(2)}) collective-permute-start(bf16[2,576,1152]{2,1,0:T(8,128)(2,1)} %get-tuple-element.143), channel_id=1, source_target_pairs={{0,4},{4,0},{1,5},{5,1},{2,6},{6,2},{3,7},{7,3},{8,12},{12,8},{9,1... | collective-permute-start | bytes 7962632 | tf_op jit(solution)/shard_map/ppermute | solution.py:783
  301.7 43.8 %collective-permute-start.41 = (bf16[4,144,1152]{2,1,0:T(8,128)(2,1)}, bf16[4,144,1152]{2,1,0:T(8,128)(2,1)}, u32[]{:S(2)}, u32[]{:S(2)}) collective-permute-start(bf16[4,144,1152]{2,1,0:T(8,128)(2,1)} %collective-permute-done.30.rest_0_), channel_id=1, source_target_pairs={{0,4},{4,0},{1,5},{5,1},{2,6},{6,2},{3,7},{7,3},{8,12},{12,8},{9,1... | collective-permute-start | bytes 3981320 | tf_op jit(solution)/shard_map/ppermute | solution.py:783
  332.0 44.0 %collective-permute-start.39 = (bf16[2,576,1152]{2,1,0:T(8,128)(2,1)}, bf16[2,576,1152]{2,1,0:T(8,128)(2,1)}, u32[]{:S(2)}, u32[]{:S(2)}) collective-permute-start(bf16[2,576,1152]{2,1,0:T(8,128)(2,1)} %get-tuple-element.141), channel_id=1, source_target_pairs={{0,4},{4,0},{1,5},{5,1},{2,6},{6,2},{3,7},{7,3},{8,12},{12,8},{9,1... | collective-permute-start | bytes 7962632 | tf_op jit(solution)/shard_map/ppermute | solution.py:783
  333.7 42.2 %collective-permute-start.32 = (bf16[4,144,1152]{2,1,0:T(8,128)(2,1)}, bf16[4,144,1152]{2,1,0:T(8,128)(2,1)}, u32[]{:S(2)}, u32[]{:S(2)}) collective-permute-start(bf16[4,144,1152]{2,1,0:T(8,128)(2,1)} %collective-permute-done.30.rest_0_), channel_id=1, source_target_pairs={{0,8},{8,16},{16,24},{24,0},{1,9},{9,17},{17,25},{25,1},{2,10},{10... | collective-permute-start | bytes 3981320 | tf_op jit(solution)/shard_map/ppermute | solution.py:792
  333.7 51.6 %collective-permute-start.34 = (bf16[4,144,1152]{2,1,0:T(8,128)(2,1)}, bf16[4,144,1152]{2,1,0:T(8,128)(2,1)}, u32[]{:S(2)}, u32[]{:S(2)}) collective-permute-start(bf16[4,144,1152]{2,1,0:T(8,128)(2,1)} %collective-permute-done.31.rest_2_), channel_id=1, source_target_pairs={{0,4},{4,0},{1,5},{5,1},{2,6},{6,2},{3,7},{7,3},{8,12},{12,8},{9,1... | collective-permute-start | bytes 3981320 | tf_op jit(solution)/shard_map/ppermute | solution.py:783
  341.3 39.7 %all-to-all-start.5 = ((bf16[4,144,1152]{2,1,0:T(8,128)(2,1)}), bf16[4,144,1152]{2,1,0:T(8,128)(2,1)}, u32[]{:S(2)}, u32[]{:S(2)}) async-start(bf16[4,144,1152]{2,1,0:T(8,128)(2,1)} %bitcast.37.rest_4_), calls=%async_computation.5 | async-start | bytes 2654208 | tf_op jit(solution)/shard_map/all_to_all | solution.py:814
  375.1 42.8 %collective-permute-start.43 = (bf16[2,576,1152]{2,1,0:T(8,128)(2,1)}, bf16[2,576,1152]{2,1,0:T(8,128)(2,1)}, u32[]{:S(2)}, u32[]{:S(2)}) collective-permute-start(bf16[2,576,1152]{2,1,0:T(8,128)(2,1)} %get-tuple-element.152), channel_id=1, source_target_pairs={{0,4},{4,0},{1,5},{5,1},{2,6},{6,2},{3,7},{7,3},{8,12},{12,8},{9,1... | collective-permute-start | bytes 7962632 | tf_op jit(solution)/shard_map/ppermute | solution.py:783
  380.9 40.6 %collective-permute-start.44 = (bf16[4,144,1152]{2,1,0:T(8,128)(2,1)}, bf16[4,144,1152]{2,1,0:T(8,128)(2,1)}, u32[]{:S(2)}, u32[]{:S(2)}) collective-permute-start(bf16[4,144,1152]{2,1,0:T(8,128)(2,1)} %bitcast.36.rest_5_), channel_id=1, source_target_pairs={{0,8},{8,16},{16,24},{24,0},{1,9},{9,17},{17,25},{25,1},{2,10},{10... | collective-permute-start | bytes 3981320 | tf_op jit(solution)/shard_map/ppermute | solution.py:792
  380.9 46.0 %all-to-all-start.6 = ((bf16[4,144,1152]{2,1,0:T(8,128)(2,1)}), bf16[4,144,1152]{2,1,0:T(8,128)(2,1)}, u32[]{:S(2)}, u32[]{:S(2)}) async-start(bf16[4,144,1152]{2,1,0:T(8,128)(2,1)} %bitcast.35.rest_4_), calls=%async_computation.6 | async-start | bytes 2654208 | tf_op jit(solution)/shard_map/all_to_all | solution.py:814
  414.7 39.2 %collective-permute-start.45 = (bf16[2,576,1152]{2,1,0:T(8,128)(2,1)}, bf16[2,576,1152]{2,1,0:T(8,128)(2,1)}, u32[]{:S(2)}, u32[]{:S(2)}) collective-permute-start(bf16[2,576,1152]{2,1,0:T(8,128)(2,1)} %get-tuple-element.161), channel_id=1, source_target_pairs={{0,4},{4,0},{1,5},{5,1},{2,6},{6,2},{3,7},{7,3},{8,12},{12,8},{9,1... | collective-permute-start | bytes 7962632 | tf_op jit(solution)/shard_map/ppermute | solution.py:783
  424.3 33.3 %collective-permute-start.46 = (bf16[4,144,1152]{2,1,0:T(8,128)(2,1)}, bf16[4,144,1152]{2,1,0:T(8,128)(2,1)}, u32[]{:S(2)}, u32[]{:S(2)}) collective-permute-start(bf16[4,144,1152]{2,1,0:T(8,128)(2,1)} %add_convert_fusion.7.rest_1_), channel_id=1, source_target_pairs={{0,8},{8,16},{16,24},{24,0},{1,9},{9,17},{17,25},{25,1},{2,10},{10... | collective-permute-start | bytes 3981320 | tf_op jit(solution)/shard_map/ppermute | solution.py:792
  426.9 34.7 %all-to-all-start.7 = ((bf16[4,144,1152]{2,1,0:T(8,128)(2,1)}), bf16[4,144,1152]{2,1,0:T(8,128)(2,1)}, u32[]{:S(2)}, u32[]{:S(2)}) async-start(bf16[4,144,1152]{2,1,0:T(8,128)(2,1)} %bitcast.40.rest_0_), calls=%async_computation.7 | async-start | bytes 2654208 | tf_op jit(solution)/shard_map/all_to_all | solution.py:814
  460.3 79.9 %collective-permute-start.48 = (bf16[4,144,1152]{2,1,0:T(8,128)(2,1)}, bf16[4,144,1152]{2,1,0:T(8,128)(2,1)}, u32[]{:S(2)}, u32[]{:S(2)}) collective-permute-start(bf16[4,144,1152]{2,1,0:T(8,128)(2,1)} %add_convert_fusion.6.rest_1_), channel_id=1, source_target_pairs={{0,8},{8,16},{16,24},{24,0},{1,9},{9,17},{17,25},{25,1},{2,10},{10... | collective-permute-start | bytes 3981320 | tf_op jit(solution)/shard_map/ppermute | solution.py:792
  461.6 34.2 %all-to-all-start.9 = ((bf16[4,144,1152]{2,1,0:T(8,128)(2,1)}), bf16[4,144,1152]{2,1,0:T(8,128)(2,1)}, u32[]{:S(2)}, u32[]{:S(2)}) async-start(bf16[4,144,1152]{2,1,0:T(8,128)(2,1)} %bitcast.42.rest_0_), calls=%async_computation.9 | async-start | bytes 2654208 | tf_op jit(solution)/shard_map/all_to_all | solution.py:814
  489.9 53.2 %collective-permute-start.52 = (bf16[592,1152]{1,0:T(8,128)(2,1)}, bf16[592,1152]{1,0:T(8,128)(2,1)S(1)}, u32[]{:S(2)}, u32[]{:S(2)}) collective-permute-start(bf16[592,1152]{1,0:T(8,128)(2,1)} %get-tuple-element.186), channel_id=1, source_target_pairs={{0,4},{4,0},{1,5},{5,1},{2,6},{6,2},{3,7},{7,3},{8,12},{12,8},{9,1... | collective-permute-start | bytes 4091912 | tf_op jit(solution)/shard_map/ppermute | solution.py:783
  492.9 51.7 %collective-permute-start.49 = (bf16[2,128,1152]{2,1,0:T(8,128)(2,1)}, bf16[2,128,1152]{2,1,0:T(8,128)(2,1)}, u32[]{:S(2)}, u32[]{:S(2)}) collective-permute-start(bf16[2,128,1152]{2,1,0:T(8,128)(2,1)} %get-tuple-element.281), channel_id=1, source_target_pairs={{0,1},{1,0},{2,3},{3,2},{4,5},{5,4},{6,7},{7,6},{8,9},{9,8},{10,11... | collective-permute-start | bytes 1769480 | tf_op jit(solution)/shard_map/ppermute | solution.py:786
  494.6 50.0 %collective-permute-start.50 = (bf16[2,128,1152]{2,1,0:T(8,128)(2,1)}, bf16[2,128,1152]{2,1,0:T(8,128)(2,1)}, u32[]{:S(2)}, u32[]{:S(2)}) collective-permute-start(bf16[2,128,1152]{2,1,0:T(8,128)(2,1)} %get-tuple-element.280), channel_id=1, source_target_pairs={{0,2},{1,3},{2,0},{3,1},{4,6},{5,7},{6,4},{7,5},{8,10},{9,11},{10,... | collective-permute-start | bytes 1769480 | tf_op jit(solution)/shard_map/ppermute | solution.py:786
  495.8 48.8 %collective-permute-start.51 = (bf16[2,128,1152]{2,1,0:T(8,128)(2,1)S(1)}, bf16[2,128,1152]{2,1,0:T(8,128)(2,1)}, u32[]{:S(2)}, u32[]{:S(2)}) collective-permute-start(bf16[2,128,1152]{2,1,0:T(8,128)(2,1)S(1)} %get-tuple-element.279), channel_id=1, source_target_pairs={{0,3},{1,2},{2,1},{3,0},{4,7},{5,6},{6,5},{7,4},{8,11},{9,10},{10,... | collective-permute-start | bytes 1769480 | tf_op jit(solution)/shard_map/ppermute | solution.py:786
  528.5 40.4 %all-to-all-start.10 = ((bf16[32,37,144]{2,1,0:T(8,128)(2,1)}), bf16[32,37,144]{2,1,0:T(8,128)(2,1)S(1)}, u32[]{:S(2)}, u32[]{:S(2)}) async-start(bf16[32,37,144]{2,1,0:T(8,128)(2,1)} %pad_maximum_fusion), calls=%async_computation.10 | async-start | bytes 1310720 | tf_op jit(solution)/shard_map/all_to_all | solution.py:795
  540.2 51.1 %collective-permute-start.47 = (bf16[592,1152]{1,0:T(8,128)(2,1)}, bf16[592,1152]{1,0:T(8,128)(2,1)}, u32[]{:S(2)}, u32[]{:S(2)}) collective-permute-start(bf16[592,1152]{1,0:T(8,128)(2,1)} %get-tuple-element.181), channel_id=1, source_target_pairs={{0,4},{4,0},{1,5},{5,1},{2,6},{6,2},{3,7},{7,3},{8,12},{12,8},{9,1... | collective-permute-start | bytes 4091912 | tf_op jit(solution)/shard_map/ppermute | solution.py:783
  577.9 46.1 %collective-permute-start.54 = (bf16[288,576]{1,0:T(8,128)(2,1)S(1)}, bf16[288,576]{1,0:T(8,128)(2,1)}, u32[]{:S(2)}, u32[]{:S(2)}) collective-permute-start(bf16[288,576]{1,0:T(8,128)(2,1)S(1)} %get-tuple-element.286), channel_id=1, source_target_pairs={{0,8},{8,0},{16,24},{24,16},{1,9},{9,1},{17,25},{25,17},{2,10},{10... | collective-permute-start | bytes 995336 | tf_op jit(solution)/shard_map/ppermute | solution.py:789
  579.0 45.2 %collective-permute-start.55 = (bf16[288,576]{1,0:T(8,128)(2,1)S(1)}, bf16[288,576]{1,0:T(8,128)(2,1)}, u32[]{:S(2)}, u32[]{:S(2)}) collective-permute-start(bf16[288,576]{1,0:T(8,128)(2,1)S(1)} %get-tuple-element.285), channel_id=1, source_target_pairs={{0,16},{8,24},{16,0},{24,8},{1,17},{9,25},{17,1},{25,9},{2,18},{10... | collective-permute-start | bytes 995336 | tf_op jit(solution)/shard_map/ppermute | solution.py:789
  581.3 45.1 %collective-permute-start.56 = (bf16[288,576]{1,0:T(8,128)(2,1)S(1)}, bf16[288,576]{1,0:T(8,128)(2,1)}, u32[]{:S(2)}, u32[]{:S(2)}) collective-permute-start(bf16[288,576]{1,0:T(8,128)(2,1)S(1)} %get-tuple-element.284), channel_id=1, source_target_pairs={{0,24},{8,16},{16,8},{24,0},{1,25},{9,17},{17,9},{25,1},{2,26},{10... | collective-permute-start | bytes 995336 | tf_op jit(solution)/shard_map/ppermute | solution.py:789
  591.3 72.4 %collective-permute-start.57 = (bf16[592,1152]{1,0:T(8,128)(2,1)}, bf16[592,1152]{1,0:T(8,128)(2,1)}, u32[]{:S(2)}, u32[]{:S(2)}) collective-permute-start(bf16[592,1152]{1,0:T(8,128)(2,1)} %add_convert_fusion.3.rest_6_), channel_id=1, source_target_pairs={{0,3},{1,2},{2,1},{3,0},{4,7},{5,6},{6,5},{7,4},{8,11},{9,10},{10,... | collective-permute-start | bytes 4091912 | tf_op jit(solution)/shard_map/ppermute | solution.py:786
  595.7 68.0 %collective-permute-start.58 = (bf16[592,1152]{1,0:T(8,128)(2,1)}, bf16[592,1152]{1,0:T(8,128)(2,1)}, u32[]{:S(2)}, u32[]{:S(2)}) collective-permute-start(bf16[592,1152]{1,0:T(8,128)(2,1)} %add_convert_fusion.4.rest_1_), channel_id=1, source_target_pairs={{0,1},{1,0},{2,3},{3,2},{4,5},{5,4},{6,7},{7,6},{8,9},{9,8},{10,11... | collective-permute-start | bytes 4091912 | tf_op jit(solution)/shard_map/ppermute | solution.py:786
  623.9 39.8 %collective-permute-start.59 = (bf16[592,1152]{1,0:T(8,128)(2,1)}, bf16[592,1152]{1,0:T(8,128)(2,1)}, u32[]{:S(2)}, u32[]{:S(2)}) collective-permute-start(bf16[592,1152]{1,0:T(8,128)(2,1)} %add_convert_fusion.2.rest_2_.rest_4_), channel_id=1, source_target_pairs={{0,2},{1,3},{2,0},{3,1},{4,6},{5,7},{6,4},{7,5},{8,10},{9,11},{10,... | collective-permute-start | bytes 4091912 | tf_op jit(solution)/shard_map/ppermute | solution.py:786
  624.3 36.3 %collective-permute-start.60 = (bf16[592,1152]{1,0:T(8,128)(2,1)}, bf16[592,1152]{1,0:T(8,128)(2,1)}, u32[]{:S(2)}, u32[]{:S(2)}) collective-permute-start(bf16[592,1152]{1,0:T(8,128)(2,1)} %get-tuple-element.200), channel_id=1, source_target_pairs={{0,4},{4,0},{1,5},{5,1},{2,6},{6,2},{3,7},{7,3},{8,12},{12,8},{9,1... | collective-permute-start | bytes 4091912 | tf_op jit(solution)/shard_map/ppermute | solution.py:783
  656.9 35.7 %all-to-all-start.13 = ((bf16[4,2,128,1152]{3,2,1,0:T(8,128)(2,1)}), bf16[4,2,128,1152]{3,2,1,0:T(8,128)(2,1)S(1)}, u32[]{:S(2)}, u32[]{:S(2)}) async-start(bf16[4,2,128,1152]{3,2,1,0:T(8,128)(2,1)} %get-tuple-element.197), calls=%async_computation.13 | async-start | bytes 4718592 | tf_op jit(solution)/shard_map/all_to_all | solution.py:814
  693.4 33.4 %all-to-all-start.14 = ((bf16[32,39,72]{2,1,0:T(8,128)(2,1)}), bf16[32,39,72]{2,1,0:T(8,128)(2,1)S(1)}, u32[]{:S(2)}, u32[]{:S(2)}) async-start(bf16[32,39,72]{2,1,0:T(8,128)(2,1)} %pad_maximum_fusion.2), calls=%async_computation.14 | async-start | bytes 655360 | tf_op jit(solution)/shard_map/all_to_all | solution.py:795
  (88 other events, 1565.5 us)
